TPU v7x, 32 devices: a whole 2x2x4 slice. The times are simulated.
32 devices in a mesh: freq: 4 (over y, x), tile: 8 (over z, core).
Axes of the slice: x: 2, y: 2, z: 4, core: 2. Of those that a mesh axis runs over, the one named last changes fastest.
Arguments:
- u_data: bfloat16 [8, 4096, 128], P('freq', 'tile'), may hold values from -6 to 6
- u_basis: bfloat16 [8, 16, 16, 2, 48, 256], P('freq', 'tile'), may hold values from -0.25 to 0.25
- v_basis: bfloat16 [8, 16, 16, 2, 48, 256], P('freq', None, 'tile'), may hold values from -0.21875 to 0.21875
- ranks: int32 [8, 16, 16], P('freq'), may hold values from 8 to 48, as said below
- time_mask: int32 [64, 64], replicated, may hold values 0 or 1
Outputs:
- result: bfloat16 [8, 4096, 128], P('freq', 'tile')
Inputs may be any that keep to these rules, and one draw needn't show every extreme that they name: For every tile and every m, ranks[2 m + 1, i, j] = 56 - ranks[2 m, i, j].
All inputs are finite; a program needn't handle non-finite values.
Results may differ from a plain program's by a relative error of at most 0.006.
Values may be sent and summed in bfloat16 or wider, within the bound.
No kernel may reach another device: no remote copies, remote signals or barrier semaphores. Data moves between devices by JAX's collectives and lax.ppermute only.
A program may use at most 128 MiB of HBM per device.

v0:
```python
import math

import jax
import jax.numpy as jnp
from jax import lax
from jax.sharding import PartitionSpec as P

first_bin = 3
highest = lax.Precision.HIGHEST


def rotate(values):
    half_width = values.shape[-1] // 2
    return jnp.concatenate([-values[..., half_width:], values[..., :half_width]], axis=-1)


def conj_apply(leading, trailing):
    half_width = leading.shape[-1] // 2
    real_part = leading[..., :half_width] + trailing[..., half_width:]
    imag_part = leading[..., half_width:] - trailing[..., :half_width]
    return jnp.concatenate([real_part, imag_part], axis=-1)


def plain_apply(leading, trailing):
    half_width = leading.shape[-1] // 2
    real_part = leading[..., :half_width] - trailing[..., half_width:]
    imag_part = leading[..., half_width:] + trailing[..., :half_width]
    return jnp.concatenate([real_part, imag_part], axis=-1)


def rank_weights(tile_ranks, slot_count):
    slots = jnp.arange(slot_count, dtype=jnp.int32)
    return (slots < tile_ranks[..., None]).astype(jnp.float32)[..., None]


def dft_tables(freq_count, time_count):
    sample_ids = jnp.arange(time_count, dtype=jnp.int32)
    bin_ids = jnp.arange(freq_count, dtype=jnp.int32) + first_bin
    phase = sample_ids[:, None] * bin_ids[None, :] % time_count
    angle = 2.0 * math.pi / time_count * phase.astype(jnp.float32)
    factor = 1.0 / math.sqrt(time_count)
    return (jnp.cos(angle) * factor, jnp.sin(angle) * factor)


def pair_tables(tile_ranks, slot_count):
    total = slot_count // 6 + slot_count
    first_ranks = tile_ranks[0::2][..., None, None]
    packed_ids = jnp.arange(total, dtype=jnp.int32)[:, None]
    slot_ids = jnp.arange(slot_count, dtype=jnp.int32)[None, :]
    lower = ((packed_ids == slot_ids) & (packed_ids < first_ranks)).astype(jnp.bfloat16)
    upper = (packed_ids - first_ranks == slot_ids).astype(jnp.bfloat16)
    return (lower, upper)


def pack_pairs(coeffs, lower, upper):
    paired = coeffs.reshape((coeffs.shape[0] // 2, 2) + coeffs.shape[1:])
    packed = jnp.einsum(
        "mijpk,mijkq->mijpq", lower, paired[:, 0], preferred_element_type=jnp.float32
    )
    packed = packed + jnp.einsum(
        "mijpk,mijkq->mijpq", upper, paired[:, 1], preferred_element_type=jnp.float32
    )
    return packed.astype(jnp.bfloat16)


def unpack_pairs(packed, lower, upper):
    first = jnp.einsum("mijpk,mijpq->mijkq", lower, packed, preferred_element_type=jnp.float32)
    second = jnp.einsum("mijpk,mijpq->mijkq", upper, packed, preferred_element_type=jnp.float32)
    joined = jnp.stack([first, second], axis=1)
    return joined.reshape((joined.shape[0] * 2,) + joined.shape[2:]).astype(jnp.bfloat16)


def local(u_data, u_basis, v_basis, ranks, time_mask):
    freq_local = u_data.shape[0]
    row_count = u_data.shape[1]
    width = u_data.shape[2]
    row_tiles = u_basis.shape[1]
    slot_count = u_basis.shape[4]
    tile_width = u_basis.shape[5]
    col_tiles = v_basis.shape[2]
    time_count = time_mask.shape[0]
    tile_index = lax.axis_index("tile")
    row_ranks = lax.dynamic_slice_in_dim(ranks, tile_index * row_tiles, row_tiles, 1)
    col_ranks = lax.dynamic_slice_in_dim(ranks, tile_index * col_tiles, col_tiles, 2)
    weights = rank_weights(row_ranks, slot_count)
    local_rows = u_data.reshape(freq_local, row_tiles, tile_width, width)
    product = jnp.einsum(
        "fijckp,fipq->fijckq", u_basis, local_rows, preferred_element_type=jnp.float32
    )
    coeffs = (conj_apply(product[:, :, :, 0], product[:, :, :, 1]) * weights).astype(jnp.bfloat16)
    send_lower, send_upper = pair_tables(row_ranks, slot_count)
    packed = pack_pairs(coeffs, send_lower, send_upper)
    landed = lax.all_to_all(packed, "tile", split_axis=2, concat_axis=1, tiled=True)
    take_lower, take_upper = pair_tables(col_ranks, slot_count)
    arrived = unpack_pairs(landed, take_lower, take_upper)
    image = jnp.einsum("fijckp,fijkq->fjcpq", v_basis, arrived, preferred_element_type=jnp.float32)
    columns = plain_apply(image[:, :, 0], image[:, :, 1])
    columns = columns.reshape(freq_local, col_tiles * tile_width, width).astype(jnp.bfloat16)
    kept = time_mask.astype(jnp.float32)
    spread = lax.all_to_all(columns, "freq", split_axis=1, concat_axis=0, tiled=True)
    cos_table, sin_table = dft_tables(spread.shape[0], time_count)
    doubled = jnp.concatenate([kept, kept], axis=-1)
    values = spread.astype(jnp.float32)
    signal = jnp.einsum("tf,fnq->tnq", cos_table, values, precision=highest)
    signal = signal + jnp.einsum("tf,fnq->tnq", sin_table, rotate(values), precision=highest)
    signal = signal * doubled[:, None, :]
    result = jnp.einsum("tf,tnq->fnq", cos_table, signal, precision=highest)
    result = result - jnp.einsum("tf,tnq->fnq", sin_table, rotate(signal), precision=highest)
    mixed = lax.all_to_all(
        result.astype(jnp.bfloat16), "freq", split_axis=0, concat_axis=1, tiled=True
    )
    local_cols = mixed.reshape(freq_local, col_tiles, tile_width, width)
    product = jnp.einsum(
        "fijckp,fjpq->fijckq", v_basis, local_cols, preferred_element_type=jnp.float32
    )
    coeffs = conj_apply(product[:, :, :, 0], product[:, :, :, 1]).astype(jnp.bfloat16)
    send_lower, send_upper = pair_tables(col_ranks, slot_count)
    packed = pack_pairs(coeffs, send_lower, send_upper)
    landed = lax.all_to_all(packed, "tile", split_axis=1, concat_axis=2, tiled=True)
    take_lower, take_upper = pair_tables(row_ranks, slot_count)
    returned = unpack_pairs(landed, take_lower, take_upper)
    output = jnp.einsum(
        "fijckp,fijkq->ficpq", u_basis, returned, preferred_element_type=jnp.float32
    )
    rows_out = plain_apply(output[:, :, 0], output[:, :, 1])
    return rows_out.reshape(freq_local, row_count, width).astype(jnp.bfloat16)


def solution(mesh):
    placed = (
        P("freq", "tile", None),
        P("freq", "tile", None, None, None, None),
        P("freq", None, "tile", None, None, None),
        P("freq", None, None),
        P(),
    )
    return jax.shard_map(
        local, mesh=mesh, in_specs=placed, out_specs=P("freq", "tile", None), check_vma=False
    )
```

profile of v0, /device:TPU:0, one launch (start us, length us, event | category | flops | bytes accessed | tf_op | source)
XLA Modules:
  0.0 87.3 jit_solution(7035130628254395631)
XLA Ops:
  0.0 0.9 constant_dynamic-slice_fusion
  0.9 0.8 dynamic-slice_bitcast_fusion.1
  1.9 2.9 %fusion.114 = f32[2,2,16,2,48,128]{5,4,3,2,1,0:T(8,128)S(1)} fusion(bf16[2,2,16,2,48,256]{5,4,3,2,1,0:T(8,128)(2,1)} %param.6, bf16[2,2,256,128,1,1]{3,2,5,4,1,0:T(8,128)(2,1)} %bitcast.147), kind=kOutput, calls=%fused_computation.155 | convolution fusion | flops 402653184 | bytes 6553600 | tf_op jit(solution)/shard_map/fijckp,fipq->fijckq/dot_general | solution.py:87
  4.8 0.3 slice_bitcast_fusion.3
  5.1 0.9 %fusion.14 = (f32[1,2,2,16,48,64]{5,4,3,2,1,0:T(8,128)S(1)}, f32[1,2,2,16,48,64]{5,4,3,2,1,0:T(8,128)S(1)}) fusion(f32[2,2,16,48,128]{4,3,2,1,0:T(8,128)S(1)} %get-tuple-element.14, f32[2,2,16,48,128]{4,3,2,1,0:T(8,128)S(1)} %get-tuple-element.13), kind=kLoop, calls=%fused_computation.20 | loop fusion | flops 393216 | bytes 4718592 | tf_op jit(solution)/shard_map/concatenate | solution.py:21
  6.0 0.9 %fusion.15 = bf16[1,2,2,16,48,128]{5,4,3,2,1,0:T(8,128)(2,1)S(1)} fusion(f32[1,2,2,16,48,64]{5,4,3,2,1,0:T(8,128)S(1)} %get-tuple-element.12, f32[1,2,2,16,48,64]{5,4,3,2,1,0:T(8,128)S(1)} %get-tuple-element.11, f32[2,2,16,48]{3,2,1,0:T(8,128)S(1)} %fusion.71), kind=kLoop, calls=%fused_computation.24 | loop fusion | flops 1179648 | bytes 2371584 | tf_op jit(solution)/shard_map/convert_element_type | solution.py:90
  6.9 0.5 fusion.37
  7.3 0.5 fusion.25
  7.8 0.8 copy.42
  8.6 6.3 %all-to-all-start = ((bf16[1,2,16,56,128]{4,3,1,0,2:T(8,128)(2,1)}), bf16[1,2,16,56,128]{4,3,1,0,2:T(8,128)(2,1)}, u32[]{:S(2)}, u32[]{:S(2)}) async-start(bf16[1,2,16,56,128]{4,3,1,0,2:T(8,128)(2,1)} %copy.42), calls=%async_computation | async-start | bytes 917504 | tf_op jit(solution)/shard_map/all_to_all | solution.py:93
  15.2 13.8 %all-to-all-done = bf16[1,2,16,56,128]{4,3,1,0,2:T(8,128)(2,1)} async-done(((bf16[1,2,16,56,128]{4,3,1,0,2:T(8,128)(2,1)}), bf16[1,2,16,56,128]{4,3,1,0,2:T(8,128)(2,1)}, u32[]{:S(2)}, u32[]{:S(2)}) %all-to-all-start) | async-done | bytes 458784 | tf_op jit(solution)/shard_map/all_to_all | solution.py:93
  29.0 1.1 %copy.43 = bf16[1,2,8,2,56,128]{5,4,3,1,2,0:T(8,128)(2,1)S(1)} copy(bf16[1,2,8,2,56,128]{5,4,1,3,2,0:T(8,128)(2,1)} %bitcast.13) | data formatting | bytes 917504 | tf_op jit(solution)/shard_map/all_to_all | solution.py:93
  30.6 0.7 fusion.16
  31.5 0.8 copy.47
  32.3 1.9 %copy.48 = bf16[2,512,128]{2,0,1:T(2,128)(2,1)} copy(bf16[2,512,128]{2,1,0:T(8,128)(2,1)} %bitcast.144) | data formatting | bytes 524288 | tf_op jit(solution)/shard_map/convert_element_type | solution.py:98
  34.2 3.7 %all-to-all-start.1 = ((bf16[2,512,128]{2,0,1:T(2,128)(2,1)}), bf16[2,512,128]{2,0,1:T(2,128)(2,1)S(1)}, u32[]{:S(2)}, u32[]{:S(2)}) async-start(bf16[2,512,128]{2,0,1:T(2,128)(2,1)} %copy.48), calls=%async_computation.1 | async-start | bytes 524288 | tf_op jit(solution)/shard_map/all_to_all | solution.py:100
  38.0 5.3 %all-to-all-done.1 = bf16[2,512,128]{2,0,1:T(2,128)(2,1)S(1)} async-done(((bf16[2,512,128]{2,0,1:T(2,128)(2,1)}), bf16[2,512,128]{2,0,1:T(2,128)(2,1)S(1)}, u32[]{:S(2)}, u32[]{:S(2)}) %all-to-all-start.1) | async-done | bytes 262176 | tf_op jit(solution)/shard_map/all_to_all | solution.py:100
  44.0 3.6 %fusion.46 = f32[64,128,128]{2,0,1:T(8,128)S(1)} fusion(f32[8,128,64]{2,0,1:T(8,128)S(1)} %slice.155, f32[8,128,64]{2,0,1:T(8,128)S(1)} %slice_negate_fusion.1, s32[8]{0:T(128)S(1)} %iota_add_fusion), kind=kOutput, calls=%fused_computation.66 | convolution fusion | flops 100802048 | bytes 4718624 | tf_op jit(solution)/shard_map/tf,fnq->tnq/dot_general | solution.py:105
  47.6 2.3 %add_multiply_fusion = f32[64,128,128]{2,0,1:T(8,128)S(1)} fusion(f32[64,128,128]{2,0,1:T(8,128)S(1)} %fusion.46, bf16[8,128,128]{2,0,1:T(8,128)(2,1)S(1)} %bitcast.137, f32[64,128]{1,0:T(8,128)S(1)} %pad_maximum_fusion.3, s32[8]{0:T(128)S(1)} %iota_add_fusion), kind=kOutput, calls=%fused_computation.5 | convolution fusion | flops 102768128 | bytes 8683552 | tf_op jit(solution)/shard_map/tf,fnq->tnq/dot_general | solution.py:104
  49.9 1.7 %slice_negate_fusion = (f32[64,128,64]{2,0,1:T(8,128)S(1)}, f32[64,128,64]{2,0,1:T(8,128)S(1)}) fusion(f32[64,128,128]{2,0,1:T(8,128)S(1)} %add_multiply_fusion), kind=kLoop, calls=%fused_computation | loop fusion | flops 524288 | bytes 8388608 | tf_op jit(solution)/shard_map/neg | solution.py:14
  51.6 2.2 %fusion.77 = f32[8,128,128]{2,0,1:T(8,128)S(1)} fusion(f32[64,128,128]{2,0,1:T(8,128)S(1)} %add_multiply_fusion, s32[8]{0:T(128)S(1)} %iota_add_fusion), kind=kOutput, calls=%fused_computation.117 | convolution fusion | flops 100670976 | bytes 4718624 | tf_op jit(solution)/shard_map/tf,tnq->fnq/dot_general | solution.py:107
  53.7 3.0 %fusion.26 = bf16[8,128,128]{2,0,1:T(8,128)(2,1)S(1)} fusion(f32[8,128,128]{2,0,1:T(8,128)S(1)} %fusion.77, f32[64,128,64]{2,0,1:T(8,128)S(1)} %get-tuple-element.6, f32[64,128,64]{2,0,1:T(8,128)S(1)} %get-tuple-element.5, s32[8]{0:T(128)S(1)} %iota_add_fusion), kind=kOutput, calls=%fused_computation.38 | convolution fusion | flops 101981696 | bytes 4980768 | tf_op jit(solution)/shard_map/tf,tnq->fnq/dot_general | solution.py:108
  56.8 8.1 %all_to_all.63 = bf16[8,128,128]{2,1,0:T(8,128)(2,1)S(1)} all-to-all(bf16[8,128,128]{2,1,0:T(8,128)(2,1)S(1)} %copy.51), channel_id=1, replica_groups=mesh['freq'=4,'tile'=8] {'freq'}, dimensions={0} | all-to-all | bytes 524288 | tf_op jit(solution)/shard_map/all_to_all | solution.py:109
  64.9 1.0 %fusion.8 = f32[2,16,2,2,48,128]{5,4,3,1,2,0:T(8,128)S(1)} fusion(bf16[2,2,256,128,1,1]{3,2,5,4,1,0:T(8,128)(2,1)S(1)} %bitcast.143, bf16[2,16,2,2,48,256]{5,4,3,2,1,0:T(8,128)(2,1)S(1)} %copy-done), kind=kOutput, calls=%fused_computation.10 | convolution fusion | flops 402653184 | bytes 6553600 | tf_op jit(solution)/shard_map/fijckp,fjpq->fijckq/dot_general | solution.py:113
  65.9 0.3 slice_bitcast_fusion.1
  66.2 0.9 %fusion.40 = (bf16[1,2,16,2,48,64]{5,4,2,3,1,0:T(8,128)(2,1)S(1)}, bf16[1,2,16,2,48,64]{5,4,2,3,1,0:T(8,128)(2,1)S(1)}) fusion(f32[2,16,2,48,128]{4,3,1,2,0:T(8,128)S(1)} %get-tuple-element.10, f32[2,16,2,48,128]{4,3,1,2,0:T(8,128)S(1)} %get-tuple-element.9), kind=kLoop, calls=%fused_computation.50 | loop fusion | flops 786432 | bytes 3932160 | tf_op jit(solution)/shard_map/concatenate | solution.py:21
  67.1 0.4 fusion.52
  67.6 0.5 fusion.33
  68.0 0.5 fusion.24
  68.5 16.5 %all_to_all.64 = bf16[1,16,2,56,128]{4,3,2,0,1:T(8,128)(2,1)S(1)} all-to-all(bf16[1,16,2,56,128]{4,3,2,0,1:T(8,128)(2,1)S(1)} %fusion.24), channel_id=1, replica_groups=mesh['freq'=4,'tile'=8] {'tile'}, dimensions={1} | all-to-all | bytes 917504 | tf_op jit(solution)/shard_map/all_to_all | solution.py:119
  85.6 0.6 convolution_bitcast_fusion
  86.4 0.8 copy.61
  (36 shorter events, 2.7 us)
Async XLA Ops:
  0.0 30.6 %copy-start = (bf16[2,16,2,2,48,256]{5,4,3,2,1,0:T(8,128)(2,1)S(1)}, bf16[2,16,2,2,48,256]{5,4,3,2,1,0:T(8,128)(2,1)}, u32[]{:S(2)}) copy-start(bf16[2,16,2,2,48,256]{5,4,3,2,1,0:T(8,128)(2,1)} %param.7) | copy-start | bytes 9437188
  6.8 8.1 %copy-start.2 = (s32[64,64]{1,0:T(8,128)S(1)}, s32[64,64]{1,0:T(8,128)}, u32[]{:S(2)}) copy-start(s32[64,64]{1,0:T(8,128)} %param.9) | copy-start | bytes 49156
  6.8 8.1 %copy-start.3 = (s32[2,16,16]{2,1,0:T(8,128)S(1)}, s32[2,16,16]{2,1,0:T(8,128)}, u32[]{:S(2)}) copy-start(s32[2,16,16]{2,1,0:T(8,128)} %param.8) | copy-start | bytes 6148
  8.6 20.4 %all-to-all-start = ((bf16[1,2,16,56,128]{4,3,1,0,2:T(8,128)(2,1)}), bf16[1,2,16,56,128]{4,3,1,0,2:T(8,128)(2,1)}, u32[]{:S(2)}, u32[]{:S(2)}) async-start(bf16[1,2,16,56,128]{4,3,1,0,2:T(8,128)(2,1)} %copy.42), calls=%async_computation | async-start | bytes 917504 | tf_op jit(solution)/shard_map/all_to_all | solution.py:93
  34.2 9.1 %all-to-all-start.1 = ((bf16[2,512,128]{2,0,1:T(2,128)(2,1)}), bf16[2,512,128]{2,0,1:T(2,128)(2,1)S(1)}, u32[]{:S(2)}, u32[]{:S(2)}) async-start(bf16[2,512,128]{2,0,1:T(2,128)(2,1)} %copy.48), calls=%async_computation.1 | async-start | bytes 524288 | tf_op jit(solution)/shard_map/all_to_all | solution.py:100
  67.5 18.0 %copy-start.1 = (bf16[2,2,16,2,48,256]{5,4,3,2,1,0:T(8,128)(2,1)S(1)}, bf16[2,2,16,2,48,256]{5,4,3,2,1,0:T(8,128)(2,1)}, u32[]{:S(2)}) copy-start(bf16[2,2,16,2,48,256]{5,4,3,2,1,0:T(8,128)(2,1)} %param.6) | copy-start | bytes 9437188
where the time goes:
time: 87.7 us; the launch traced here: 87.3 us
  blocking collectives  24.6 us (28%)
  matrix products  19.2 us (22%)
  waiting for transfers between devices  19.1 us (22%)
  starting transfers between devices  10 us (11%)
  local copies, waits for them, and re-layouts  8.38 us (10%)
  other arithmetic  5.69 us (6%)
    all_to_all x1, blocking collectives, local(): lax.all_to_all(packed, 'tile', split_axis=1, concat_axis=2, tiled=True)  16.5 us
    all_to_all x1, waiting for transfers between devices, local(): lax.all_to_all(packed, 'tile', split_axis=2, concat_axis=1, tiled=True)  13.8 us
    all_to_all x1, blocking collectives, local(): lax.all_to_all(result.astype(jnp.bfloat16), 'freq', split_axis=0, concat_...  8.11 us
    all_to_all x1, starting transfers between devices, local(): lax.all_to_all(packed, 'tile', split_axis=2, concat_axis=1, tiled=True)  6.32 us
    all_to_all x1, waiting for transfers between devices, local(): lax.all_to_all(columns, 'freq', split_axis=1, concat_axis=0, tiled=True)  5.29 us
    all_to_all x1, starting transfers between devices, local(): lax.all_to_all(columns, 'freq', split_axis=1, concat_axis=0, tiled=True)  3.72 us
    dot_general x1, matrix products, local(): jnp.einsum('tf,fnq->tnq', sin_table, rotate(values), precision=highest)  3.6 us
    dot_general x1, matrix products, local(): jnp.einsum('tf,tnq->fnq', sin_table, rotate(signal), precision=highest)  3.03 us
  transfers between devices with their start and end apart: 2, of which 2 were waited for; matrix products, arithmetic and copies ran while one was open for 0% of the time, Pallas kernels for 0%

commit v1 on v0

v1 whole, which is shorter than its diff:
```python
import functools
import math

import jax
import jax.numpy as jnp
import numpy as np
from jax import lax
from jax.experimental import pallas as pl
from jax.experimental.pallas import tpu as pltpu
from jax.sharding import PartitionSpec as P

vmem_limit = 48 * 1024 * 1024
bf16 = jnp.bfloat16
f32 = jnp.float32

whole = pl.BlockSpec(memory_space=pltpu.VMEM)
scalars = pl.BlockSpec(memory_space=pltpu.SMEM)
far = pl.BlockSpec(memory_space=pltpu.HBM)
anywhere = pl.BlockSpec(memory_space=pl.ANY)


def hold(value):
    return pltpu.with_memory_space_constraint(value, pltpu.HBM)


def call(kernel, name, ins, outs, scratch, flops=0, moved=0):
    specs = [spec for spec, _ in ins]
    shapes = [jax.ShapeDtypeStruct(shape, kind) for shape, kind in outs]
    return pl.pallas_call(
        kernel,
        in_specs=specs,
        out_specs=[whole] * len(outs),
        out_shape=shapes,
        scratch_shapes=scratch,
        compiler_params=pltpu.CompilerParams(vmem_limit_bytes=vmem_limit),
        cost_estimate=pl.CostEstimate(flops=flops, bytes_accessed=moved, transcendentals=0),
        name=name,
    )(*[value for _, value in ins])


def dot(lhs, rhs, lhs_dim, rhs_dim, precision=None):
    return lax.dot_general(
        lhs, rhs, (((lhs_dim,), (rhs_dim,)), ((), ())),
        precision=precision, preferred_element_type=f32,
    )


def lag_tables(count, time_count, lanes):
    samples = np.arange(time_count)[:, None]
    lags = np.arange(count)[None, :]
    angle = 2.0 * math.pi / time_count * ((samples * lags) % time_count)
    table = np.zeros((time_count, lanes), np.float32)
    table[:, :count] = np.cos(angle) / time_count
    table[:, count : 2 * count] = np.sin(angle) / time_count
    return table


def lag_choice(count, quarter):
    side = count * 2 * quarter
    choice = np.zeros((2 * count, count, 2, count, 2, quarter), np.float32)
    for f in range(count):
        for g in range(count):
            sign = 1.0 if g >= f else -1.0
            lag = abs(g - f)
            choice[lag, f, 0, g, 0] = 1.0
            choice[lag, f, 1, g, 1] = 1.0
            choice[count + lag, f, 0, g, 1] = -sign
            choice[count + lag, f, 1, g, 0] = sign
    same = np.arange(quarter)[:, None] == np.arange(side)[None, :] % quarter
    return choice.reshape(2 * count, 2 * count * side), same.astype(np.float32)


def pack_rows(stage, slot, row, rank, first, second):
    size = first.shape[0]
    stage[slot, pl.ds(row, size), :] = first
    stage[slot, pl.ds(row + rank, size), :] = second


def unpack_rows(stage, slot, row, rank, total, coeffs, base):
    slots = total - total // 7
    first = stage[slot, pl.ds(row, slots), :]
    second = stage[slot, pl.ds(row + rank, slots), :]
    ids = lax.broadcasted_iota(jnp.int32, first.shape, 0)
    at = pl.ds(pl.multiple_of(base, 16), slots)
    coeffs[0, at, :] = jnp.where(ids < rank, first, 0.0).astype(bf16)
    coeffs[1, at, :] = jnp.where(ids < total - rank, second, 0.0).astype(bf16)


def side_by_side(real, imag):
    flat = (-1, real.shape[-1])
    return jnp.concatenate([real.reshape(flat), imag.reshape(flat)], axis=1)


def plain_product(coeffs, both):
    half, tile = coeffs.shape[1] // 2, both.shape[1] // 2
    product = dot(coeffs, both, 0, 0)
    lead, trail = product[:, :tile], product[:, tile:]
    return jnp.concatenate([lead[:half] - trail[half:], lead[half:] + trail[:half]], axis=0)


def unstage(outs, stage, m, span, size, me):
    for s in range(len(outs)):
        for c in range(span):
            block = stage[(m * len(outs) + (me ^ s)) * span + c, pl.ds(0, size), :]
            outs[s][m, pl.ds(c * size, size), :] = block.astype(bf16)


def adjoint_kernel(devices, parts, ranks_far, u_far, basis_far, other_far, *rest):
    outs, other = rest[:devices], rest[devices]
    ranks, u_ref, basis, turned, stage, sems = rest[devices + 1 :]
    freqs, rows, _, cols, _, slots, tile = basis_far.shape
    total = slots + slots // 6
    half = u_ref.shape[2] // 2
    per = devices // parts
    me = lax.axis_index("tile")
    rank_copy = pltpu.make_async_copy(ranks_far, ranks, sems.at[0])
    data_copy = pltpu.make_async_copy(u_far, u_ref, sems.at[1])
    other_copy = pltpu.make_async_copy(other_far, other, sems.at[2])
    data_copy.start()
    rank_copy.start()
    copies = {}
    for i in range(rows):
        for p in range(parts):
            for f in range(freqs):
                at = pl.ds(p * per, per)
                copies[f, i, p] = pltpu.make_async_copy(
                    basis_far.at[f, i, at], basis.at[f, i, at], sems.at[3 + (f * rows + i) * parts + p]
                )
                copies[f, i, p].start()
    other_copy.start()
    data_copy.wait()
    for f in range(freqs):
        values = u_ref[f].astype(f32)
        lane = lax.broadcasted_iota(jnp.int32, values.shape, 1)
        rolled = pltpu.roll(values, half, 1)
        turned[f] = jnp.where(lane < half, rolled, -rolled).astype(bf16)
    waited = False
    for m in range(freqs // 2):
        for i in range(rows):
            here = pl.ds(i * tile, tile)
            for p in range(parts):
                pair = []
                at = pl.ds(p * per, per)
                for f in (2 * m, 2 * m + 1):
                    copies[f, i, p].wait()
                    both = side_by_side(basis[f, i, at, :, 0], basis[f, i, at, :, 1])
                    data = jnp.concatenate([u_ref[f, here, :], turned[f, here, :]], axis=0)
                    pair.append(dot(both, data, 1, 0))
                if not waited:
                    rank_copy.wait()
                    waited = True
                for n in range(per * cols):
                    col = p * per * cols + n
                    rank = ranks[2 * m, me * rows + i, col]
                    cut = slice(n * slots, (n + 1) * slots)
                    pack_rows(stage, m * devices * cols + col, i * total, rank, pair[0][cut], pair[1][cut])
        unstage(outs, stage, m, cols, rows * total, me)
    other_copy.wait()


def image_kernel(devices, owners, ranks_near, basis, *rest):
    packed = rest[:devices][::-1]
    outs = rest[-owners - 5 : -5]
    ranks, stage, coeffs, z, sem = rest[-5:]
    freqs, _, rows, cols, _, slots, tile = basis.shape
    total = slots + slots // 6
    half = coeffs.shape[3] // 2
    quarter = half // owners
    size = rows * total
    me, mine = lax.axis_index("tile"), lax.axis_index("freq")
    rank_copy = pltpu.make_async_copy(ranks_near, ranks, sem)
    rank_copy.start()
    for m in range(freqs // 2):
        for s in range(devices):
            for c in range(cols):
                block = packed[s][m, pl.ds(c * size, size), :]
                stage[(m * devices + s) * cols + c, pl.ds(0, size), :] = block.astype(f32)
    rank_copy.wait()
    for m in range(freqs // 2):
        for c in range(cols):
            for s in range(devices):
                for i in range(rows):
                    row = (me ^ s) * rows + i
                    rank = ranks[2 * m, row, me * cols + c]
                    slot = (m * devices + s) * cols + c
                    unpack_rows(stage, slot, i * total, rank, total, coeffs.at[c], row * slots)
            for n in range(2):
                f = 2 * m + n
                both = side_by_side(basis[f, :, :, c, 0], basis[f, :, :, c, 1])
                z[f, :, pl.ds(c * tile, tile)] = plain_product(coeffs[c, n], both)
    for r in range(owners):
        low = pl.multiple_of((mine ^ r) * quarter, quarter)
        for f in range(freqs):
            real = z[f, pl.ds(low, quarter), :]
            imag = z[f, pl.ds(half + low, quarter), :]
            outs[r][f] = jnp.concatenate([real, imag], axis=0).astype(bf16)


def window_kernel(mask, table, choice, same, high, low, full):
    exact = lax.Precision.HIGHEST
    full[...] = dot(mask[...].astype(f32), table[...], 0, 0, exact)
    quarter, side = same.shape
    mine = full[pl.ds(pl.multiple_of(lax.axis_index("freq") * quarter, quarter), quarter), :]
    entries = dot(mine[:, : choice.shape[0]], choice[...], 1, 0, exact)
    for n in range(side // quarter):
        block = entries[:, n * side : (n + 1) * side] * same[...]
        upper = block.astype(bf16)
        high[n * quarter : (n + 1) * quarter, :] = upper
        low[n * quarter : (n + 1) * quarter, :] = (block - upper.astype(f32)).astype(bf16)


def mix_kernel(owners, high, low, *rest):
    arrived = rest[:owners][::-1]
    outs = rest[owners : 2 * owners]
    z, w = rest[2 * owners :]
    freqs, rows, span = arrived[0].shape
    mine = lax.axis_index("freq")
    size = freqs * rows
    for r in range(owners):
        z[pl.ds(pl.multiple_of((mine ^ r) * size, 16), size), :] = arrived[r][...].reshape(size, span)
    w[...] = dot(high[...], z[...], 1, 0) + dot(low[...], z[...], 1, 0)
    for r in range(owners):
        block = w[pl.ds(pl.multiple_of((mine ^ r) * size, 16), size), :]
        outs[r][...] = block.reshape(freqs, rows, span).astype(bf16)


def forward_kernel(devices, owners, ranks_near, basis, *rest):
    arrived = rest[:owners][::-1]
    outs = rest[owners : owners + devices]
    ranks, w, stage, sem = rest[owners + devices :]
    freqs, _, rows, cols, _, slots, tile = basis.shape
    total = slots + slots // 6
    half = w.shape[2] // 2
    quarter = half // owners
    me, mine = lax.axis_index("tile"), lax.axis_index("freq")
    rank_copy = pltpu.make_async_copy(ranks_near, ranks, sem)
    rank_copy.start()
    for r in range(owners):
        low = pl.multiple_of((mine ^ r) * quarter, quarter)
        for f in range(freqs):
            for c in range(cols):
                at = slice(c * tile, (c + 1) * tile)
                real, imag = arrived[r][f, :quarter, at], arrived[r][f, quarter:, at]
                w[f, c, pl.ds(low, quarter), :tile] = real
                w[f, c, pl.ds(half + low, quarter), :tile] = imag
                w[f, c, pl.ds(low, quarter), tile:] = imag
                w[f, c, pl.ds(half + low, quarter), tile:] = -real
    rank_copy.wait()
    for m in range(freqs // 2):
        for c in range(cols):
            pair = []
            for f in (2 * m, 2 * m + 1):
                both = side_by_side(basis[f, :, :, c, 0], basis[f, :, :, c, 1])
                pair.append(dot(both, w[f, c], 1, 1))
            for d in range(devices):
                for i in range(rows):
                    rank = ranks[2 * m, d * rows + i, me * cols + c]
                    cut = slice((d * rows + i) * slots, (d * rows + i + 1) * slots)
                    slot = (m * devices + d) * cols + c
                    pack_rows(stage, slot, i * total, rank, pair[0][cut], pair[1][cut])
        unstage(outs, stage, m, cols, rows * total, me)


def result_kernel(devices, ranks_near, basis, *rest):
    packed = rest[:devices][::-1]
    out, ranks, stage, coeffs, sem = rest[devices:]
    freqs, rows, _, cols, _, slots, tile = basis.shape
    total = slots + slots // 6
    size = rows * total
    me = lax.axis_index("tile")
    rank_copy = pltpu.make_async_copy(ranks_near, ranks, sem)
    rank_copy.start()
    for m in range(freqs // 2):
        for s in range(devices):
            for c in range(cols):
                block = packed[s][m, pl.ds(c * size, size), :]
                stage[(m * devices + s) * cols + c, pl.ds(0, size), :] = block.astype(f32)
    rank_copy.wait()
    for m in range(freqs // 2):
        for i in range(rows):
            for s in range(devices):
                for c in range(cols):
                    col = (me ^ s) * cols + c
                    rank = ranks[2 * m, me * rows + i, col]
                    slot = (m * devices + s) * cols + c
                    unpack_rows(stage, slot, i * total, rank, total, coeffs.at[i], col * slots)
            for n in range(2):
                f = 2 * m + n
                both = side_by_side(basis[f, i, :, :, 0], basis[f, i, :, :, 1])
                r = plain_product(coeffs[i, n], both)
                out[f, pl.ds(i * tile, tile), :] = r.T.astype(bf16)


def send(value, axis, s):
    if s == 0:
        return value
    return lax.ppermute(value, axis, [(d, d ^ s) for d in range(lax.axis_size(axis))])


def spread(values, axis):
    return [(whole, send(values[s], axis, s)) for s in reversed(range(len(values)))]


def local(u_data, u_basis, v_basis, ranks, time_mask):
    freqs, row_count, width = u_data.shape
    rows, col_tiles, _, slots, tile = u_basis.shape[1:]
    row_tiles, cols = v_basis.shape[1:3]
    total = slots // 6 + slots
    pairs = freqs // 2
    devices = lax.axis_size("tile")
    owners = lax.axis_size("freq")
    stage_rows = rows * total + 2 * slots
    quarter = width // 2 // owners
    count = owners * freqs
    side = count * 2 * quarter
    by_cols = u_basis.reshape(freqs, rows, devices, cols, 2, slots, tile)
    by_rows = v_basis.reshape(freqs, devices, rows, cols, 2, slots, tile)
    per_device = [((pairs, cols * rows * total, width), bf16)] * devices
    per_owner = [((freqs, 2 * quarter, cols * tile), bf16)] * owners
    work = {"flops": 4 * row_count * slots * width * col_tiles * freqs * 2, "moved": u_basis.size * 2}
    ranks_here = pltpu.SMEM(ranks.shape, jnp.int32)
    stage = pltpu.VMEM((pairs * devices * cols, stage_rows, width), f32)
    one = pltpu.SemaphoreType.DMA

    table = lag_tables(count, time_mask.shape[0], 128)
    choice, same = lag_choice(count, quarter)
    window = call(
        window_kernel,
        "window",
        [(whole, jnp.asarray(x)) for x in (time_mask, table, choice, same)],
        [((side, side), bf16)] * 2,
        [pltpu.VMEM((width // 2, 128), f32)],
        flops=6 * quarter * 2 * count * 2 * count * side,
    )

    parts = math.gcd(devices, 2)
    *packed, near = call(
        functools.partial(adjoint_kernel, devices, parts),
        "adjoint",
        [(far, hold(x)) for x in (ranks, u_data, by_cols, by_rows)],
        per_device + [(by_rows.shape, bf16)],
        [
            ranks_here,
            pltpu.VMEM((freqs, row_count, width), bf16),
            pltpu.VMEM(by_cols.shape, bf16),
            pltpu.VMEM((freqs, row_count, width), bf16),
            stage,
            one((3 + freqs * rows * parts,)),
        ],
        **work,
    )
    images = call(
        functools.partial(image_kernel, devices, owners),
        "image",
        [(whole, ranks), (whole, near)] + spread(packed, "tile") + [(anywhere, window[0])],
        per_owner,
        [
            ranks_here,
            stage,
            pltpu.VMEM((cols, 2, row_tiles * slots, width), bf16),
            pltpu.VMEM((freqs, width, cols * tile), f32),
            one,
        ],
        **work,
    )
    mixed = call(
        functools.partial(mix_kernel, owners),
        "mix",
        [(whole, x) for x in window] + spread(images, "freq"),
        per_owner,
        [pltpu.VMEM((side, cols * tile), bf16), pltpu.VMEM((side, cols * tile), f32)],
        flops=4 * side * side * cols * tile,
    )
    packed = call(
        functools.partial(forward_kernel, devices, owners),
        "forward",
        [(whole, ranks), (whole, near)] + spread(mixed, "freq"),
        per_device,
        [ranks_here, pltpu.VMEM((freqs, cols, width, 2 * tile), bf16), stage, one],
        **work,
    )
    [out] = call(
        functools.partial(result_kernel, devices),
        "result",
        [(whole, ranks), (whole, by_cols)] + spread(packed, "tile"),
        [((freqs, row_count, width), bf16)],
        [ranks_here, stage, pltpu.VMEM((rows, 2, col_tiles * slots, width), bf16), one],
        **work,
    )
    return out


def solution(mesh):
    placed = (
        P("freq", "tile", None),
        P("freq", "tile", None, None, None, None),
        P("freq", None, "tile", None, None, None),
        P("freq", None, None),
        P(),
    )
    return jax.shard_map(
        local, mesh=mesh, in_specs=placed, out_specs=P("freq", "tile", None), check_vma=False
    )
```

time: 87.7 us -> 54.2 us (0.62)
  blocking collectives: 24.6 us -> 0 us
  matrix products: 19.2 us -> 0 us
  starting transfers between devices: 10 us -> 26.2 us
  Pallas kernels: 0 us -> 11 us
  local copies, waits for them, and re-layouts: 8.38 us -> 0.02 us
  other arithmetic: 5.69 us -> 0 us
  waiting for transfers between devices: 19.1 us -> 16.6 us
    ppermute x0 -> x20, starting transfers between devices: none -> 26.2 us  [send(): lax.ppermute(value, axis, [(d, d ^ s) for d in range(lax.axis_size(axis))])]
    all_to_all x2 -> x0, blocking collectives: 24.6 us -> none  [the longest x1 16.5 us: local(): lax.all_to_all(packed, 'tile', split_axis=1, concat_axis=2, tiled=True)]
    dot_general x16 -> x0, matrix products: 19.2 us -> none  [the longest x1 3.6 us: local(): jnp.einsum('tf,fnq->tnq', sin_table, rotate(values), precision=highest)]
    all_to_all x2 -> x0, waiting for transfers between devices: 19.1 us -> none  [the longest x1 13.8 us: local(): lax.all_to_all(packed, 'tile', split_axis=2, concat_axis=1, tiled=True)]
    ppermute x0 -> x20, waiting for transfers between devices: none -> 16.6 us  [send(): lax.ppermute(value, axis, [(d, d ^ s) for d in range(lax.axis_size(axis))])]
    pallas_call x0 -> x6, Pallas kernels: none -> 11 us  [call(): pl.pallas_call(kernel, in_specs=specs, out_specs=[whole] * len(outs), out...]
    all_to_all x2 -> x0, starting transfers between devices: 10 us -> none  [the longest x1 6.32 us: local(): lax.all_to_all(packed, 'tile', split_axis=2, concat_axis=1, tiled=True)]
    convert_element_type x3 -> x0, local copies, waits for them, and re-layouts: 2.74 us -> none  [the longest x1 1.91 us: local(): columns.reshape(freq_local, col_tiles * tile_width, width)]
  transfers between devices with their start and end apart: 2 -> 20, of which waited for: 2 -> 12; matrix products, arithmetic and copies ran while one was open for 0% -> 0% of each run, Pallas kernels for 0% -> 1%
where the time goes in v1:
time: 54.2 us; the launch traced here: 54 us
  starting transfers between devices  26.2 us (48%)
  waiting for transfers between devices  16.6 us (31%)
  Pallas kernels  11 us (20%)
    ppermute x20, starting transfers between devices, send(): lax.ppermute(value, axis, [(d, d ^ s) for d in range(lax.axis_size(axis))])  26.2 us
    ppermute x20, waiting for transfers between devices, send(): lax.ppermute(value, axis, [(d, d ^ s) for d in range(lax.axis_size(axis))])  16.6 us
    pallas_call x6, Pallas kernels, call(): pl.pallas_call(kernel, in_specs=specs, out_specs=[whole] * len(outs), out...  11 us
  transfers between devices with their start and end apart: 20, of which 12 were waited for; matrix products, arithmetic and copies ran while one was open for 0% of the time, Pallas kernels for 1%

profile of v1, /device:TPU:0, one launch (start us, length us, event | category | flops | bytes accessed | tf_op | source)
XLA Modules:
  0.0 54.0 jit_solution(9192487682572096745)
XLA Ops:
  0.0 4.1 %adjoint.1 = (bf16[1,224,128]{2,1,0:T(8,128)(2,1)S(1)}, bf16[1,224,128]{2,1,0:T(8,128)(2,1)S(1)}, bf16[1,224,128]{2,1,0:T(8,128)(2,1)S(1)}, bf16[1,224,128]{2,1,...) custom-call(s32[2,16,16]{2,1,0:T(8,128)} %ranks_near.5, ...), custom_call_target="tpu_custom_call" | custom-call | flops 805306368 | bytes 3145728 | tf_op jit(solution)/shard_map/adjoint/pallas_call | solution.py:29
  4.1 4.6 %collective-permute-start = (bf16[1,224,128]{2,1,0:T(8,128)(2,1)S(1)}, bf16[1,224,128]{2,1,0:T(8,128)(2,1)S(1)}, u32[]{:S(2)}, u32[]{:S(2)}) collective-permute-start(bf16[1,224,128]{2,1,0:T(8,128)(2,1)S(1)} %get-tuple-element.35), channel_id=1, source_target_pairs={{0,7},{1,6},{2,5},{3,4},{4,3},{5,2},{6,1},{7,0},{8,15},{9,14},{10,... | collective-permute-start | bytes 172040 | tf_op jit(solution)/shard_map/ppermute | solution.py:297
  8.7 0.6 %collective-permute-start.1 = (bf16[1,224,128]{2,1,0:T(8,128)(2,1)S(1)}, bf16[1,224,128]{2,1,0:T(8,128)(2,1)S(1)}, u32[]{:S(2)}, u32[]{:S(2)}) collective-permute-start(bf16[1,224,128]{2,1,0:T(8,128)(2,1)S(1)} %get-tuple-element.36), channel_id=1, source_target_pairs={{0,6},{1,7},{2,4},{3,5},{4,2},{5,3},{6,0},{7,1},{8,14},{9,15},{10,... | collective-permute-start | bytes 172040 | tf_op jit(solution)/shard_map/ppermute | solution.py:297
  9.7 2.2 %collective-permute-start.3 = (bf16[1,224,128]{2,1,0:T(8,128)(2,1)S(1)}, bf16[1,224,128]{2,1,0:T(8,128)(2,1)S(1)}, u32[]{:S(2)}, u32[]{:S(2)}) collective-permute-start(bf16[1,224,128]{2,1,0:T(8,128)(2,1)S(1)} %get-tuple-element.38), channel_id=1, source_target_pairs={{0,4},{1,5},{2,6},{3,7},{4,0},{5,1},{6,2},{7,3},{8,12},{9,13},{10,... | collective-permute-start | bytes 172040 | tf_op jit(solution)/shard_map/ppermute | solution.py:297
  11.9 1.0 %collective-permute-start.4 = (bf16[1,224,128]{2,1,0:T(8,128)(2,1)S(1)}, bf16[1,224,128]{2,1,0:T(8,128)(2,1)S(1)}, u32[]{:S(2)}, u32[]{:S(2)}) collective-permute-start(bf16[1,224,128]{2,1,0:T(8,128)(2,1)S(1)} %get-tuple-element.39), channel_id=1, source_target_pairs={{0,3},{1,2},{2,1},{3,0},{4,7},{5,6},{6,5},{7,4},{8,11},{9,10},{10,... | collective-permute-start | bytes 172040 | tf_op jit(solution)/shard_map/ppermute | solution.py:297
  12.9 0.9 %collective-permute-start.5 = (bf16[1,224,128]{2,1,0:T(8,128)(2,1)S(1)}, bf16[1,224,128]{2,1,0:T(8,128)(2,1)S(1)}, u32[]{:S(2)}, u32[]{:S(2)}) collective-permute-start(bf16[1,224,128]{2,1,0:T(8,128)(2,1)S(1)} %get-tuple-element.40), channel_id=1, source_target_pairs={{0,2},{1,3},{2,0},{3,1},{4,6},{5,7},{6,4},{7,5},{8,10},{9,11},{10,... | collective-permute-start | bytes 172040 | tf_op jit(solution)/shard_map/ppermute | solution.py:297
  13.8 1.7 %collective-permute-done.1.rest_1_ = bf16[1,224,128]{2,1,0:T(8,128)(2,1)S(1)} collective-permute-done((bf16[1,224,128]{2,1,0:T(8,128)(2,1)S(1)}, bf16[1,224,128]{2,1,0:T(8,128)(2,1)S(1)}, u32[]{:S(2)}, u32[]{:S(2)}) %collective-permute-start.1) | collective-permute-done | bytes 57376 | tf_op jit(solution)/shard_map/ppermute | solution.py:297
  15.4 0.7 %window.1 = (bf16[256,256]{1,0:T(8,128)(2,1)S(1)}, bf16[256,256]{1,0:T(8,128)(2,1)S(1)}) custom-call(s32[64,64]{1,0:T(8,128)S(1)} %copy-done.3, f32[64,128]{1,0:T(8,128)S(1)} %copy-done.4, f32[16,4096]{1,0:T(8,128)S(1)} %copy-done.2, f32[16,256]{1,0:T(8,128)S(1)} %copy-done.5), custom_call_target="tpu_custom_call" | custom-call | flops 6291456 | tf_op jit(solution)/shard_map/window/pallas_call | solution.py:29
  16.2 2.0 %collective-permute-done.2.rest_2_ = bf16[1,224,128]{2,1,0:T(8,128)(2,1)S(1)} collective-permute-done((bf16[1,224,128]{2,1,0:T(8,128)(2,1)S(1)}, bf16[1,224,128]{2,1,0:T(8,128)(2,1)S(1)}, u32[]{:S(2)}, u32[]{:S(2)}) %collective-permute-start.2) | collective-permute-done | bytes 57376 | tf_op jit(solution)/shard_map/ppermute | solution.py:297
  18.2 1.4 %collective-permute-done.3.rest_3_ = bf16[1,224,128]{2,1,0:T(8,128)(2,1)S(1)} collective-permute-done((bf16[1,224,128]{2,1,0:T(8,128)(2,1)S(1)}, bf16[1,224,128]{2,1,0:T(8,128)(2,1)S(1)}, u32[]{:S(2)}, u32[]{:S(2)}) %collective-permute-start.3) | collective-permute-done | bytes 57376 | tf_op jit(solution)/shard_map/ppermute | solution.py:297
  19.6 1.6 %image.1 = (bf16[2,32,512]{2,1,0:T(8,128)(2,1)S(1)}, bf16[2,32,512]{2,1,0:T(8,128)(2,1)S(1)}, bf16[2,32,512]{2,1,0:T(8,128)(2,1)S(1)}, bf16[2,32,512]{2,1,0:T(8,128)(2,1)S(1)}) custom-call(s32[2,16,16]{2,1,0:T(8,128)S(1)} %copy-done.1, bf16[2,8,2,2,2,48,256]{6,5,4,3,2,1,0:T(8,128)(2,1)S(1)} %get-tuple-element.32.basis, ...), custom_call_target="tpu_custom_call" | custom-call | flops 805306368 | bytes 3145728 | tf_op jit(solution)/shard_map/image/pallas_call | solution.py:29
  21.2 2.5 %collective-permute-start.7 = (bf16[2,32,512]{2,1,0:T(8,128)(2,1)S(1)}, bf16[2,32,512]{2,1,0:T(8,128)(2,1)S(1)}, u32[]{:S(2)}, u32[]{:S(2)}) collective-permute-start(bf16[2,32,512]{2,1,0:T(8,128)(2,1)S(1)} %get-tuple-element.43), channel_id=1, source_target_pairs={{0,24},{8,16},{16,8},{24,0},{1,25},{9,17},{17,9},{25,1},{2,26},{10... | collective-permute-start | bytes 196616 | tf_op jit(solution)/shard_map/ppermute | solution.py:297
  24.2 0.5 %collective-permute-start.9 = (bf16[2,32,512]{2,1,0:T(8,128)(2,1)S(1)}, bf16[2,32,512]{2,1,0:T(8,128)(2,1)S(1)}, u32[]{:S(2)}, u32[]{:S(2)}) collective-permute-start(bf16[2,32,512]{2,1,0:T(8,128)(2,1)S(1)} %get-tuple-element.45), channel_id=1, source_target_pairs={{0,8},{8,0},{16,24},{24,16},{1,9},{9,1},{17,25},{25,17},{2,10},{10... | collective-permute-start | bytes 196616 | tf_op jit(solution)/shard_map/ppermute | solution.py:297
  24.8 1.7 %collective-permute-done.7.rest_0_ = bf16[2,32,512]{2,1,0:T(8,128)(2,1)S(1)} collective-permute-done((bf16[2,32,512]{2,1,0:T(8,128)(2,1)S(1)}, bf16[2,32,512]{2,1,0:T(8,128)(2,1)S(1)}, u32[]{:S(2)}, u32[]{:S(2)}) %collective-permute-start.7) | collective-permute-done | bytes 65568 | tf_op jit(solution)/shard_map/ppermute | solution.py:297
  26.5 1.5 %collective-permute-done.8.rest_1_ = bf16[2,32,512]{2,1,0:T(8,128)(2,1)S(1)} collective-permute-done((bf16[2,32,512]{2,1,0:T(8,128)(2,1)S(1)}, bf16[2,32,512]{2,1,0:T(8,128)(2,1)S(1)}, u32[]{:S(2)}, u32[]{:S(2)}) %collective-permute-start.8) | collective-permute-done | bytes 65568 | tf_op jit(solution)/shard_map/ppermute | solution.py:297
  28.0 0.5 collective-permute-done.9.rest_2_
  28.9 1.6 %collective-permute-start.10 = (bf16[2,32,512]{2,1,0:T(8,128)(2,1)S(1)}, bf16[2,32,512]{2,1,0:T(8,128)(2,1)S(1)}, u32[]{:S(2)}, u32[]{:S(2)}) collective-permute-start(bf16[2,32,512]{2,1,0:T(8,128)(2,1)S(1)} %get-tuple-element.47), channel_id=1, source_target_pairs={{0,24},{8,16},{16,8},{24,0},{1,25},{9,17},{17,9},{25,1},{2,26},{10... | collective-permute-start | bytes 196616 | tf_op jit(solution)/shard_map/ppermute | solution.py:297
  30.4 0.6 %collective-permute-start.11 = (bf16[2,32,512]{2,1,0:T(8,128)(2,1)S(1)}, bf16[2,32,512]{2,1,0:T(8,128)(2,1)S(1)}, u32[]{:S(2)}, u32[]{:S(2)}) collective-permute-start(bf16[2,32,512]{2,1,0:T(8,128)(2,1)S(1)} %get-tuple-element.48), channel_id=1, source_target_pairs={{0,16},{8,24},{16,0},{24,8},{1,17},{9,25},{17,1},{25,9},{2,18},{10... | collective-permute-start | bytes 196616 | tf_op jit(solution)/shard_map/ppermute | solution.py:297
  31.0 1.4 %collective-permute-start.12 = (bf16[2,32,512]{2,1,0:T(8,128)(2,1)S(1)}, bf16[2,32,512]{2,1,0:T(8,128)(2,1)S(1)}, u32[]{:S(2)}, u32[]{:S(2)}) collective-permute-start(bf16[2,32,512]{2,1,0:T(8,128)(2,1)S(1)} %get-tuple-element.49), channel_id=1, source_target_pairs={{0,8},{8,0},{16,24},{24,16},{1,9},{9,1},{17,25},{25,17},{2,10},{10... | collective-permute-start | bytes 196616 | tf_op jit(solution)/shard_map/ppermute | solution.py:297
  32.4 1.7 %collective-permute-done.10.rest_0_ = bf16[2,32,512]{2,1,0:T(8,128)(2,1)S(1)} collective-permute-done((bf16[2,32,512]{2,1,0:T(8,128)(2,1)S(1)}, bf16[2,32,512]{2,1,0:T(8,128)(2,1)S(1)}, u32[]{:S(2)}, u32[]{:S(2)}) %collective-permute-start.10) | collective-permute-done | bytes 65568 | tf_op jit(solution)/shard_map/ppermute | solution.py:297
  34.1 0.7 %collective-permute-done.11.rest_1_ = bf16[2,32,512]{2,1,0:T(8,128)(2,1)S(1)} collective-permute-done((bf16[2,32,512]{2,1,0:T(8,128)(2,1)S(1)}, bf16[2,32,512]{2,1,0:T(8,128)(2,1)S(1)}, u32[]{:S(2)}, u32[]{:S(2)}) %collective-permute-start.11) | collective-permute-done | bytes 65568 | tf_op jit(solution)/shard_map/ppermute | solution.py:297
  35.3 1.8 %forward.1 = (bf16[1,224,128]{2,1,0:T(8,128)(2,1)S(1)}, bf16[1,224,128]{2,1,0:T(8,128)(2,1)S(1)}, bf16[1,224,128]{2,1,0:T(8,128)(2,1)S(1)}, bf16[1,224,128]{2,1,...) custom-call(s32[2,16,16]{2,1,0:T(8,128)S(1)} %copy-done.1, ...), custom_call_target="tpu_custom_call" | custom-call | flops 805306368 | bytes 3145728 | tf_op jit(solution)/shard_map/forward/pallas_call | solution.py:29
  37.1 2.4 %collective-permute-start.13 = (bf16[1,224,128]{2,1,0:T(8,128)(2,1)S(1)}, bf16[1,224,128]{2,1,0:T(8,128)(2,1)S(1)}, u32[]{:S(2)}, u32[]{:S(2)}) collective-permute-start(bf16[1,224,128]{2,1,0:T(8,128)(2,1)S(1)} %get-tuple-element.51), channel_id=1, source_target_pairs={{0,7},{1,6},{2,5},{3,4},{4,3},{5,2},{6,1},{7,0},{8,15},{9,14},{10,... | collective-permute-start | bytes 172040 | tf_op jit(solution)/shard_map/ppermute | solution.py:297
  39.5 1.7 %collective-permute-start.14 = (bf16[1,224,128]{2,1,0:T(8,128)(2,1)S(1)}, bf16[1,224,128]{2,1,0:T(8,128)(2,1)S(1)}, u32[]{:S(2)}, u32[]{:S(2)}) collective-permute-start(bf16[1,224,128]{2,1,0:T(8,128)(2,1)S(1)} %get-tuple-element.52), channel_id=1, source_target_pairs={{0,6},{1,7},{2,4},{3,5},{4,2},{5,3},{6,0},{7,1},{8,14},{9,15},{10,... | collective-permute-start | bytes 172040 | tf_op jit(solution)/shard_map/ppermute | solution.py:297
  41.2 2.6 %collective-permute-start.16 = (bf16[1,224,128]{2,1,0:T(8,128)(2,1)S(1)}, bf16[1,224,128]{2,1,0:T(8,128)(2,1)S(1)}, u32[]{:S(2)}, u32[]{:S(2)}) collective-permute-start(bf16[1,224,128]{2,1,0:T(8,128)(2,1)S(1)} %get-tuple-element.54), channel_id=1, source_target_pairs={{0,4},{1,5},{2,6},{3,7},{4,0},{5,1},{6,2},{7,3},{8,12},{9,13},{10,... | collective-permute-start | bytes 172040 | tf_op jit(solution)/shard_map/ppermute | solution.py:297
  43.7 0.9 %collective-permute-start.17 = (bf16[1,224,128]{2,1,0:T(8,128)(2,1)S(1)}, bf16[1,224,128]{2,1,0:T(8,128)(2,1)S(1)}, u32[]{:S(2)}, u32[]{:S(2)}) collective-permute-start(bf16[1,224,128]{2,1,0:T(8,128)(2,1)S(1)} %get-tuple-element.55), channel_id=1, source_target_pairs={{0,3},{1,2},{2,1},{3,0},{4,7},{5,6},{6,5},{7,4},{8,11},{9,10},{10,... | collective-permute-start | bytes 172040 | tf_op jit(solution)/shard_map/ppermute | solution.py:297
  44.7 0.9 %collective-permute-start.18 = (bf16[1,224,128]{2,1,0:T(8,128)(2,1)S(1)}, bf16[1,224,128]{2,1,0:T(8,128)(2,1)S(1)}, u32[]{:S(2)}, u32[]{:S(2)}) collective-permute-start(bf16[1,224,128]{2,1,0:T(8,128)(2,1)S(1)} %get-tuple-element.56), channel_id=1, source_target_pairs={{0,2},{1,3},{2,0},{3,1},{4,6},{5,7},{6,4},{7,5},{8,10},{9,11},{10,... | collective-permute-start | bytes 172040 | tf_op jit(solution)/shard_map/ppermute | solution.py:297
  45.6 1.1 %collective-permute-start.19 = (bf16[1,224,128]{2,1,0:T(8,128)(2,1)S(1)}, bf16[1,224,128]{2,1,0:T(8,128)(2,1)S(1)}, u32[]{:S(2)}, u32[]{:S(2)}) collective-permute-start(bf16[1,224,128]{2,1,0:T(8,128)(2,1)S(1)} %get-tuple-element.57), channel_id=1, source_target_pairs={{0,1},{1,0},{2,3},{3,2},{4,5},{5,4},{6,7},{7,6},{8,9},{9,8},{10,11... | collective-permute-start | bytes 172040 | tf_op jit(solution)/shard_map/ppermute | solution.py:297
  46.6 3.2 %collective-permute-done.15.rest_2_ = bf16[1,224,128]{2,1,0:T(8,128)(2,1)S(1)} collective-permute-done((bf16[1,224,128]{2,1,0:T(8,128)(2,1)S(1)}, bf16[1,224,128]{2,1,0:T(8,128)(2,1)S(1)}, u32[]{:S(2)}, u32[]{:S(2)}) %collective-permute-start.15) | collective-permute-done | bytes 57376 | tf_op jit(solution)/shard_map/ppermute | solution.py:297
  49.9 1.3 %collective-permute-done.16.rest_3_ = bf16[1,224,128]{2,1,0:T(8,128)(2,1)S(1)} collective-permute-done((bf16[1,224,128]{2,1,0:T(8,128)(2,1)S(1)}, bf16[1,224,128]{2,1,0:T(8,128)(2,1)S(1)}, u32[]{:S(2)}, u32[]{:S(2)}) %collective-permute-start.16) | collective-permute-done | bytes 57376 | tf_op jit(solution)/shard_map/ppermute | solution.py:297
  51.1 0.5 collective-permute-done.18.rest_5_
  51.6 2.4 %result.1 = bf16[2,512,128]{2,1,0:T(8,128)(2,1)} custom-call(s32[2,16,16]{2,1,0:T(8,128)S(1)} %copy-done.1, bf16[2,2,8,2,2,48,256]{6,5,4,3,2,1,0:T(8,128)(2,1)S(1)} %bitcast.3, bf16[1,224,128]{2,1,0:T(8,128)(2,1)S(1)} %collective-permute-done.13.rest_0_, bf16[1,224,128]{2,1,0:T(8,128)(2,1)S(1)} %collective-permute-done.14.rest_1_, ...), custom_call_target="tpu_custom_call" | custom-call | flops 805306368 | bytes 3145728 | tf_op jit(solution)/shard_map/result/pallas_call | solution.py:29
  (26 shorter events, 1.7 us)
Async XLA Ops:
  0.0 15.4 %copy-start.2 = (f32[16,4096]{1,0:T(8,128)S(1)}, f32[16,4096]{1,0:T(8,128)}, u32[]{:S(2)}) copy-start(f32[16,4096]{1,0:T(8,128)} %constant.7.clone.choice) | copy-start | bytes 786436
  0.0 15.4 %copy-start.3 = (s32[64,64]{1,0:T(8,128)S(1)}, s32[64,64]{1,0:T(8,128)}, u32[]{:S(2)}) copy-start(s32[64,64]{1,0:T(8,128)} %mask.1) | copy-start | bytes 49156
  0.0 15.4 %copy-start.4 = (f32[64,128]{1,0:T(8,128)S(1)}, f32[64,128]{1,0:T(8,128)}, u32[]{:S(2)}) copy-start(f32[64,128]{1,0:T(8,128)} %constant.6.clone.table) | copy-start | bytes 98308
  0.0 15.4 %copy-start.5 = (f32[16,256]{1,0:T(8,128)S(1)}, f32[16,256]{1,0:T(8,128)}, u32[]{:S(2)}) copy-start(f32[16,256]{1,0:T(8,128)} %constant.8.clone.same) | copy-start | bytes 49156
  0.0 19.6 %copy-start.1 = (s32[2,16,16]{2,1,0:T(8,128)S(1)}, s32[2,16,16]{2,1,0:T(8,128)}, u32[]{:S(2)}) copy-start(s32[2,16,16]{2,1,0:T(8,128)} %ranks_near.5) | copy-start | bytes 6148
  4.1 8.8 %collective-permute-start = (bf16[1,224,128]{2,1,0:T(8,128)(2,1)S(1)}, bf16[1,224,128]{2,1,0:T(8,128)(2,1)S(1)}, u32[]{:S(2)}, u32[]{:S(2)}) collective-permute-start(bf16[1,224,128]{2,1,0:T(8,128)(2,1)S(1)} %get-tuple-element.35), channel_id=1, source_target_pairs={{0,7},{1,6},{2,5},{3,4},{4,3},{5,2},{6,1},{7,0},{8,15},{9,14},{10,... | collective-permute-start | bytes 172040 | tf_op jit(solution)/shard_map/ppermute | solution.py:297
  8.7 6.7 %collective-permute-start.1 = (bf16[1,224,128]{2,1,0:T(8,128)(2,1)S(1)}, bf16[1,224,128]{2,1,0:T(8,128)(2,1)S(1)}, u32[]{:S(2)}, u32[]{:S(2)}) collective-permute-start(bf16[1,224,128]{2,1,0:T(8,128)(2,1)S(1)} %get-tuple-element.36), channel_id=1, source_target_pairs={{0,6},{1,7},{2,4},{3,5},{4,2},{5,3},{6,0},{7,1},{8,14},{9,15},{10,... | collective-permute-start | bytes 172040 | tf_op jit(solution)/shard_map/ppermute | solution.py:297
  9.4 8.8 %collective-permute-start.2 = (bf16[1,224,128]{2,1,0:T(8,128)(2,1)S(1)}, bf16[1,224,128]{2,1,0:T(8,128)(2,1)S(1)}, u32[]{:S(2)}, u32[]{:S(2)}) collective-permute-start(bf16[1,224,128]{2,1,0:T(8,128)(2,1)S(1)} %get-tuple-element.37), channel_id=1, source_target_pairs={{0,5},{1,4},{2,7},{3,6},{4,1},{5,0},{6,3},{7,2},{8,13},{9,12},{10,... | collective-permute-start | bytes 172040 | tf_op jit(solution)/shard_map/ppermute | solution.py:297
  9.7 9.8 %collective-permute-start.3 = (bf16[1,224,128]{2,1,0:T(8,128)(2,1)S(1)}, bf16[1,224,128]{2,1,0:T(8,128)(2,1)S(1)}, u32[]{:S(2)}, u32[]{:S(2)}) collective-permute-start(bf16[1,224,128]{2,1,0:T(8,128)(2,1)S(1)} %get-tuple-element.38), channel_id=1, source_target_pairs={{0,4},{1,5},{2,6},{3,7},{4,0},{5,1},{6,2},{7,3},{8,12},{9,13},{10,... | collective-permute-start | bytes 172040 | tf_op jit(solution)/shard_map/ppermute | solution.py:297
  11.9 7.6 %collective-permute-start.4 = (bf16[1,224,128]{2,1,0:T(8,128)(2,1)S(1)}, bf16[1,224,128]{2,1,0:T(8,128)(2,1)S(1)}, u32[]{:S(2)}, u32[]{:S(2)}) collective-permute-start(bf16[1,224,128]{2,1,0:T(8,128)(2,1)S(1)} %get-tuple-element.39), channel_id=1, source_target_pairs={{0,3},{1,2},{2,1},{3,0},{4,7},{5,6},{6,5},{7,4},{8,11},{9,10},{10,... | collective-permute-start | bytes 172040 | tf_op jit(solution)/shard_map/ppermute | solution.py:297
  12.9 6.7 %collective-permute-start.5 = (bf16[1,224,128]{2,1,0:T(8,128)(2,1)S(1)}, bf16[1,224,128]{2,1,0:T(8,128)(2,1)S(1)}, u32[]{:S(2)}, u32[]{:S(2)}) collective-permute-start(bf16[1,224,128]{2,1,0:T(8,128)(2,1)S(1)} %get-tuple-element.40), channel_id=1, source_target_pairs={{0,2},{1,3},{2,0},{3,1},{4,6},{5,7},{6,4},{7,5},{8,10},{9,11},{10,... | collective-permute-start | bytes 172040 | tf_op jit(solution)/shard_map/ppermute | solution.py:297
  15.4 4.2 %collective-permute-start.6 = (bf16[1,224,128]{2,1,0:T(8,128)(2,1)S(1)}, bf16[1,224,128]{2,1,0:T(8,128)(2,1)S(1)}, u32[]{:S(2)}, u32[]{:S(2)}) collective-permute-start(bf16[1,224,128]{2,1,0:T(8,128)(2,1)S(1)} %get-tuple-element.41), channel_id=1, source_target_pairs={{0,1},{1,0},{2,3},{3,2},{4,5},{5,4},{6,7},{7,6},{8,9},{9,8},{10,11... | collective-permute-start | bytes 172040 | tf_op jit(solution)/shard_map/ppermute | solution.py:297
  19.6 32.1 %copy-start = (bf16[2,2,16,2,48,256]{5,4,3,2,1,0:T(8,128)(2,1)S(1)}, bf16[2,2,16,2,48,256]{5,4,3,2,1,0:T(8,128)(2,1)}, u32[]{:S(2)}) copy-start(bf16[2,2,16,2,48,256]{5,4,3,2,1,0:T(8,128)(2,1)} %param.9) | copy-start | bytes 9437188
  21.2 5.3 %collective-permute-start.7 = (bf16[2,32,512]{2,1,0:T(8,128)(2,1)S(1)}, bf16[2,32,512]{2,1,0:T(8,128)(2,1)S(1)}, u32[]{:S(2)}, u32[]{:S(2)}) collective-permute-start(bf16[2,32,512]{2,1,0:T(8,128)(2,1)S(1)} %get-tuple-element.43), channel_id=1, source_target_pairs={{0,24},{8,16},{16,8},{24,0},{1,25},{9,17},{17,9},{25,1},{2,26},{10... | collective-permute-start | bytes 196616 | tf_op jit(solution)/shard_map/ppermute | solution.py:297
  23.7 4.3 %collective-permute-start.8 = (bf16[2,32,512]{2,1,0:T(8,128)(2,1)S(1)}, bf16[2,32,512]{2,1,0:T(8,128)(2,1)S(1)}, u32[]{:S(2)}, u32[]{:S(2)}) collective-permute-start(bf16[2,32,512]{2,1,0:T(8,128)(2,1)S(1)} %get-tuple-element.44), channel_id=1, source_target_pairs={{0,16},{8,24},{16,0},{24,8},{1,17},{9,25},{17,1},{25,9},{2,18},{10... | collective-permute-start | bytes 196616 | tf_op jit(solution)/shard_map/ppermute | solution.py:297
  24.2 4.3 %collective-permute-start.9 = (bf16[2,32,512]{2,1,0:T(8,128)(2,1)S(1)}, bf16[2,32,512]{2,1,0:T(8,128)(2,1)S(1)}, u32[]{:S(2)}, u32[]{:S(2)}) collective-permute-start(bf16[2,32,512]{2,1,0:T(8,128)(2,1)S(1)} %get-tuple-element.45), channel_id=1, source_target_pairs={{0,8},{8,0},{16,24},{24,16},{1,9},{9,1},{17,25},{25,17},{2,10},{10... | collective-permute-start | bytes 196616 | tf_op jit(solution)/shard_map/ppermute | solution.py:297
  28.9 5.2 %collective-permute-start.10 = (bf16[2,32,512]{2,1,0:T(8,128)(2,1)S(1)}, bf16[2,32,512]{2,1,0:T(8,128)(2,1)S(1)}, u32[]{:S(2)}, u32[]{:S(2)}) collective-permute-start(bf16[2,32,512]{2,1,0:T(8,128)(2,1)S(1)} %get-tuple-element.47), channel_id=1, source_target_pairs={{0,24},{8,16},{16,8},{24,0},{1,25},{9,17},{17,9},{25,1},{2,26},{10... | collective-permute-start | bytes 196616 | tf_op jit(solution)/shard_map/ppermute | solution.py:297
  30.4 4.4 %collective-permute-start.11 = (bf16[2,32,512]{2,1,0:T(8,128)(2,1)S(1)}, bf16[2,32,512]{2,1,0:T(8,128)(2,1)S(1)}, u32[]{:S(2)}, u32[]{:S(2)}) collective-permute-start(bf16[2,32,512]{2,1,0:T(8,128)(2,1)S(1)} %get-tuple-element.48), channel_id=1, source_target_pairs={{0,16},{8,24},{16,0},{24,8},{1,17},{9,25},{17,1},{25,9},{2,18},{10... | collective-permute-start | bytes 196616 | tf_op jit(solution)/shard_map/ppermute | solution.py:297
  31.0 4.3 %collective-permute-start.12 = (bf16[2,32,512]{2,1,0:T(8,128)(2,1)S(1)}, bf16[2,32,512]{2,1,0:T(8,128)(2,1)S(1)}, u32[]{:S(2)}, u32[]{:S(2)}) collective-permute-start(bf16[2,32,512]{2,1,0:T(8,128)(2,1)S(1)} %get-tuple-element.49), channel_id=1, source_target_pairs={{0,8},{8,0},{16,24},{24,16},{1,9},{9,1},{17,25},{25,17},{2,10},{10... | collective-permute-start | bytes 196616 | tf_op jit(solution)/shard_map/ppermute | solution.py:297
  37.1 7.6 %collective-permute-start.13 = (bf16[1,224,128]{2,1,0:T(8,128)(2,1)S(1)}, bf16[1,224,128]{2,1,0:T(8,128)(2,1)S(1)}, u32[]{:S(2)}, u32[]{:S(2)}) collective-permute-start(bf16[1,224,128]{2,1,0:T(8,128)(2,1)S(1)} %get-tuple-element.51), channel_id=1, source_target_pairs={{0,7},{1,6},{2,5},{3,4},{4,3},{5,2},{6,1},{7,0},{8,15},{9,14},{10,... | collective-permute-start | bytes 172040 | tf_op jit(solution)/shard_map/ppermute | solution.py:297
  39.5 6.1 %collective-permute-start.14 = (bf16[1,224,128]{2,1,0:T(8,128)(2,1)S(1)}, bf16[1,224,128]{2,1,0:T(8,128)(2,1)S(1)}, u32[]{:S(2)}, u32[]{:S(2)}) collective-permute-start(bf16[1,224,128]{2,1,0:T(8,128)(2,1)S(1)} %get-tuple-element.52), channel_id=1, source_target_pairs={{0,6},{1,7},{2,4},{3,5},{4,2},{5,3},{6,0},{7,1},{8,14},{9,15},{10,... | collective-permute-start | bytes 172040 | tf_op jit(solution)/shard_map/ppermute | solution.py:297
  41.2 8.7 %collective-permute-start.15 = (bf16[1,224,128]{2,1,0:T(8,128)(2,1)S(1)}, bf16[1,224,128]{2,1,0:T(8,128)(2,1)S(1)}, u32[]{:S(2)}, u32[]{:S(2)}) collective-permute-start(bf16[1,224,128]{2,1,0:T(8,128)(2,1)S(1)} %get-tuple-element.53), channel_id=1, source_target_pairs={{0,5},{1,4},{2,7},{3,6},{4,1},{5,0},{6,3},{7,2},{8,13},{9,12},{10,... | collective-permute-start | bytes 172040 | tf_op jit(solution)/shard_map/ppermute | solution.py:297
  41.2 9.9 %collective-permute-start.16 = (bf16[1,224,128]{2,1,0:T(8,128)(2,1)S(1)}, bf16[1,224,128]{2,1,0:T(8,128)(2,1)S(1)}, u32[]{:S(2)}, u32[]{:S(2)}) collective-permute-start(bf16[1,224,128]{2,1,0:T(8,128)(2,1)S(1)} %get-tuple-element.54), channel_id=1, source_target_pairs={{0,4},{1,5},{2,6},{3,7},{4,0},{5,1},{6,2},{7,3},{8,12},{9,13},{10,... | collective-permute-start | bytes 172040 | tf_op jit(solution)/shard_map/ppermute | solution.py:297
  43.7 7.4 %collective-permute-start.17 = (bf16[1,224,128]{2,1,0:T(8,128)(2,1)S(1)}, bf16[1,224,128]{2,1,0:T(8,128)(2,1)S(1)}, u32[]{:S(2)}, u32[]{:S(2)}) collective-permute-start(bf16[1,224,128]{2,1,0:T(8,128)(2,1)S(1)} %get-tuple-element.55), channel_id=1, source_target_pairs={{0,3},{1,2},{2,1},{3,0},{4,7},{5,6},{6,5},{7,4},{8,11},{9,10},{10,... | collective-permute-start | bytes 172040 | tf_op jit(solution)/shard_map/ppermute | solution.py:297
  44.7 6.9 %collective-permute-start.18 = (bf16[1,224,128]{2,1,0:T(8,128)(2,1)S(1)}, bf16[1,224,128]{2,1,0:T(8,128)(2,1)S(1)}, u32[]{:S(2)}, u32[]{:S(2)}) collective-permute-start(bf16[1,224,128]{2,1,0:T(8,128)(2,1)S(1)} %get-tuple-element.56), channel_id=1, source_target_pairs={{0,2},{1,3},{2,0},{3,1},{4,6},{5,7},{6,4},{7,5},{8,10},{9,11},{10,... | collective-permute-start | bytes 172040 | tf_op jit(solution)/shard_map/ppermute | solution.py:297
  45.6 6.0 %collective-permute-start.19 = (bf16[1,224,128]{2,1,0:T(8,128)(2,1)S(1)}, bf16[1,224,128]{2,1,0:T(8,128)(2,1)S(1)}, u32[]{:S(2)}, u32[]{:S(2)}) collective-permute-start(bf16[1,224,128]{2,1,0:T(8,128)(2,1)S(1)} %get-tuple-element.57), channel_id=1, source_target_pairs={{0,1},{1,0},{2,3},{3,2},{4,5},{5,4},{6,7},{7,6},{8,9},{9,8},{10,11... | collective-permute-start | bytes 172040 | tf_op jit(solution)/shard_map/ppermute | solution.py:297

commit v2 on v1

v2 whole, which is shorter than its diff:
```python
import functools
import math

import jax
import jax.numpy as jnp
import numpy as np
from jax import lax
from jax.experimental import pallas as pl
from jax.experimental.pallas import tpu as pltpu
from jax.sharding import PartitionSpec as P

vmem_limit = 48 * 1024 * 1024
bf16 = jnp.bfloat16
f32 = jnp.float32

whole = pl.BlockSpec(memory_space=pltpu.VMEM)
scalars = pl.BlockSpec(memory_space=pltpu.SMEM)
far = pl.BlockSpec(memory_space=pltpu.HBM)
anywhere = pl.BlockSpec(memory_space=pl.ANY)


def hold(value):
    return pltpu.with_memory_space_constraint(value, pltpu.HBM)


def call(kernel, name, ins, outs, scratch, flops=0, moved=0):
    specs = [spec for spec, _ in ins]
    shapes = [jax.ShapeDtypeStruct(shape, kind) for shape, kind in outs]
    return pl.pallas_call(
        kernel,
        in_specs=specs,
        out_specs=[whole] * len(outs),
        out_shape=shapes,
        scratch_shapes=scratch,
        compiler_params=pltpu.CompilerParams(vmem_limit_bytes=vmem_limit),
        cost_estimate=pl.CostEstimate(flops=flops, bytes_accessed=moved, transcendentals=0),
        name=name,
    )(*[value for _, value in ins])


def dot(lhs, rhs, lhs_dim, rhs_dim, precision=None):
    return lax.dot_general(
        lhs, rhs, (((lhs_dim,), (rhs_dim,)), ((), ())),
        precision=precision, preferred_element_type=f32,
    )


def lag_tables(count, time_count, lanes):
    samples = np.arange(time_count)[:, None]
    lags = np.arange(count)[None, :]
    angle = 2.0 * math.pi / time_count * ((samples * lags) % time_count)
    table = np.zeros((time_count, lanes), np.float32)
    table[:, :count] = np.cos(angle) / time_count
    table[:, count : 2 * count] = np.sin(angle) / time_count
    return table


def lag_choice(count, quarter):
    side = count * 2 * quarter
    choice = np.zeros((2 * count, count, 2, count, 2, quarter), np.float32)
    for f in range(count):
        for g in range(count):
            sign = 1.0 if g >= f else -1.0
            lag = abs(g - f)
            choice[lag, f, 0, g, 0] = 1.0
            choice[lag, f, 1, g, 1] = 1.0
            choice[count + lag, f, 0, g, 1] = -sign
            choice[count + lag, f, 1, g, 0] = sign
    same = np.arange(quarter)[:, None] == np.arange(side)[None, :] % quarter
    return choice.reshape(2 * count, 2 * count * side), same.astype(np.float32)


def pack_rows(stage, slot, row, rank, first, second):
    size = first.shape[0]
    stage[slot, pl.ds(row, size), :] = first
    stage[slot, pl.ds(row + rank, size), :] = second


def unpack_rows(stage, slot, row, rank, total, coeffs, base):
    slots = total - total // 7
    first = stage[slot, pl.ds(row, slots), :]
    second = stage[slot, pl.ds(row + rank, slots), :]
    ids = lax.broadcasted_iota(jnp.int32, first.shape, 0)
    at = pl.ds(pl.multiple_of(base, 16), slots)
    coeffs[0, at, :] = jnp.where(ids < rank, first, 0.0).astype(bf16)
    coeffs[1, at, :] = jnp.where(ids < total - rank, second, 0.0).astype(bf16)


def side_by_side(real, imag):
    flat = (-1, real.shape[-1])
    return jnp.concatenate([real.reshape(flat), imag.reshape(flat)], axis=1)


def plain_product(coeffs, both):
    half, tile = coeffs.shape[1] // 2, both.shape[1] // 2
    product = dot(coeffs, both, 0, 0)
    lead, trail = product[:, :tile], product[:, tile:]
    return jnp.concatenate([lead[:half] - trail[half:], lead[half:] + trail[:half]], axis=0)


def split_blocks(devices):
    part = devices // 4
    return [(3 * part, part), (0, 2 * part), (2 * part, part)]


def block_base(me, block):
    first, size = block
    return (me ^ first) & ~(size - 1)


def unstage(outs, stage, m, slots, span, size, places):
    for out, place in zip(outs, places):
        for c in range(span):
            rows = stage[(m * slots + place) * span + c, pl.ds(0, size), :]
            out[m, pl.ds(c * size, size), :] = rows.astype(bf16)


def adjoint_kernel(blocks, bring, ranks_far, u_far, basis_far, other_far, *rest):
    partners = sum(size for _, size in blocks)
    ranks, u_ref, basis, turned, stage, sems = rest[-6:]
    outs = rest[-6 - partners - bring : -6 - bring]
    freqs, rows, _, cols, _, slots, tile = basis_far.shape
    total = slots + slots // 6
    half = u_ref.shape[2] // 2
    me = lax.axis_index("tile")
    rank_copy = pltpu.make_async_copy(ranks_far, ranks, sems.at[0])
    data_copy = pltpu.make_async_copy(u_far, u_ref, sems.at[1])
    data_copy.start()
    rank_copy.start()
    copies = {}
    at = 0
    for b, block in enumerate(blocks):
        for i in range(rows):
            for f in range(freqs):
                copies[b, i, f] = pltpu.make_async_copy(
                    basis_far.at[f, i, pl.ds(block_base(me, block), block[1])],
                    basis.at[f, i, pl.ds(at, block[1])],
                    sems.at[3 + (b * rows + i) * freqs + f],
                )
                copies[b, i, f].start()
        at += block[1]
    if bring:
        other_copy = pltpu.make_async_copy(other_far, rest[-7], sems.at[2])
        other_copy.start()
    data_copy.wait()
    for f in range(freqs):
        values = u_ref[f].astype(f32)
        lane = lax.broadcasted_iota(jnp.int32, values.shape, 1)
        rolled = pltpu.roll(values, half, 1)
        turned[f] = jnp.where(lane < half, rolled, -rolled).astype(bf16)
    rank_copy.wait()
    at = 0
    for b, block in enumerate(blocks):
        first, size = block
        base = block_base(me, block)
        for m in range(freqs // 2):
            for i in range(rows):
                here = pl.ds(i * tile, tile)
                pair = []
                for f in (2 * m, 2 * m + 1):
                    copies[b, i, f].wait()
                    both = side_by_side(basis[f, i, at : at + size, :, 0], basis[f, i, at : at + size, :, 1])
                    data = jnp.concatenate([u_ref[f, here, :], turned[f, here, :]], axis=0)
                    pair.append(dot(both, data, 1, 0))
                for n in range(size * cols):
                    rank = ranks[2 * m, me * rows + i, base * cols + n]
                    cut = slice(n * slots, (n + 1) * slots)
                    slot = (m * partners + at) * cols + n
                    pack_rows(stage, slot, i * total, rank, pair[0][cut], pair[1][cut])
            places = [at + ((me ^ (first + n)) & (size - 1)) for n in range(size)]
            unstage(outs[at : at + size], stage, m, partners, cols, rows * total, places)
        at += size
    if bring:
        other_copy.wait()


def image_kernel(block, owners, first, last, ranks_near, basis, *rest):
    packed, rest = rest[: block[1]][::-1], rest[block[1] :]
    if not first:
        before, rest = rest[0], rest[1:]
    ranks, stage, coeffs, z, sem = rest[-5:]
    freqs, _, rows, cols, _, slots, tile = basis.shape
    total = slots + slots // 6
    half = coeffs.shape[3] // 2
    quarter = half // owners
    size = rows * total
    start, count = block
    me, mine = lax.axis_index("tile"), lax.axis_index("freq")
    near = pl.ds(block_base(me, block), count)
    rank_copy = pltpu.make_async_copy(ranks_near, ranks, sem)
    rank_copy.start()
    for m in range(freqs // 2):
        for n in range(count):
            for c in range(cols):
                rows_in = packed[n][m, pl.ds(c * size, size), :]
                stage[(m * count + n) * cols + c, pl.ds(0, size), :] = rows_in.astype(f32)
    rank_copy.wait()
    for m in range(freqs // 2):
        for c in range(cols):
            for n in range(count):
                partner = me ^ (start + n)
                for i in range(rows):
                    rank = ranks[2 * m, partner * rows + i, me * cols + c]
                    slot = (m * count + n) * cols + c
                    place = ((partner & (count - 1)) * rows + i) * slots
                    unpack_rows(stage, slot, i * total, rank, total, coeffs.at[c], place)
            for n in range(2):
                f = 2 * m + n
                both = side_by_side(basis[f, near, :, c, 0], basis[f, near, :, c, 1])
                part = plain_product(coeffs[c, n], both)
                at = pl.ds(c * tile, tile)
                if not first:
                    part = part + before[f, :, at]
                if last:
                    z[f, :, at] = part
                else:
                    rest[-6][f, :, at] = part
    if last:
        outs = rest[-5 - owners : -5]
        for r in range(owners):
            low = pl.multiple_of((mine ^ r) * quarter, quarter)
            for f in range(freqs):
                real = z[f, pl.ds(low, quarter), :]
                imag = z[f, pl.ds(half + low, quarter), :]
                outs[r][f] = jnp.concatenate([real, imag], axis=0).astype(bf16)


def window_kernel(mask, table, choice, same, high, low, full):
    exact = lax.Precision.HIGHEST
    full[...] = dot(mask[...].astype(f32), table[...], 0, 0, exact)
    quarter, side = same.shape
    mine = full[pl.ds(pl.multiple_of(lax.axis_index("freq") * quarter, quarter), quarter), :]
    entries = dot(mine[:, : choice.shape[0]], choice[...], 1, 0, exact)
    for n in range(side // quarter):
        block = entries[:, n * side : (n + 1) * side] * same[...]
        upper = block.astype(bf16)
        high[n * quarter : (n + 1) * quarter, :] = upper
        low[n * quarter : (n + 1) * quarter, :] = (block - upper.astype(f32)).astype(bf16)


def mix_kernel(owners, high, low, *rest):
    arrived = rest[:owners][::-1]
    outs = rest[owners : 2 * owners]
    z, w = rest[2 * owners :]
    freqs, rows, span = arrived[0].shape
    mine = lax.axis_index("freq")
    size = freqs * rows
    for r in range(owners):
        z[pl.ds(pl.multiple_of((mine ^ r) * size, 16), size), :] = arrived[r][...].reshape(size, span)
    w[...] = dot(high[...], z[...], 1, 0) + dot(low[...], z[...], 1, 0)
    for r in range(owners):
        block = w[pl.ds(pl.multiple_of((mine ^ r) * size, 16), size), :]
        outs[r][...] = block.reshape(freqs, rows, span).astype(bf16)


def forward_kernel(blocks, owners, ranks_near, basis, *rest):
    partners = sum(size for _, size in blocks)
    ranks, stage, sem = rest[-3:]
    if owners:
        arrived = rest[:owners][::-1]
        outs, w = rest[-4 - partners : -4], rest[-4]
    else:
        outs, w = rest[-3 - partners : -3], rest[0]
    freqs, _, rows, cols, _, slots, tile = basis.shape
    total = slots + slots // 6
    half = w.shape[2] // 2
    me, mine = lax.axis_index("tile"), lax.axis_index("freq")
    rank_copy = pltpu.make_async_copy(ranks_near, ranks, sem)
    rank_copy.start()
    for r in range(owners):
        quarter = half // owners
        low = pl.multiple_of((mine ^ r) * quarter, quarter)
        for f in range(freqs):
            for c in range(cols):
                at = slice(c * tile, (c + 1) * tile)
                real, imag = arrived[r][f, :quarter, at], arrived[r][f, quarter:, at]
                w[f, c, pl.ds(low, quarter), :tile] = real
                w[f, c, pl.ds(half + low, quarter), :tile] = imag
                w[f, c, pl.ds(low, quarter), tile:] = imag
                w[f, c, pl.ds(half + low, quarter), tile:] = -real
    rank_copy.wait()
    at = 0
    for block in blocks:
        first, size = block
        base = block_base(me, block)
        near = pl.ds(base, size)
        for m in range(freqs // 2):
            for c in range(cols):
                pair = []
                for f in (2 * m, 2 * m + 1):
                    both = side_by_side(basis[f, near, :, c, 0], basis[f, near, :, c, 1])
                    pair.append(dot(both, w[f, c], 1, 1))
                for n in range(size):
                    for i in range(rows):
                        rank = ranks[2 * m, (base + n) * rows + i, me * cols + c]
                        cut = slice((n * rows + i) * slots, (n * rows + i + 1) * slots)
                        slot = (m * partners + at + n) * cols + c
                        pack_rows(stage, slot, i * total, rank, pair[0][cut], pair[1][cut])
            places = [at + ((me ^ (first + n)) & (size - 1)) for n in range(size)]
            unstage(outs[at : at + size], stage, m, partners, cols, rows * total, places)
        at += size


def result_kernel(block, first, last, ranks_near, basis, *rest):
    packed, rest = rest[: block[1]][::-1], rest[block[1] :]
    if not first:
        before, rest = rest[0], rest[1:]
    out, ranks, stage, coeffs, sem = rest
    freqs, rows, _, cols, _, slots, tile = basis.shape
    total = slots + slots // 6
    size = rows * total
    start, count = block
    me = lax.axis_index("tile")
    near = pl.ds(block_base(me, block), count)
    rank_copy = pltpu.make_async_copy(ranks_near, ranks, sem)
    rank_copy.start()
    for m in range(freqs // 2):
        for n in range(count):
            for c in range(cols):
                rows_in = packed[n][m, pl.ds(c * size, size), :]
                stage[(m * count + n) * cols + c, pl.ds(0, size), :] = rows_in.astype(f32)
    rank_copy.wait()
    for m in range(freqs // 2):
        for i in range(rows):
            for n in range(count):
                partner = me ^ (start + n)
                for c in range(cols):
                    rank = ranks[2 * m, me * rows + i, partner * cols + c]
                    slot = (m * count + n) * cols + c
                    place = ((partner & (count - 1)) * cols + c) * slots
                    unpack_rows(stage, slot, i * total, rank, total, coeffs.at[i], place)
            for n in range(2):
                f = 2 * m + n
                both = side_by_side(basis[f, i, near, :, 0], basis[f, i, near, :, 1])
                part = plain_product(coeffs[i, n], both)
                if not first:
                    part = part + before[f, i]
                if last:
                    out[f, pl.ds(i * tile, tile), :] = part.T.astype(bf16)
                else:
                    out[f, i] = part


def send(value, axis, s):
    if s == 0:
        return value
    return lax.ppermute(value, axis, [(d, d ^ s) for d in range(lax.axis_size(axis))])


def spread(values, axis, first=0):
    return [(whole, send(values[n], axis, first + n)) for n in reversed(range(len(values)))]


def local(u_data, u_basis, v_basis, ranks, time_mask):
    freqs, row_count, width = u_data.shape
    rows, col_tiles, _, slots, tile = u_basis.shape[1:]
    row_tiles, cols = v_basis.shape[1:3]
    total = slots // 6 + slots
    pairs = freqs // 2
    devices = lax.axis_size("tile")
    owners = lax.axis_size("freq")
    stage_rows = rows * total + 2 * slots
    quarter = width // 2 // owners
    count = owners * freqs
    side = count * 2 * quarter
    by_cols = u_basis.reshape(freqs, rows, devices, cols, 2, slots, tile)
    by_rows = v_basis.reshape(freqs, devices, rows, cols, 2, slots, tile)
    per_owner = [((freqs, 2 * quarter, cols * tile), bf16)] * owners
    work = {"flops": 4 * row_count * slots * width * col_tiles * freqs * 2, "moved": u_basis.size * 2}
    ranks_here = pltpu.SMEM(ranks.shape, jnp.int32)
    one = pltpu.SemaphoreType.DMA
    packed_kind = ((pairs, cols * rows * total, width), bf16)
    blocks = split_blocks(devices)

    def stage(partners):
        return pltpu.VMEM((pairs * partners * cols, stage_rows, width), f32)

    def share(partners):
        return {name: value * partners // devices for name, value in work.items()}

    table = lag_tables(count, time_mask.shape[0], 128)
    choice, same = lag_choice(count, quarter)
    window = call(
        window_kernel,
        "window",
        [(whole, jnp.asarray(x)) for x in (time_mask, table, choice, same)],
        [((side, side), bf16)] * 2,
        [pltpu.VMEM((width // 2, 128), f32)],
        flops=6 * quarter * 2 * count * 2 * count * side,
    )

    packed, after = {}, []
    for part in (blocks[:1], blocks[1:]):
        partners = sum(size for _, size in part)
        bring = len(part) > 1
        made = call(
            functools.partial(adjoint_kernel, part, int(bring)),
            "adjoint",
            [(far, hold(x)) for x in (ranks, u_data, by_cols, by_rows)] + after,
            [packed_kind] * partners + ([(by_rows.shape, bf16)] if bring else []),
            [
                ranks_here,
                pltpu.VMEM((freqs, row_count, width), bf16),
                pltpu.VMEM((freqs, rows, partners, cols, 2, slots, tile), bf16),
                pltpu.VMEM((freqs, row_count, width), bf16),
                stage(partners),
                one((3 + freqs * rows * len(part),)),
            ],
            **share(partners),
        )
        for block in part:
            packed[block], made = made[: block[1]], made[block[1] :]
        after = [(anywhere, packed[blocks[0]][0])]
    [near] = made
    images = []
    for n, block in enumerate(blocks):
        first, last = n == 0, n == len(blocks) - 1
        images = call(
            functools.partial(image_kernel, block, owners, first, last),
            "image",
            [(whole, ranks), (whole, near)]
            + spread(packed[block], "tile", block[0])
            + [(whole, x) for x in images]
            + ([(anywhere, window[0])] if first else []),
            per_owner if last else [((freqs, width, cols * tile), f32)],
            [
                ranks_here,
                stage(block[1]),
                pltpu.VMEM((cols, 2, block[1] * rows * slots, width), bf16),
                pltpu.VMEM((freqs, width, cols * tile), f32),
                one,
            ],
            **share(block[1]),
        )
    mixed = call(
        functools.partial(mix_kernel, owners),
        "mix",
        [(whole, x) for x in window] + spread(images, "freq"),
        per_owner,
        [pltpu.VMEM((side, cols * tile), bf16), pltpu.VMEM((side, cols * tile), f32)],
        flops=4 * side * side * cols * tile,
    )
    *made, w = call(
        functools.partial(forward_kernel, blocks[:1], owners),
        "forward",
        [(whole, ranks), (whole, near)] + spread(mixed, "freq"),
        [packed_kind] * blocks[0][1] + [((freqs, cols, width, 2 * tile), bf16)],
        [ranks_here, stage(blocks[0][1]), one],
        **share(blocks[0][1]),
    )
    partners = devices - blocks[0][1]
    made += call(
        functools.partial(forward_kernel, blocks[1:], 0),
        "forward",
        [(whole, ranks), (whole, near), (whole, w)],
        [packed_kind] * partners,
        [ranks_here, stage(partners), one],
        **share(partners),
    )
    out = []
    for n, block in enumerate(blocks):
        first, last = n == 0, n == len(blocks) - 1
        packed, made = made[: block[1]], made[block[1] :]
        out = call(
            functools.partial(result_kernel, block, first, last),
            "result",
            [(whole, ranks), (whole, by_cols)]
            + spread(packed, "tile", block[0])
            + [(whole, x) for x in out],
            [((freqs, row_count, width), bf16) if last else ((freqs, rows, width, tile), f32)],
            [
                ranks_here,
                stage(block[1]),
                pltpu.VMEM((rows, 2, block[1] * cols * slots, width), bf16),
                one,
            ],
            **share(block[1]),
        )
    return out[0]


def solution(mesh):
    placed = (
        P("freq", "tile", None),
        P("freq", "tile", None, None, None, None),
        P("freq", None, "tile", None, None, None),
        P("freq", None, None),
        P(),
    )
    return jax.shard_map(
        local, mesh=mesh, in_specs=placed, out_specs=P("freq", "tile", None), check_vma=False
    )
```

time: 54.2 us -> 55.8 us (1.030)
  Pallas kernels: 11 us -> 17.6 us
  waiting for transfers between devices: 16.6 us -> 12.1 us
    pallas_call x6 -> x12, Pallas kernels: 11 us -> 17.6 us  [call(): pl.pallas_call(kernel, in_specs=specs, out_specs=[whole] * len(outs), out...]
    ppermute x20, waiting for transfers between devices: 16.6 us -> 12.1 us  [send(): lax.ppermute(value, axis, [(d, d ^ s) for d in range(lax.axis_size(axis))])]
  transfers between devices with their start and end apart: 20 -> 20, of which waited for: 12 -> 8; matrix products, arithmetic and copies ran while one was open for 0% -> 0% of each run, Pallas kernels for 1% -> 20%
where the time goes in v2:
time: 55.8 us; the launch traced here: 55.7 us
  starting transfers between devices  25.7 us (46%)
  Pallas kernels  17.6 us (32%)
  waiting for transfers between devices  12.1 us (22%)
    ppermute x20, starting transfers between devices, send(): lax.ppermute(value, axis, [(d, d ^ s) for d in range(lax.axis_size(axis))])  25.7 us
    pallas_call x12, Pallas kernels, call(): pl.pallas_call(kernel, in_specs=specs, out_specs=[whole] * len(outs), out...  17.6 us
    ppermute x20, waiting for transfers between devices, send(): lax.ppermute(value, axis, [(d, d ^ s) for d in range(lax.axis_size(axis))])  12.1 us
  transfers between devices with their start and end apart: 20, of which 8 were waited for; matrix products, arithmetic and copies ran while one was open for 0% of the time, Pallas kernels for 20%

profile of v2, /device:TPU:0, one launch (start us, length us, event | category | flops | bytes accessed | tf_op | source)
XLA Modules:
  0.0 55.7 jit_solution(17814982825713668086)
XLA Ops:
  0.0 2.0 %adjoint.2 = (bf16[1,224,128]{2,1,0:T(8,128)(2,1)S(1)}, bf16[1,224,128]{2,1,0:T(8,128)(2,1)S(1)}) custom-call(s32[2,16,16]{2,1,0:T(8,128)} %ranks_near.15, bf16[2,512,128]{2,1,0:T(8,128)(2,1)} %u_far.3, bf16[2,2,8,2,2,48,256]{6,5,4,3,2,1,0:T(8,128)(2,1)} %bitcast.2, bf16[2,8,2,2,2,48,256]{6,5,4,3,2,1,0:T(8,128)(2,1)} %bitcast.7), custom_call_target="tpu_custom_call" | custom-call | flops 201326592 | bytes 786432 | tf_op jit(solution)/shard_map/adjoint/pallas_call | solution.py:29
  2.0 4.6 %collective-permute-start.5 = (bf16[1,224,128]{2,1,0:T(8,128)(2,1)S(1)}, bf16[1,224,128]{2,1,0:T(8,128)(2,1)S(1)}, u32[]{:S(2)}, u32[]{:S(2)}) collective-permute-start(bf16[1,224,128]{2,1,0:T(8,128)(2,1)S(1)} %get-tuple-element.43), channel_id=1, source_target_pairs={{0,7},{1,6},{2,5},{3,4},{4,3},{5,2},{6,1},{7,0},{8,15},{9,14},{10,... | collective-permute-start | bytes 172040 | tf_op jit(solution)/shard_map/ppermute | solution.py:347
  6.5 0.7 %collective-permute-start.6 = (bf16[1,224,128]{2,1,0:T(8,128)(2,1)S(1)}, bf16[1,224,128]{2,1,0:T(8,128)(2,1)S(1)}, u32[]{:S(2)}, u32[]{:S(2)}) collective-permute-start(bf16[1,224,128]{2,1,0:T(8,128)(2,1)S(1)} %get-tuple-element.33.rest_0_), channel_id=1, source_target_pairs={{0,6},{1,7},{2,4},{3,5},{4,2},{5,3},{6,0},{7,1},{8,14},{9,15},{10,... | collective-permute-start | bytes 172040 | tf_op jit(solution)/shard_map/ppermute | solution.py:347
  7.2 3.4 %adjoint.3 = (bf16[1,224,128]{2,1,0:T(8,128)(2,1)S(1)}, bf16[1,224,128]{2,1,0:T(8,128)(2,1)S(1)}, bf16[1,224,128]{2,1,0:T(8,128)(2,1)S(1)}, bf16[1,224,128]{2,1,...) custom-call(s32[2,16,16]{2,1,0:T(8,128)} %ranks_near.15, ...), custom_call_target="tpu_custom_call" | custom-call | flops 603979776 | bytes 2359296 | tf_op jit(solution)/shard_map/adjoint/pallas_call | solution.py:29
  10.7 1.8 %collective-permute-start.3 = (bf16[1,224,128]{2,1,0:T(8,128)(2,1)S(1)}, bf16[1,224,128]{2,1,0:T(8,128)(2,1)S(1)}, u32[]{:S(2)}, u32[]{:S(2)}) collective-permute-start(bf16[1,224,128]{2,1,0:T(8,128)(2,1)S(1)} %get-tuple-element.40), channel_id=1, source_target_pairs={{0,2},{1,3},{2,0},{3,1},{4,6},{5,7},{6,4},{7,5},{8,10},{9,11},{10,... | collective-permute-start | bytes 172040 | tf_op jit(solution)/shard_map/ppermute | solution.py:347
  12.6 2.1 %collective-permute-start = (bf16[1,224,128]{2,1,0:T(8,128)(2,1)S(1)}, bf16[1,224,128]{2,1,0:T(8,128)(2,1)S(1)}, u32[]{:S(2)}, u32[]{:S(2)}) collective-permute-start(bf16[1,224,128]{2,1,0:T(8,128)(2,1)S(1)} %get-tuple-element.37), channel_id=1, source_target_pairs={{0,5},{1,4},{2,7},{3,6},{4,1},{5,0},{6,3},{7,2},{8,13},{9,12},{10,... | collective-permute-start | bytes 172040 | tf_op jit(solution)/shard_map/ppermute | solution.py:347
  14.7 0.9 %collective-permute-start.1 = (bf16[1,224,128]{2,1,0:T(8,128)(2,1)S(1)}, bf16[1,224,128]{2,1,0:T(8,128)(2,1)S(1)}, u32[]{:S(2)}, u32[]{:S(2)}) collective-permute-start(bf16[1,224,128]{2,1,0:T(8,128)(2,1)S(1)} %get-tuple-element.38), channel_id=1, source_target_pairs={{0,4},{1,5},{2,6},{3,7},{4,0},{5,1},{6,2},{7,3},{8,12},{9,13},{10,... | collective-permute-start | bytes 172040 | tf_op jit(solution)/shard_map/ppermute | solution.py:347
  15.6 0.7 %window.1 = (bf16[256,256]{1,0:T(8,128)(2,1)S(1)}, bf16[256,256]{1,0:T(8,128)(2,1)S(1)}) custom-call(s32[64,64]{1,0:T(8,128)S(1)} %copy-done.3, f32[64,128]{1,0:T(8,128)S(1)} %copy-done.4, f32[16,4096]{1,0:T(8,128)S(1)} %copy-done.2, f32[16,256]{1,0:T(8,128)S(1)} %copy-done.5), custom_call_target="tpu_custom_call" | custom-call | flops 6291456 | tf_op jit(solution)/shard_map/window/pallas_call | solution.py:29
  16.3 1.2 %image.3.rest_4_ = f32[2,128,512]{2,1,0:T(8,128)S(1)} custom-call(s32[2,16,16]{2,1,0:T(8,128)S(1)} %copy-done.1, bf16[2,8,2,2,2,48,256]{6,5,4,3,2,1,0:T(8,128)(2,1)S(1)} %get-tuple-element.34.basis, bf16[1,224,128]{2,1,0:T(8,128)(2,1)S(1)} %collective-permute-done.5.rest_0_, bf16[1,224,128]{2,1,0:T(8,128)(2,1)S(1)} %collective-permute-done.6.rest_1_, ...), custom_call_target="tpu_custom_call" | custom-call | flops 201326592 | bytes 786432 | tf_op jit(solution)/shard_map/image/pallas_call | solution.py:29
  17.6 1.4 %image.4.rest_2_ = f32[2,128,512]{2,1,0:T(8,128)S(1)} custom-call(s32[2,16,16]{2,1,0:T(8,128)S(1)} %copy-done.1, bf16[2,8,2,2,2,48,256]{6,5,4,3,2,1,0:T(8,128)(2,1)S(1)} %get-tuple-element.34.basis, bf16[1,224,128]{2,1,0:T(8,128)(2,1)S(1)} %collective-permute-done.2.rest_0_, bf16[1,224,128]{2,1,0:T(8,128)(2,1)S(1)} %collective-permute-done.3.rest_1_, ...), custom_call_target="tpu_custom_call" | custom-call | flops 402653184 | bytes 1572864 | tf_op jit(solution)/shard_map/image/pallas_call | solution.py:29
  19.0 2.5 %collective-permute-done.1.rest_1_ = bf16[1,224,128]{2,1,0:T(8,128)(2,1)S(1)} collective-permute-done((bf16[1,224,128]{2,1,0:T(8,128)(2,1)S(1)}, bf16[1,224,128]{2,1,0:T(8,128)(2,1)S(1)}, u32[]{:S(2)}, u32[]{:S(2)}) %collective-permute-start.1) | collective-permute-done | bytes 57376 | tf_op jit(solution)/shard_map/ppermute | solution.py:347
  21.5 1.2 %image.5 = (bf16[2,32,512]{2,1,0:T(8,128)(2,1)S(1)}, bf16[2,32,512]{2,1,0:T(8,128)(2,1)S(1)}, bf16[2,32,512]{2,1,0:T(8,128)(2,1)S(1)}, bf16[2,32,512]{2,1,0:T(8,128)(2,1)S(1)}) custom-call(s32[2,16,16]{2,1,0:T(8,128)S(1)} %copy-done.1, bf16[2,8,2,2,2,48,256]{6,5,4,3,2,1,0:T(8,128)(2,1)S(1)} %get-tuple-element.34.basis, ...), custom_call_target="tpu_custom_call" | custom-call | flops 201326592 | bytes 786432 | tf_op jit(solution)/shard_map/image/pallas_call | solution.py:29
  22.7 2.4 %collective-permute-start.7 = (bf16[2,32,512]{2,1,0:T(8,128)(2,1)S(1)}, bf16[2,32,512]{2,1,0:T(8,128)(2,1)S(1)}, u32[]{:S(2)}, u32[]{:S(2)}) collective-permute-start(bf16[2,32,512]{2,1,0:T(8,128)(2,1)S(1)} %get-tuple-element.44), channel_id=1, source_target_pairs={{0,24},{8,16},{16,8},{24,0},{1,25},{9,17},{17,9},{25,1},{2,26},{10... | collective-permute-start | bytes 196616 | tf_op jit(solution)/shard_map/ppermute | solution.py:347
  25.1 0.5 collective-permute-start.8
  25.7 0.6 %collective-permute-start.9 = (bf16[2,32,512]{2,1,0:T(8,128)(2,1)S(1)}, bf16[2,32,512]{2,1,0:T(8,128)(2,1)S(1)}, u32[]{:S(2)}, u32[]{:S(2)}) collective-permute-start(bf16[2,32,512]{2,1,0:T(8,128)(2,1)S(1)} %get-tuple-element.46), channel_id=1, source_target_pairs={{0,8},{8,0},{16,24},{24,16},{1,9},{9,1},{17,25},{25,17},{2,10},{10... | collective-permute-start | bytes 196616 | tf_op jit(solution)/shard_map/ppermute | solution.py:347
  26.3 1.8 %collective-permute-done.7.rest_0_ = bf16[2,32,512]{2,1,0:T(8,128)(2,1)S(1)} collective-permute-done((bf16[2,32,512]{2,1,0:T(8,128)(2,1)S(1)}, bf16[2,32,512]{2,1,0:T(8,128)(2,1)S(1)}, u32[]{:S(2)}, u32[]{:S(2)}) %collective-permute-start.7) | collective-permute-done | bytes 65568 | tf_op jit(solution)/shard_map/ppermute | solution.py:347
  28.0 1.4 %collective-permute-done.8.rest_1_ = bf16[2,32,512]{2,1,0:T(8,128)(2,1)S(1)} collective-permute-done((bf16[2,32,512]{2,1,0:T(8,128)(2,1)S(1)}, bf16[2,32,512]{2,1,0:T(8,128)(2,1)S(1)}, u32[]{:S(2)}, u32[]{:S(2)}) %collective-permute-start.8) | collective-permute-done | bytes 65568 | tf_op jit(solution)/shard_map/ppermute | solution.py:347
  30.3 1.6 %collective-permute-start.10 = (bf16[2,32,512]{2,1,0:T(8,128)(2,1)S(1)}, bf16[2,32,512]{2,1,0:T(8,128)(2,1)S(1)}, u32[]{:S(2)}, u32[]{:S(2)}) collective-permute-start(bf16[2,32,512]{2,1,0:T(8,128)(2,1)S(1)} %get-tuple-element.48), channel_id=1, source_target_pairs={{0,24},{8,16},{16,8},{24,0},{1,25},{9,17},{17,9},{25,1},{2,26},{10... | collective-permute-start | bytes 196616 | tf_op jit(solution)/shard_map/ppermute | solution.py:347
  32.4 1.5 %collective-permute-start.12 = (bf16[2,32,512]{2,1,0:T(8,128)(2,1)S(1)}, bf16[2,32,512]{2,1,0:T(8,128)(2,1)S(1)}, u32[]{:S(2)}, u32[]{:S(2)}) collective-permute-start(bf16[2,32,512]{2,1,0:T(8,128)(2,1)S(1)} %get-tuple-element.50), channel_id=1, source_target_pairs={{0,8},{8,0},{16,24},{24,16},{1,9},{9,1},{17,25},{25,17},{2,10},{10... | collective-permute-start | bytes 196616 | tf_op jit(solution)/shard_map/ppermute | solution.py:347
  33.9 1.7 %collective-permute-done.10.rest_0_ = bf16[2,32,512]{2,1,0:T(8,128)(2,1)S(1)} collective-permute-done((bf16[2,32,512]{2,1,0:T(8,128)(2,1)S(1)}, bf16[2,32,512]{2,1,0:T(8,128)(2,1)S(1)}, u32[]{:S(2)}, u32[]{:S(2)}) %collective-permute-start.10) | collective-permute-done | bytes 65568 | tf_op jit(solution)/shard_map/ppermute | solution.py:347
  35.6 0.7 %collective-permute-done.11.rest_1_ = bf16[2,32,512]{2,1,0:T(8,128)(2,1)S(1)} collective-permute-done((bf16[2,32,512]{2,1,0:T(8,128)(2,1)S(1)}, bf16[2,32,512]{2,1,0:T(8,128)(2,1)S(1)}, u32[]{:S(2)}, u32[]{:S(2)}) %collective-permute-start.11) | collective-permute-done | bytes 65568 | tf_op jit(solution)/shard_map/ppermute | solution.py:347
  36.7 1.2 %forward.2 = (bf16[1,224,128]{2,1,0:T(8,128)(2,1)S(1)}, bf16[1,224,128]{2,1,0:T(8,128)(2,1)S(1)}, bf16[2,2,128,512]{3,2,1,0:T(8,128)(2,1)S(1)}) custom-call(s32[2,16,16]{2,1,0:T(8,128)S(1)} %copy-done.1, bf16[2,8,2,2,2,48,256]{6,5,4,3,2,1,0:T(8,128)(2,1)S(1)} %get-tuple-element.34.basis, bf16[2,32,512]{2,1,0:T(8,128)(2,1)S(1)} %collective-permute-done.10.rest_0_, ...), custom_call_target="tpu_custom_call" | custom-call | flops 201326592 | bytes 786432 | tf_op jit(solution)/shard_map/forward/pallas_call | solution.py:29
  37.9 1.4 %collective-permute-start.18 = (bf16[1,224,128]{2,1,0:T(8,128)(2,1)S(1)}, bf16[1,224,128]{2,1,0:T(8,128)(2,1)S(1)}, u32[]{:S(2)}, u32[]{:S(2)}) collective-permute-start(bf16[1,224,128]{2,1,0:T(8,128)(2,1)S(1)} %get-tuple-element.59), channel_id=1, source_target_pairs={{0,7},{1,6},{2,5},{3,4},{4,3},{5,2},{6,1},{7,0},{8,15},{9,14},{10,... | collective-permute-start | bytes 172040 | tf_op jit(solution)/shard_map/ppermute | solution.py:347
  39.2 1.8 %collective-permute-start.19 = (bf16[1,224,128]{2,1,0:T(8,128)(2,1)S(1)}, bf16[1,224,128]{2,1,0:T(8,128)(2,1)S(1)}, u32[]{:S(2)}, u32[]{:S(2)}) collective-permute-start(bf16[1,224,128]{2,1,0:T(8,128)(2,1)S(1)} %get-tuple-element.60), channel_id=1, source_target_pairs={{0,6},{1,7},{2,4},{3,5},{4,2},{5,3},{6,0},{7,1},{8,14},{9,15},{10,... | collective-permute-start | bytes 172040 | tf_op jit(solution)/shard_map/ppermute | solution.py:347
  41.1 1.6 %forward.3 = (bf16[1,224,128]{2,1,0:T(8,128)(2,1)S(1)}, bf16[1,224,128]{2,1,0:T(8,128)(2,1)S(1)}, bf16[1,224,128]{2,1,0:T(8,128)(2,1)S(1)}, bf16[1,224,128]{2,1,...) custom-call(s32[2,16,16]{2,1,0:T(8,128)S(1)} %copy-done.1, ...), custom_call_target="tpu_custom_call" | custom-call | flops 603979776 | bytes 2359296 | tf_op jit(solution)/shard_map/forward/pallas_call | solution.py:29
  42.8 2.1 %collective-permute-start.16 = (bf16[1,224,128]{2,1,0:T(8,128)(2,1)S(1)}, bf16[1,224,128]{2,1,0:T(8,128)(2,1)S(1)}, u32[]{:S(2)}, u32[]{:S(2)}) collective-permute-start(bf16[1,224,128]{2,1,0:T(8,128)(2,1)S(1)} %get-tuple-element.56), channel_id=1, source_target_pairs={{0,2},{1,3},{2,0},{3,1},{4,6},{5,7},{6,4},{7,5},{8,10},{9,11},{10,... | collective-permute-start | bytes 172040 | tf_op jit(solution)/shard_map/ppermute | solution.py:347
  44.9 1.7 %collective-permute-start.13 = (bf16[1,224,128]{2,1,0:T(8,128)(2,1)S(1)}, bf16[1,224,128]{2,1,0:T(8,128)(2,1)S(1)}, u32[]{:S(2)}, u32[]{:S(2)}) collective-permute-start(bf16[1,224,128]{2,1,0:T(8,128)(2,1)S(1)} %get-tuple-element.53), channel_id=1, source_target_pairs={{0,5},{1,4},{2,7},{3,6},{4,1},{5,0},{6,3},{7,2},{8,13},{9,12},{10,... | collective-permute-start | bytes 172040 | tf_op jit(solution)/shard_map/ppermute | solution.py:347
  46.6 1.3 %collective-permute-start.14 = (bf16[1,224,128]{2,1,0:T(8,128)(2,1)S(1)}, bf16[1,224,128]{2,1,0:T(8,128)(2,1)S(1)}, u32[]{:S(2)}, u32[]{:S(2)}) collective-permute-start(bf16[1,224,128]{2,1,0:T(8,128)(2,1)S(1)} %get-tuple-element.54), channel_id=1, source_target_pairs={{0,4},{1,5},{2,6},{3,7},{4,0},{5,1},{6,2},{7,3},{8,12},{9,13},{10,... | collective-permute-start | bytes 172040 | tf_op jit(solution)/shard_map/ppermute | solution.py:347
  48.0 1.2 %result.3.rest_4_ = f32[2,2,128,256]{3,2,1,0:T(8,128)S(1)} custom-call(s32[2,16,16]{2,1,0:T(8,128)S(1)} %copy-done.1, bf16[2,2,8,2,2,48,256]{6,5,4,3,2,1,0:T(8,128)(2,1)S(1)} %bitcast.4, bf16[1,224,128]{2,1,0:T(8,128)(2,1)S(1)} %collective-permute-done.18.rest_0_, bf16[1,224,128]{2,1,0:T(8,128)(2,1)S(1)} %collective-permute-done.19.rest_1_), custom_call_target="tpu_custom_call" | custom-call | flops 201326592 | bytes 786432 | tf_op jit(solution)/shard_map/result/pallas_call | solution.py:29
  49.2 1.4 %result.4.rest_2_ = f32[2,2,128,256]{3,2,1,0:T(8,128)S(1)} custom-call(s32[2,16,16]{2,1,0:T(8,128)S(1)} %copy-done.1, bf16[2,2,8,2,2,48,256]{6,5,4,3,2,1,0:T(8,128)(2,1)S(1)} %bitcast.5, bf16[1,224,128]{2,1,0:T(8,128)(2,1)S(1)} %collective-permute-done.15.rest_0_, bf16[1,224,128]{2,1,0:T(8,128)(2,1)S(1)} %collective-permute-done.16.rest_1_, ...), custom_call_target="tpu_custom_call" | custom-call | flops 402653184 | bytes 1572864 | tf_op jit(solution)/shard_map/result/pallas_call | solution.py:29
  50.6 3.1 %collective-permute-done.14.rest_1_ = bf16[1,224,128]{2,1,0:T(8,128)(2,1)S(1)} collective-permute-done((bf16[1,224,128]{2,1,0:T(8,128)(2,1)S(1)}, bf16[1,224,128]{2,1,0:T(8,128)(2,1)S(1)}, u32[]{:S(2)}, u32[]{:S(2)}) %collective-permute-start.14) | collective-permute-done | bytes 57376 | tf_op jit(solution)/shard_map/ppermute | solution.py:347
  53.7 2.0 %result.5 = bf16[2,512,128]{2,1,0:T(8,128)(2,1)} custom-call(s32[2,16,16]{2,1,0:T(8,128)S(1)} %copy-done.1, bf16[2,2,8,2,2,48,256]{6,5,4,3,2,1,0:T(8,128)(2,1)S(1)} %bitcast.6, bf16[1,224,128]{2,1,0:T(8,128)(2,1)S(1)} %collective-permute-done.13.rest_0_, bf16[1,224,128]{2,1,0:T(8,128)(2,1)S(1)} %collective-permute-done.14.rest_1_, ...), custom_call_target="tpu_custom_call" | custom-call | flops 201326592 | bytes 786432 | tf_op jit(solution)/shard_map/result/pallas_call | solution.py:29
  (32 shorter events, 2.1 us)
Async XLA Ops:
  2.0 10.6 %collective-permute-start.5 = (bf16[1,224,128]{2,1,0:T(8,128)(2,1)S(1)}, bf16[1,224,128]{2,1,0:T(8,128)(2,1)S(1)}, u32[]{:S(2)}, u32[]{:S(2)}) collective-permute-start(bf16[1,224,128]{2,1,0:T(8,128)(2,1)S(1)} %get-tuple-element.43), channel_id=1, source_target_pairs={{0,7},{1,6},{2,5},{3,4},{4,3},{5,2},{6,1},{7,0},{8,15},{9,14},{10,... | collective-permute-start | bytes 172040 | tf_op jit(solution)/shard_map/ppermute | solution.py:347
  6.5 9.0 %copy-start.2 = (f32[16,4096]{1,0:T(8,128)S(1)}, f32[16,4096]{1,0:T(8,128)}, u32[]{:S(2)}) copy-start(f32[16,4096]{1,0:T(8,128)} %constant.7.clone.choice) | copy-start | bytes 786436
  6.5 9.0 %copy-start.3 = (s32[64,64]{1,0:T(8,128)S(1)}, s32[64,64]{1,0:T(8,128)}, u32[]{:S(2)}) copy-start(s32[64,64]{1,0:T(8,128)} %mask.1) | copy-start | bytes 49156
  6.5 9.0 %copy-start.4 = (f32[64,128]{1,0:T(8,128)S(1)}, f32[64,128]{1,0:T(8,128)}, u32[]{:S(2)}) copy-start(f32[64,128]{1,0:T(8,128)} %constant.6.clone.table) | copy-start | bytes 98308
  6.5 9.0 %copy-start.5 = (f32[16,256]{1,0:T(8,128)S(1)}, f32[16,256]{1,0:T(8,128)}, u32[]{:S(2)}) copy-start(f32[16,256]{1,0:T(8,128)} %constant.8.clone.same) | copy-start | bytes 49156
  6.5 9.8 %copy-start.1 = (s32[2,16,16]{2,1,0:T(8,128)S(1)}, s32[2,16,16]{2,1,0:T(8,128)}, u32[]{:S(2)}) copy-start(s32[2,16,16]{2,1,0:T(8,128)} %ranks_near.15) | copy-start | bytes 6148
  6.5 8.2 %collective-permute-start.6 = (bf16[1,224,128]{2,1,0:T(8,128)(2,1)S(1)}, bf16[1,224,128]{2,1,0:T(8,128)(2,1)S(1)}, u32[]{:S(2)}, u32[]{:S(2)}) collective-permute-start(bf16[1,224,128]{2,1,0:T(8,128)(2,1)S(1)} %get-tuple-element.33.rest_0_), channel_id=1, source_target_pairs={{0,6},{1,7},{2,4},{3,5},{4,2},{5,3},{6,0},{7,1},{8,14},{9,15},{10,... | collective-permute-start | bytes 172040 | tf_op jit(solution)/shard_map/ppermute | solution.py:347
  10.7 6.9 %collective-permute-start.2 = (bf16[1,224,128]{2,1,0:T(8,128)(2,1)S(1)}, bf16[1,224,128]{2,1,0:T(8,128)(2,1)S(1)}, u32[]{:S(2)}, u32[]{:S(2)}) collective-permute-start(bf16[1,224,128]{2,1,0:T(8,128)(2,1)S(1)} %get-tuple-element.39), channel_id=1, source_target_pairs={{0,3},{1,2},{2,1},{3,0},{4,7},{5,6},{6,5},{7,4},{8,11},{9,10},{10,... | collective-permute-start | bytes 172040 | tf_op jit(solution)/shard_map/ppermute | solution.py:347
  10.7 6.8 %collective-permute-start.3 = (bf16[1,224,128]{2,1,0:T(8,128)(2,1)S(1)}, bf16[1,224,128]{2,1,0:T(8,128)(2,1)S(1)}, u32[]{:S(2)}, u32[]{:S(2)}) collective-permute-start(bf16[1,224,128]{2,1,0:T(8,128)(2,1)S(1)} %get-tuple-element.40), channel_id=1, source_target_pairs={{0,2},{1,3},{2,0},{3,1},{4,6},{5,7},{6,4},{7,5},{8,10},{9,11},{10,... | collective-permute-start | bytes 172040 | tf_op jit(solution)/shard_map/ppermute | solution.py:347
  12.5 5.1 %collective-permute-start.4 = (bf16[1,224,128]{2,1,0:T(8,128)(2,1)S(1)}, bf16[1,224,128]{2,1,0:T(8,128)(2,1)S(1)}, u32[]{:S(2)}, u32[]{:S(2)}) collective-permute-start(bf16[1,224,128]{2,1,0:T(8,128)(2,1)S(1)} %get-tuple-element.41), channel_id=1, source_target_pairs={{0,1},{1,0},{2,3},{3,2},{4,5},{5,4},{6,7},{7,6},{8,9},{9,8},{10,11... | collective-permute-start | bytes 172040 | tf_op jit(solution)/shard_map/ppermute | solution.py:347
  12.6 6.4 %collective-permute-start = (bf16[1,224,128]{2,1,0:T(8,128)(2,1)S(1)}, bf16[1,224,128]{2,1,0:T(8,128)(2,1)S(1)}, u32[]{:S(2)}, u32[]{:S(2)}) collective-permute-start(bf16[1,224,128]{2,1,0:T(8,128)(2,1)S(1)} %get-tuple-element.37), channel_id=1, source_target_pairs={{0,5},{1,4},{2,7},{3,6},{4,1},{5,0},{6,3},{7,2},{8,13},{9,12},{10,... | collective-permute-start | bytes 172040 | tf_op jit(solution)/shard_map/ppermute | solution.py:347
  14.7 6.8 %collective-permute-start.1 = (bf16[1,224,128]{2,1,0:T(8,128)(2,1)S(1)}, bf16[1,224,128]{2,1,0:T(8,128)(2,1)S(1)}, u32[]{:S(2)}, u32[]{:S(2)}) collective-permute-start(bf16[1,224,128]{2,1,0:T(8,128)(2,1)S(1)} %get-tuple-element.38), channel_id=1, source_target_pairs={{0,4},{1,5},{2,6},{3,7},{4,0},{5,1},{6,2},{7,3},{8,12},{9,13},{10,... | collective-permute-start | bytes 172040 | tf_op jit(solution)/shard_map/ppermute | solution.py:347
  22.7 5.3 %collective-permute-start.7 = (bf16[2,32,512]{2,1,0:T(8,128)(2,1)S(1)}, bf16[2,32,512]{2,1,0:T(8,128)(2,1)S(1)}, u32[]{:S(2)}, u32[]{:S(2)}) collective-permute-start(bf16[2,32,512]{2,1,0:T(8,128)(2,1)S(1)} %get-tuple-element.44), channel_id=1, source_target_pairs={{0,24},{8,16},{16,8},{24,0},{1,25},{9,17},{17,9},{25,1},{2,26},{10... | collective-permute-start | bytes 196616 | tf_op jit(solution)/shard_map/ppermute | solution.py:347
  25.1 4.3 %collective-permute-start.8 = (bf16[2,32,512]{2,1,0:T(8,128)(2,1)S(1)}, bf16[2,32,512]{2,1,0:T(8,128)(2,1)S(1)}, u32[]{:S(2)}, u32[]{:S(2)}) collective-permute-start(bf16[2,32,512]{2,1,0:T(8,128)(2,1)S(1)} %get-tuple-element.45), channel_id=1, source_target_pairs={{0,16},{8,24},{16,0},{24,8},{1,17},{9,25},{17,1},{25,9},{2,18},{10... | collective-permute-start | bytes 196616 | tf_op jit(solution)/shard_map/ppermute | solution.py:347
  25.7 4.3 %collective-permute-start.9 = (bf16[2,32,512]{2,1,0:T(8,128)(2,1)S(1)}, bf16[2,32,512]{2,1,0:T(8,128)(2,1)S(1)}, u32[]{:S(2)}, u32[]{:S(2)}) collective-permute-start(bf16[2,32,512]{2,1,0:T(8,128)(2,1)S(1)} %get-tuple-element.46), channel_id=1, source_target_pairs={{0,8},{8,0},{16,24},{24,16},{1,9},{9,1},{17,25},{25,17},{2,10},{10... | collective-permute-start | bytes 196616 | tf_op jit(solution)/shard_map/ppermute | solution.py:347
  30.3 5.2 %collective-permute-start.10 = (bf16[2,32,512]{2,1,0:T(8,128)(2,1)S(1)}, bf16[2,32,512]{2,1,0:T(8,128)(2,1)S(1)}, u32[]{:S(2)}, u32[]{:S(2)}) collective-permute-start(bf16[2,32,512]{2,1,0:T(8,128)(2,1)S(1)} %get-tuple-element.48), channel_id=1, source_target_pairs={{0,24},{8,16},{16,8},{24,0},{1,25},{9,17},{17,9},{25,1},{2,26},{10... | collective-permute-start | bytes 196616 | tf_op jit(solution)/shard_map/ppermute | solution.py:347
  31.9 4.3 %collective-permute-start.11 = (bf16[2,32,512]{2,1,0:T(8,128)(2,1)S(1)}, bf16[2,32,512]{2,1,0:T(8,128)(2,1)S(1)}, u32[]{:S(2)}, u32[]{:S(2)}) collective-permute-start(bf16[2,32,512]{2,1,0:T(8,128)(2,1)S(1)} %get-tuple-element.49), channel_id=1, source_target_pairs={{0,16},{8,24},{16,0},{24,8},{1,17},{9,25},{17,1},{25,9},{2,18},{10... | collective-permute-start | bytes 196616 | tf_op jit(solution)/shard_map/ppermute | solution.py:347
  32.4 4.3 %collective-permute-start.12 = (bf16[2,32,512]{2,1,0:T(8,128)(2,1)S(1)}, bf16[2,32,512]{2,1,0:T(8,128)(2,1)S(1)}, u32[]{:S(2)}, u32[]{:S(2)}) collective-permute-start(bf16[2,32,512]{2,1,0:T(8,128)(2,1)S(1)} %get-tuple-element.50), channel_id=1, source_target_pairs={{0,8},{8,0},{16,24},{24,16},{1,9},{9,1},{17,25},{25,17},{2,10},{10... | collective-permute-start | bytes 196616 | tf_op jit(solution)/shard_map/ppermute | solution.py:347
  36.7 11.3 %copy-start = (bf16[2,2,16,2,48,256]{5,4,3,2,1,0:T(8,128)(2,1)S(1)}, bf16[2,2,16,2,48,256]{5,4,3,2,1,0:T(8,128)(2,1)}, u32[]{:S(2)}) copy-start(bf16[2,2,16,2,48,256]{5,4,3,2,1,0:T(8,128)(2,1)} %param.9) | copy-start | bytes 9437188
  37.9 7.0 %collective-permute-start.18 = (bf16[1,224,128]{2,1,0:T(8,128)(2,1)S(1)}, bf16[1,224,128]{2,1,0:T(8,128)(2,1)S(1)}, u32[]{:S(2)}, u32[]{:S(2)}) collective-permute-start(bf16[1,224,128]{2,1,0:T(8,128)(2,1)S(1)} %get-tuple-element.59), channel_id=1, source_target_pairs={{0,7},{1,6},{2,5},{3,4},{4,3},{5,2},{6,1},{7,0},{8,15},{9,14},{10,... | collective-permute-start | bytes 172040 | tf_op jit(solution)/shard_map/ppermute | solution.py:347
  39.2 7.4 %collective-permute-start.19 = (bf16[1,224,128]{2,1,0:T(8,128)(2,1)S(1)}, bf16[1,224,128]{2,1,0:T(8,128)(2,1)S(1)}, u32[]{:S(2)}, u32[]{:S(2)}) collective-permute-start(bf16[1,224,128]{2,1,0:T(8,128)(2,1)S(1)} %get-tuple-element.60), channel_id=1, source_target_pairs={{0,6},{1,7},{2,4},{3,5},{4,2},{5,3},{6,0},{7,1},{8,14},{9,15},{10,... | collective-permute-start | bytes 172040 | tf_op jit(solution)/shard_map/ppermute | solution.py:347
  42.7 6.5 %collective-permute-start.15 = (bf16[1,224,128]{2,1,0:T(8,128)(2,1)S(1)}, bf16[1,224,128]{2,1,0:T(8,128)(2,1)S(1)}, u32[]{:S(2)}, u32[]{:S(2)}) collective-permute-start(bf16[1,224,128]{2,1,0:T(8,128)(2,1)S(1)} %get-tuple-element.55), channel_id=1, source_target_pairs={{0,3},{1,2},{2,1},{3,0},{4,7},{5,6},{6,5},{7,4},{8,11},{9,10},{10,... | collective-permute-start | bytes 172040 | tf_op jit(solution)/shard_map/ppermute | solution.py:347
  42.8 6.4 %collective-permute-start.16 = (bf16[1,224,128]{2,1,0:T(8,128)(2,1)S(1)}, bf16[1,224,128]{2,1,0:T(8,128)(2,1)S(1)}, u32[]{:S(2)}, u32[]{:S(2)}) collective-permute-start(bf16[1,224,128]{2,1,0:T(8,128)(2,1)S(1)} %get-tuple-element.56), channel_id=1, source_target_pairs={{0,2},{1,3},{2,0},{3,1},{4,6},{5,7},{6,4},{7,5},{8,10},{9,11},{10,... | collective-permute-start | bytes 172040 | tf_op jit(solution)/shard_map/ppermute | solution.py:347
  44.9 4.3 %collective-permute-start.17 = (bf16[1,224,128]{2,1,0:T(8,128)(2,1)S(1)}, bf16[1,224,128]{2,1,0:T(8,128)(2,1)S(1)}, u32[]{:S(2)}, u32[]{:S(2)}) collective-permute-start(bf16[1,224,128]{2,1,0:T(8,128)(2,1)S(1)} %get-tuple-element.57), channel_id=1, source_target_pairs={{0,1},{1,0},{2,3},{3,2},{4,5},{5,4},{6,7},{7,6},{8,9},{9,8},{10,11... | collective-permute-start | bytes 172040 | tf_op jit(solution)/shard_map/ppermute | solution.py:347
  44.9 5.7 %collective-permute-start.13 = (bf16[1,224,128]{2,1,0:T(8,128)(2,1)S(1)}, bf16[1,224,128]{2,1,0:T(8,128)(2,1)S(1)}, u32[]{:S(2)}, u32[]{:S(2)}) collective-permute-start(bf16[1,224,128]{2,1,0:T(8,128)(2,1)S(1)} %get-tuple-element.53), channel_id=1, source_target_pairs={{0,5},{1,4},{2,7},{3,6},{4,1},{5,0},{6,3},{7,2},{8,13},{9,12},{10,... | collective-permute-start | bytes 172040 | tf_op jit(solution)/shard_map/ppermute | solution.py:347
  46.6 7.1 %collective-permute-start.14 = (bf16[1,224,128]{2,1,0:T(8,128)(2,1)S(1)}, bf16[1,224,128]{2,1,0:T(8,128)(2,1)S(1)}, u32[]{:S(2)}, u32[]{:S(2)}) collective-permute-start(bf16[1,224,128]{2,1,0:T(8,128)(2,1)S(1)} %get-tuple-element.54), channel_id=1, source_target_pairs={{0,4},{1,5},{2,6},{3,7},{4,0},{5,1},{6,2},{7,3},{8,12},{9,13},{10,... | collective-permute-start | bytes 172040 | tf_op jit(solution)/shard_map/ppermute | solution.py:347

commit v3 on v1

--- a/solution.py
+++ b/solution.py
@@ -23,13 +23,12 @@
     return pltpu.with_memory_space_constraint(value, pltpu.HBM)
 
 
-def call(kernel, name, ins, outs, scratch, flops=0, moved=0):
-    specs = [spec for spec, _ in ins]
+def call(kernel, name, ins, outs, scratch, flops=0, moved=0, specs=None):
     shapes = [jax.ShapeDtypeStruct(shape, kind) for shape, kind in outs]
     return pl.pallas_call(
         kernel,
-        in_specs=specs,
-        out_specs=[whole] * len(outs),
+        in_specs=[spec for spec, _ in ins],
+        out_specs=specs or [whole] * len(outs),
         out_shape=shapes,
         scratch_shapes=scratch,
         compiler_params=pltpu.CompilerParams(vmem_limit_bytes=vmem_limit),
@@ -105,9 +104,9 @@
             outs[s][m, pl.ds(c * size, size), :] = block.astype(bf16)
 
 
-def adjoint_kernel(devices, parts, ranks_far, u_far, basis_far, other_far, *rest):
-    outs, other = rest[:devices], rest[devices]
-    ranks, u_ref, basis, turned, stage, sems = rest[devices + 1 :]
+def adjoint_kernel(devices, parts, ranks_far, u_far, basis_far, *rest):
+    outs = rest[:devices]
+    ranks, u_ref, basis, turned, stage, sems = rest[devices:]
     freqs, rows, _, cols, _, slots, tile = basis_far.shape
     total = slots + slots // 6
     half = u_ref.shape[2] // 2
@@ -115,7 +114,6 @@
     me = lax.axis_index("tile")
     rank_copy = pltpu.make_async_copy(ranks_far, ranks, sems.at[0])
     data_copy = pltpu.make_async_copy(u_far, u_ref, sems.at[1])
-    other_copy = pltpu.make_async_copy(other_far, other, sems.at[2])
     data_copy.start()
     rank_copy.start()
     copies = {}
@@ -124,10 +122,9 @@
             for f in range(freqs):
                 at = pl.ds(p * per, per)
                 copies[f, i, p] = pltpu.make_async_copy(
-                    basis_far.at[f, i, at], basis.at[f, i, at], sems.at[3 + (f * rows + i) * parts + p]
+                    basis_far.at[f, i, at], basis.at[f, i, at], sems.at[2 + (f * rows + i) * parts + p]
                 )
                 copies[f, i, p].start()
-    other_copy.start()
     data_copy.wait()
     for f in range(freqs):
         values = u_ref[f].astype(f32)
@@ -155,7 +152,6 @@
                     cut = slice(n * slots, (n + 1) * slots)
                     pack_rows(stage, m * devices * cols + col, i * total, rank, pair[0][cut], pair[1][cut])
         unstage(outs, stage, m, cols, rows * total, me)
-    other_copy.wait()
 
 
 def image_kernel(devices, owners, ranks_near, basis, *rest):
@@ -181,7 +177,7 @@
             for s in range(devices):
                 for i in range(rows):
                     row = (me ^ s) * rows + i
-                    rank = ranks[2 * m, row, me * cols + c]
+                    rank = ranks[0, (m * devices * rows + row) * cols + c]
                     slot = (m * devices + s) * cols + c
                     unpack_rows(stage, slot, i * total, rank, total, coeffs.at[c], row * slots)
             for n in range(2):
@@ -196,7 +192,15 @@
             outs[r][f] = jnp.concatenate([real, imag], axis=0).astype(bf16)
 
 
-def window_kernel(mask, table, choice, same, high, low, full):
+def prepare_kernel(ranks_far, basis_far, mask, table, choice, same, *rest):
+    basis, short, high, low, ranks, full, sems = rest[-7:]
+    freqs, devices, rows, cols = basis_far.shape[:4]
+    row_tiles, col_tiles = ranks.shape[1:]
+    me = lax.axis_index("tile")
+    basis_copy = pltpu.make_async_copy(basis_far, basis, sems.at[0])
+    rank_copy = pltpu.make_async_copy(ranks_far, ranks, sems.at[1])
+    rank_copy.start()
+    basis_copy.start()
     exact = lax.Precision.HIGHEST
     full[...] = dot(mask[...].astype(f32), table[...], 0, 0, exact)
     quarter, side = same.shape
@@ -207,6 +211,19 @@
         upper = block.astype(bf16)
         high[n * quarter : (n + 1) * quarter, :] = upper
         low[n * quarter : (n + 1) * quarter, :] = (block - upper.astype(f32)).astype(bf16)
+    rank_copy.wait()
+    at = 0
+    for m in range(freqs // 2):
+        for row in range(row_tiles):
+            for c in range(cols):
+                short[0, at] = ranks[2 * m, row, me * cols + c]
+                at += 1
+    for m in range(freqs // 2):
+        for i in range(rows):
+            for col in range(col_tiles):
+                short[0, at] = ranks[2 * m, me * rows + i, col]
+                at += 1
+    basis_copy.wait()
 
 
 def mix_kernel(owners, high, low, *rest):
@@ -254,7 +271,7 @@
                 pair.append(dot(both, w[f, c], 1, 1))
             for d in range(devices):
                 for i in range(rows):
-                    rank = ranks[2 * m, d * rows + i, me * cols + c]
+                    rank = ranks[0, (m * devices * rows + d * rows + i) * cols + c]
                     cut = slice((d * rows + i) * slots, (d * rows + i + 1) * slots)
                     slot = (m * devices + d) * cols + c
                     pack_rows(stage, slot, i * total, rank, pair[0][cut], pair[1][cut])
@@ -267,6 +284,7 @@
     freqs, rows, _, cols, _, slots, tile = basis.shape
     total = slots + slots // 6
     size = rows * total
+    before = freqs // 2 * devices * rows * cols
     me = lax.axis_index("tile")
     rank_copy = pltpu.make_async_copy(ranks_near, ranks, sem)
     rank_copy.start()
@@ -281,7 +299,7 @@
             for s in range(devices):
                 for c in range(cols):
                     col = (me ^ s) * cols + c
-                    rank = ranks[2 * m, me * rows + i, col]
+                    rank = ranks[0, before + (m * rows + i) * devices * cols + col]
                     slot = (m * devices + s) * cols + c
                     unpack_rows(stage, slot, i * total, rank, total, coeffs.at[i], col * slots)
             for n in range(2):
@@ -318,41 +336,44 @@
     per_device = [((pairs, cols * rows * total, width), bf16)] * devices
     per_owner = [((freqs, 2 * quarter, cols * tile), bf16)] * owners
     work = {"flops": 4 * row_count * slots * width * col_tiles * freqs * 2, "moved": u_basis.size * 2}
-    ranks_here = pltpu.SMEM(ranks.shape, jnp.int32)
+    count_short = pairs * (row_tiles * cols + rows * col_tiles)
+    ranks_here = pltpu.SMEM((1, count_short), jnp.int32)
     stage = pltpu.VMEM((pairs * devices * cols, stage_rows, width), f32)
     one = pltpu.SemaphoreType.DMA
 
     table = lag_tables(count, time_mask.shape[0], 128)
     choice, same = lag_choice(count, quarter)
-    window = call(
-        window_kernel,
-        "window",
-        [(whole, jnp.asarray(x)) for x in (time_mask, table, choice, same)],
-        [((side, side), bf16)] * 2,
-        [pltpu.VMEM((width // 2, 128), f32)],
-        flops=6 * quarter * 2 * count * 2 * count * side,
-    )
-
     parts = math.gcd(devices, 2)
-    *packed, near = call(
+    packed = call(
         functools.partial(adjoint_kernel, devices, parts),
         "adjoint",
-        [(far, hold(x)) for x in (ranks, u_data, by_cols, by_rows)],
-        per_device + [(by_rows.shape, bf16)],
+        [(far, hold(x)) for x in (ranks, u_data, by_cols)],
+        per_device,
         [
-            ranks_here,
+            pltpu.SMEM(ranks.shape, jnp.int32),
             pltpu.VMEM((freqs, row_count, width), bf16),
             pltpu.VMEM(by_cols.shape, bf16),
             pltpu.VMEM((freqs, row_count, width), bf16),
             stage,
-            one((3 + freqs * rows * parts,)),
+            one((2 + freqs * rows * parts,)),
         ],
         **work,
+    )
+    near, short, *window = call(
+        prepare_kernel,
+        "prepare",
+        [(far, hold(ranks)), (far, hold(by_rows))]
+        + [(whole, jnp.asarray(x)) for x in (time_mask, table, choice, same)]
+        + [(anywhere, packed[0])],
+        [(by_rows.shape, bf16), ((1, count_short), jnp.int32)] + [((side, side), bf16)] * 2,
+        [pltpu.SMEM(ranks.shape, jnp.int32), pltpu.VMEM((width // 2, 128), f32), one((2,))],
+        specs=[whole, scalars, whole, whole],
+        moved=u_basis.size * 2,
     )
     images = call(
         functools.partial(image_kernel, devices, owners),
         "image",
-        [(whole, ranks), (whole, near)] + spread(packed, "tile") + [(anywhere, window[0])],
+        [(whole, short), (whole, near)] + spread(packed, "tile"),
         per_owner,
         [
             ranks_here,
@@ -374,7 +395,7 @@
     packed = call(
         functools.partial(forward_kernel, devices, owners),
         "forward",
-        [(whole, ranks), (whole, near)] + spread(mixed, "freq"),
+        [(whole, short), (whole, near)] + spread(mixed, "freq"),
         per_device,
         [ranks_here, pltpu.VMEM((freqs, cols, width, 2 * tile), bf16), stage, one],
         **work,
@@ -382,7 +403,7 @@
     [out] = call(
         functools.partial(result_kernel, devices),
         "result",
-        [(whole, ranks), (whole, by_cols)] + spread(packed, "tile"),
+        [(whole, short), (whole, by_cols)] + spread(packed, "tile"),
         [((freqs, row_count, width), bf16)],
         [ranks_here, stage, pltpu.VMEM((rows, 2, col_tiles * slots, width), bf16), one],
         **work,

time: 54.2 us -> 53.4 us (0.985)
  waiting for transfers between devices: 16.6 us -> 14.1 us
  Pallas kernels: 11 us -> 12.6 us
    ppermute x20, waiting for transfers between devices: 16.6 us -> 14.1 us  [send(): lax.ppermute(value, axis, [(d, d ^ s) for d in range(lax.axis_size(axis))])]
    pallas_call x6, Pallas kernels: 11 us -> 12.6 us  [call(): pl.pallas_call(kernel, in_specs=[spec for spec, _ in ins], out_specs=spec...]
  transfers between devices with their start and end apart: 20 -> 20, of which waited for: 12 -> 11; matrix products, arithmetic and copies ran while one was open for 0% -> 0% of each run, Pallas kernels for 1% -> 6%
where the time goes in v3:
time: 53.4 us; the launch traced here: 53.2 us
  starting transfers between devices  26.3 us (49%)
  waiting for transfers between devices  14.1 us (26%)
  Pallas kernels  12.6 us (24%)
    ppermute x20, starting transfers between devices, send(): lax.ppermute(value, axis, [(d, d ^ s) for d in range(lax.axis_size(axis))])  26.3 us
    ppermute x20, waiting for transfers between devices, send(): lax.ppermute(value, axis, [(d, d ^ s) for d in range(lax.axis_size(axis))])  14.1 us
    pallas_call x6, Pallas kernels, call(): pl.pallas_call(kernel, in_specs=[spec for spec, _ in ins], out_specs=spec...  12.6 us
  transfers between devices with their start and end apart: 20, of which 11 were waited for; matrix products, arithmetic and copies ran while one was open for 0% of the time, Pallas kernels for 6%

profile of v3, /device:TPU:0, one launch (start us, length us, event | category | flops | bytes accessed | tf_op | source)
XLA Modules:
  0.0 53.2 jit_solution(3495334217814484178)
XLA Ops:
  0.0 4.1 %adjoint.1 = (bf16[1,224,128]{2,1,0:T(8,128)(2,1)S(1)}, bf16[1,224,128]{2,1,0:T(8,128)(2,1)S(1)}, bf16[1,224,128]{2,1,0:T(8,128)(2,1)S(1)}, bf16[1,224,128]{2,1,...) custom-call(s32[2,16,16]{2,1,0:T(8,128)} %ranks_far.3, ...), custom_call_target="tpu_custom_call" | custom-call | flops 805306368 | bytes 3145728 | tf_op jit(solution)/shard_map/adjoint/pallas_call | solution.py:28
  4.1 4.6 %collective-permute-start = (bf16[1,224,128]{2,1,0:T(8,128)(2,1)S(1)}, bf16[1,224,128]{2,1,0:T(8,128)(2,1)S(1)}, u32[]{:S(2)}, u32[]{:S(2)}) collective-permute-start(bf16[1,224,128]{2,1,0:T(8,128)(2,1)S(1)} %get-tuple-element.38), channel_id=1, source_target_pairs={{0,7},{1,6},{2,5},{3,4},{4,3},{5,2},{6,1},{7,0},{8,15},{9,14},{10,... | collective-permute-start | bytes 172040 | tf_op jit(solution)/shard_map/ppermute | solution.py:315
  8.7 0.6 %collective-permute-start.1 = (bf16[1,224,128]{2,1,0:T(8,128)(2,1)S(1)}, bf16[1,224,128]{2,1,0:T(8,128)(2,1)S(1)}, u32[]{:S(2)}, u32[]{:S(2)}) collective-permute-start(bf16[1,224,128]{2,1,0:T(8,128)(2,1)S(1)} %get-tuple-element.39), channel_id=1, source_target_pairs={{0,6},{1,7},{2,4},{3,5},{4,2},{5,3},{6,0},{7,1},{8,14},{9,15},{10,... | collective-permute-start | bytes 172040 | tf_op jit(solution)/shard_map/ppermute | solution.py:315
  9.7 2.2 %collective-permute-start.3 = (bf16[1,224,128]{2,1,0:T(8,128)(2,1)S(1)}, bf16[1,224,128]{2,1,0:T(8,128)(2,1)S(1)}, u32[]{:S(2)}, u32[]{:S(2)}) collective-permute-start(bf16[1,224,128]{2,1,0:T(8,128)(2,1)S(1)} %get-tuple-element.41), channel_id=1, source_target_pairs={{0,4},{1,5},{2,6},{3,7},{4,0},{5,1},{6,2},{7,3},{8,12},{9,13},{10,... | collective-permute-start | bytes 172040 | tf_op jit(solution)/shard_map/ppermute | solution.py:315
  11.9 1.0 %collective-permute-start.4 = (bf16[1,224,128]{2,1,0:T(8,128)(2,1)S(1)}, bf16[1,224,128]{2,1,0:T(8,128)(2,1)S(1)}, u32[]{:S(2)}, u32[]{:S(2)}) collective-permute-start(bf16[1,224,128]{2,1,0:T(8,128)(2,1)S(1)} %get-tuple-element.42), channel_id=1, source_target_pairs={{0,3},{1,2},{2,1},{3,0},{4,7},{5,6},{6,5},{7,4},{8,11},{9,10},{10,... | collective-permute-start | bytes 172040 | tf_op jit(solution)/shard_map/ppermute | solution.py:315
  12.9 0.9 %collective-permute-start.5 = (bf16[1,224,128]{2,1,0:T(8,128)(2,1)S(1)}, bf16[1,224,128]{2,1,0:T(8,128)(2,1)S(1)}, u32[]{:S(2)}, u32[]{:S(2)}) collective-permute-start(bf16[1,224,128]{2,1,0:T(8,128)(2,1)S(1)} %get-tuple-element.43), channel_id=1, source_target_pairs={{0,2},{1,3},{2,0},{3,1},{4,6},{5,7},{6,4},{7,5},{8,10},{9,11},{10,... | collective-permute-start | bytes 172040 | tf_op jit(solution)/shard_map/ppermute | solution.py:315
  13.7 1.7 %collective-permute-done.1.rest_1_ = bf16[1,224,128]{2,1,0:T(8,128)(2,1)S(1)} collective-permute-done((bf16[1,224,128]{2,1,0:T(8,128)(2,1)S(1)}, bf16[1,224,128]{2,1,0:T(8,128)(2,1)S(1)}, u32[]{:S(2)}, u32[]{:S(2)}) %collective-permute-start.1) | collective-permute-done | bytes 57376 | tf_op jit(solution)/shard_map/ppermute | solution.py:315
  15.4 3.1 %prepare.1 = (bf16[2,8,2,2,2,48,256]{6,5,4,3,2,1,0:T(8,128)(2,1)S(1)}, s32[1,64]{1,0:T(1,128)S(1)}, bf16[256,256]{1,0:T(8,128)(2,1)S(1)}, bf16[256,256]{1,0:T(8,128)(2,1)S(1)}) custom-call(s32[2,16,16]{2,1,0:T(8,128)} %ranks_far.3, bf16[2,8,2,2,2,48,256]{6,5,4,3,2,1,0:T(8,128)(2,1)} %bitcast.4, s32[64,64]{1,0:T(8,128)S(1)} %copy-done.2, ...), custom_call_target="tpu_custom_call" | custom-call | bytes 3145728 | tf_op jit(solution)/shard_map/prepare/pallas_call | solution.py:28
  18.5 1.0 %collective-permute-done.3.rest_3_ = bf16[1,224,128]{2,1,0:T(8,128)(2,1)S(1)} collective-permute-done((bf16[1,224,128]{2,1,0:T(8,128)(2,1)S(1)}, bf16[1,224,128]{2,1,0:T(8,128)(2,1)S(1)}, u32[]{:S(2)}, u32[]{:S(2)}) %collective-permute-start.3) | collective-permute-done | bytes 57376 | tf_op jit(solution)/shard_map/ppermute | solution.py:315
  19.6 1.4 %image.1 = (bf16[2,32,512]{2,1,0:T(8,128)(2,1)S(1)}, bf16[2,32,512]{2,1,0:T(8,128)(2,1)S(1)}, bf16[2,32,512]{2,1,0:T(8,128)(2,1)S(1)}, bf16[2,32,512]{2,1,0:T(8,128)(2,1)S(1)}) custom-call(s32[1,64]{1,0:T(1,128)S(1)} %get-tuple-element.34.ranks_near, bf16[2,8,2,2,2,48,256]{6,5,4,3,2,1,0:T(8,128)(2,1)S(1)} %get-tuple-element.35.basis, ...), custom_call_target="tpu_custom_call" | custom-call | flops 805306368 | bytes 3145728 | tf_op jit(solution)/shard_map/image/pallas_call | solution.py:28
  21.0 2.5 %collective-permute-start.7 = (bf16[2,32,512]{2,1,0:T(8,128)(2,1)S(1)}, bf16[2,32,512]{2,1,0:T(8,128)(2,1)S(1)}, u32[]{:S(2)}, u32[]{:S(2)}) collective-permute-start(bf16[2,32,512]{2,1,0:T(8,128)(2,1)S(1)} %get-tuple-element.45), channel_id=1, source_target_pairs={{0,24},{8,16},{16,8},{24,0},{1,25},{9,17},{17,9},{25,1},{2,26},{10... | collective-permute-start | bytes 196616 | tf_op jit(solution)/shard_map/ppermute | solution.py:315
  23.5 0.5 collective-permute-start.8
  24.0 0.5 %collective-permute-start.9 = (bf16[2,32,512]{2,1,0:T(8,128)(2,1)S(1)}, bf16[2,32,512]{2,1,0:T(8,128)(2,1)S(1)}, u32[]{:S(2)}, u32[]{:S(2)}) collective-permute-start(bf16[2,32,512]{2,1,0:T(8,128)(2,1)S(1)} %get-tuple-element.47), channel_id=1, source_target_pairs={{0,8},{8,0},{16,24},{24,16},{1,9},{9,1},{17,25},{25,17},{2,10},{10... | collective-permute-start | bytes 196616 | tf_op jit(solution)/shard_map/ppermute | solution.py:315
  24.5 1.7 %collective-permute-done.7.rest_0_ = bf16[2,32,512]{2,1,0:T(8,128)(2,1)S(1)} collective-permute-done((bf16[2,32,512]{2,1,0:T(8,128)(2,1)S(1)}, bf16[2,32,512]{2,1,0:T(8,128)(2,1)S(1)}, u32[]{:S(2)}, u32[]{:S(2)}) %collective-permute-start.7) | collective-permute-done | bytes 65568 | tf_op jit(solution)/shard_map/ppermute | solution.py:315
  26.2 1.5 %collective-permute-done.8.rest_1_ = bf16[2,32,512]{2,1,0:T(8,128)(2,1)S(1)} collective-permute-done((bf16[2,32,512]{2,1,0:T(8,128)(2,1)S(1)}, bf16[2,32,512]{2,1,0:T(8,128)(2,1)S(1)}, u32[]{:S(2)}, u32[]{:S(2)}) %collective-permute-start.8) | collective-permute-done | bytes 65568 | tf_op jit(solution)/shard_map/ppermute | solution.py:315
  27.7 0.5 collective-permute-done.9.rest_2_
  28.6 1.6 %collective-permute-start.10 = (bf16[2,32,512]{2,1,0:T(8,128)(2,1)S(1)}, bf16[2,32,512]{2,1,0:T(8,128)(2,1)S(1)}, u32[]{:S(2)}, u32[]{:S(2)}) collective-permute-start(bf16[2,32,512]{2,1,0:T(8,128)(2,1)S(1)} %get-tuple-element.49), channel_id=1, source_target_pairs={{0,24},{8,16},{16,8},{24,0},{1,25},{9,17},{17,9},{25,1},{2,26},{10... | collective-permute-start | bytes 196616 | tf_op jit(solution)/shard_map/ppermute | solution.py:315
  30.2 0.6 %collective-permute-start.11 = (bf16[2,32,512]{2,1,0:T(8,128)(2,1)S(1)}, bf16[2,32,512]{2,1,0:T(8,128)(2,1)S(1)}, u32[]{:S(2)}, u32[]{:S(2)}) collective-permute-start(bf16[2,32,512]{2,1,0:T(8,128)(2,1)S(1)} %get-tuple-element.50), channel_id=1, source_target_pairs={{0,16},{8,24},{16,0},{24,8},{1,17},{9,25},{17,1},{25,9},{2,18},{10... | collective-permute-start | bytes 196616 | tf_op jit(solution)/shard_map/ppermute | solution.py:315
  30.7 1.4 %collective-permute-start.12 = (bf16[2,32,512]{2,1,0:T(8,128)(2,1)S(1)}, bf16[2,32,512]{2,1,0:T(8,128)(2,1)S(1)}, u32[]{:S(2)}, u32[]{:S(2)}) collective-permute-start(bf16[2,32,512]{2,1,0:T(8,128)(2,1)S(1)} %get-tuple-element.51), channel_id=1, source_target_pairs={{0,8},{8,0},{16,24},{24,16},{1,9},{9,1},{17,25},{25,17},{2,10},{10... | collective-permute-start | bytes 196616 | tf_op jit(solution)/shard_map/ppermute | solution.py:315
  32.2 1.7 %collective-permute-done.10.rest_0_ = bf16[2,32,512]{2,1,0:T(8,128)(2,1)S(1)} collective-permute-done((bf16[2,32,512]{2,1,0:T(8,128)(2,1)S(1)}, bf16[2,32,512]{2,1,0:T(8,128)(2,1)S(1)}, u32[]{:S(2)}, u32[]{:S(2)}) %collective-permute-start.10) | collective-permute-done | bytes 65568 | tf_op jit(solution)/shard_map/ppermute | solution.py:315
  33.8 0.7 %collective-permute-done.11.rest_1_ = bf16[2,32,512]{2,1,0:T(8,128)(2,1)S(1)} collective-permute-done((bf16[2,32,512]{2,1,0:T(8,128)(2,1)S(1)}, bf16[2,32,512]{2,1,0:T(8,128)(2,1)S(1)}, u32[]{:S(2)}, u32[]{:S(2)}) %collective-permute-start.11) | collective-permute-done | bytes 65568 | tf_op jit(solution)/shard_map/ppermute | solution.py:315
  35.0 1.6 %forward.1 = (bf16[1,224,128]{2,1,0:T(8,128)(2,1)S(1)}, bf16[1,224,128]{2,1,0:T(8,128)(2,1)S(1)}, bf16[1,224,128]{2,1,0:T(8,128)(2,1)S(1)}, bf16[1,224,128]{2,1,...) custom-call(s32[1,64]{1,0:T(1,128)S(1)} %get-tuple-element.34.ranks_, ...), custom_call_target="tpu_custom_call" | custom-call | flops 805306368 | bytes 3145728 | tf_op jit(solution)/shard_map/forward/pallas_call | solution.py:28
  36.6 2.4 %collective-permute-start.13 = (bf16[1,224,128]{2,1,0:T(8,128)(2,1)S(1)}, bf16[1,224,128]{2,1,0:T(8,128)(2,1)S(1)}, u32[]{:S(2)}, u32[]{:S(2)}) collective-permute-start(bf16[1,224,128]{2,1,0:T(8,128)(2,1)S(1)} %get-tuple-element.53), channel_id=1, source_target_pairs={{0,7},{1,6},{2,5},{3,4},{4,3},{5,2},{6,1},{7,0},{8,15},{9,14},{10,... | collective-permute-start | bytes 172040 | tf_op jit(solution)/shard_map/ppermute | solution.py:315
  39.0 1.6 %collective-permute-start.14 = (bf16[1,224,128]{2,1,0:T(8,128)(2,1)S(1)}, bf16[1,224,128]{2,1,0:T(8,128)(2,1)S(1)}, u32[]{:S(2)}, u32[]{:S(2)}) collective-permute-start(bf16[1,224,128]{2,1,0:T(8,128)(2,1)S(1)} %get-tuple-element.54), channel_id=1, source_target_pairs={{0,6},{1,7},{2,4},{3,5},{4,2},{5,3},{6,0},{7,1},{8,14},{9,15},{10,... | collective-permute-start | bytes 172040 | tf_op jit(solution)/shard_map/ppermute | solution.py:315
  40.9 2.3 %collective-permute-start.16 = (bf16[1,224,128]{2,1,0:T(8,128)(2,1)S(1)}, bf16[1,224,128]{2,1,0:T(8,128)(2,1)S(1)}, u32[]{:S(2)}, u32[]{:S(2)}) collective-permute-start(bf16[1,224,128]{2,1,0:T(8,128)(2,1)S(1)} %get-tuple-element.56), channel_id=1, source_target_pairs={{0,4},{1,5},{2,6},{3,7},{4,0},{5,1},{6,2},{7,3},{8,12},{9,13},{10,... | collective-permute-start | bytes 172040 | tf_op jit(solution)/shard_map/ppermute | solution.py:315
  43.2 0.9 %collective-permute-start.17 = (bf16[1,224,128]{2,1,0:T(8,128)(2,1)S(1)}, bf16[1,224,128]{2,1,0:T(8,128)(2,1)S(1)}, u32[]{:S(2)}, u32[]{:S(2)}) collective-permute-start(bf16[1,224,128]{2,1,0:T(8,128)(2,1)S(1)} %get-tuple-element.57), channel_id=1, source_target_pairs={{0,3},{1,2},{2,1},{3,0},{4,7},{5,6},{6,5},{7,4},{8,11},{9,10},{10,... | collective-permute-start | bytes 172040 | tf_op jit(solution)/shard_map/ppermute | solution.py:315
  44.1 0.9 %collective-permute-start.18 = (bf16[1,224,128]{2,1,0:T(8,128)(2,1)S(1)}, bf16[1,224,128]{2,1,0:T(8,128)(2,1)S(1)}, u32[]{:S(2)}, u32[]{:S(2)}) collective-permute-start(bf16[1,224,128]{2,1,0:T(8,128)(2,1)S(1)} %get-tuple-element.58), channel_id=1, source_target_pairs={{0,2},{1,3},{2,0},{3,1},{4,6},{5,7},{6,4},{7,5},{8,10},{9,11},{10,... | collective-permute-start | bytes 172040 | tf_op jit(solution)/shard_map/ppermute | solution.py:315
  45.0 1.2 %collective-permute-start.19 = (bf16[1,224,128]{2,1,0:T(8,128)(2,1)S(1)}, bf16[1,224,128]{2,1,0:T(8,128)(2,1)S(1)}, u32[]{:S(2)}, u32[]{:S(2)}) collective-permute-start(bf16[1,224,128]{2,1,0:T(8,128)(2,1)S(1)} %get-tuple-element.59), channel_id=1, source_target_pairs={{0,1},{1,0},{2,3},{3,2},{4,5},{5,4},{6,7},{7,6},{8,9},{9,8},{10,11... | collective-permute-start | bytes 172040 | tf_op jit(solution)/shard_map/ppermute | solution.py:315
  46.2 3.1 %collective-permute-done.15.rest_2_ = bf16[1,224,128]{2,1,0:T(8,128)(2,1)S(1)} collective-permute-done((bf16[1,224,128]{2,1,0:T(8,128)(2,1)S(1)}, bf16[1,224,128]{2,1,0:T(8,128)(2,1)S(1)}, u32[]{:S(2)}, u32[]{:S(2)}) %collective-permute-start.15) | collective-permute-done | bytes 57376 | tf_op jit(solution)/shard_map/ppermute | solution.py:315
  49.3 1.2 %collective-permute-done.16.rest_3_ = bf16[1,224,128]{2,1,0:T(8,128)(2,1)S(1)} collective-permute-done((bf16[1,224,128]{2,1,0:T(8,128)(2,1)S(1)}, bf16[1,224,128]{2,1,0:T(8,128)(2,1)S(1)}, u32[]{:S(2)}, u32[]{:S(2)}) %collective-permute-start.16) | collective-permute-done | bytes 57376 | tf_op jit(solution)/shard_map/ppermute | solution.py:315
  50.6 0.5 collective-permute-done.18.rest_5_
  51.1 2.1 %result.1 = bf16[2,512,128]{2,1,0:T(8,128)(2,1)} custom-call(s32[1,64]{1,0:T(1,128)S(1)} %get-tuple-element.34.ranks_near, bf16[2,2,8,2,2,48,256]{6,5,4,3,2,1,0:T(8,128)(2,1)S(1)} %bitcast.3, bf16[1,224,128]{2,1,0:T(8,128)(2,1)S(1)} %collective-permute-done.13.rest_0_, bf16[1,224,128]{2,1,0:T(8,128)(2,1)S(1)} %collective-permute-done.14.rest_1_, ...), custom_call_target="tpu_custom_call" | custom-call | flops 805306368 | bytes 3145728 | tf_op jit(solution)/shard_map/result/pallas_call | solution.py:28
  (24 shorter events, 1.5 us)
Async XLA Ops:
  0.0 15.4 %copy-start.3 = (f32[64,128]{1,0:T(8,128)S(1)}, f32[64,128]{1,0:T(8,128)}, u32[]{:S(2)}) copy-start(f32[64,128]{1,0:T(8,128)} %constant.6.clone.table) | copy-start | bytes 98308
  0.0 15.4 %copy-start.1 = (f32[16,4096]{1,0:T(8,128)S(1)}, f32[16,4096]{1,0:T(8,128)}, u32[]{:S(2)}) copy-start(f32[16,4096]{1,0:T(8,128)} %constant.7.clone.choice) | copy-start | bytes 786436
  0.0 15.4 %copy-start.4 = (f32[16,256]{1,0:T(8,128)S(1)}, f32[16,256]{1,0:T(8,128)}, u32[]{:S(2)}) copy-start(f32[16,256]{1,0:T(8,128)} %constant.8.clone.same) | copy-start | bytes 49156
  0.0 15.4 %copy-start.2 = (s32[64,64]{1,0:T(8,128)S(1)}, s32[64,64]{1,0:T(8,128)}, u32[]{:S(2)}) copy-start(s32[64,64]{1,0:T(8,128)} %mask.1) | copy-start | bytes 49156
  4.1 8.7 %collective-permute-start = (bf16[1,224,128]{2,1,0:T(8,128)(2,1)S(1)}, bf16[1,224,128]{2,1,0:T(8,128)(2,1)S(1)}, u32[]{:S(2)}, u32[]{:S(2)}) collective-permute-start(bf16[1,224,128]{2,1,0:T(8,128)(2,1)S(1)} %get-tuple-element.38), channel_id=1, source_target_pairs={{0,7},{1,6},{2,5},{3,4},{4,3},{5,2},{6,1},{7,0},{8,15},{9,14},{10,... | collective-permute-start | bytes 172040 | tf_op jit(solution)/shard_map/ppermute | solution.py:315
  8.7 6.7 %collective-permute-start.1 = (bf16[1,224,128]{2,1,0:T(8,128)(2,1)S(1)}, bf16[1,224,128]{2,1,0:T(8,128)(2,1)S(1)}, u32[]{:S(2)}, u32[]{:S(2)}) collective-permute-start(bf16[1,224,128]{2,1,0:T(8,128)(2,1)S(1)} %get-tuple-element.39), channel_id=1, source_target_pairs={{0,6},{1,7},{2,4},{3,5},{4,2},{5,3},{6,0},{7,1},{8,14},{9,15},{10,... | collective-permute-start | bytes 172040 | tf_op jit(solution)/shard_map/ppermute | solution.py:315
  9.3 9.2 %collective-permute-start.2 = (bf16[1,224,128]{2,1,0:T(8,128)(2,1)S(1)}, bf16[1,224,128]{2,1,0:T(8,128)(2,1)S(1)}, u32[]{:S(2)}, u32[]{:S(2)}) collective-permute-start(bf16[1,224,128]{2,1,0:T(8,128)(2,1)S(1)} %get-tuple-element.40), channel_id=1, source_target_pairs={{0,5},{1,4},{2,7},{3,6},{4,1},{5,0},{6,3},{7,2},{8,13},{9,12},{10,... | collective-permute-start | bytes 172040 | tf_op jit(solution)/shard_map/ppermute | solution.py:315
  9.7 9.8 %collective-permute-start.3 = (bf16[1,224,128]{2,1,0:T(8,128)(2,1)S(1)}, bf16[1,224,128]{2,1,0:T(8,128)(2,1)S(1)}, u32[]{:S(2)}, u32[]{:S(2)}) collective-permute-start(bf16[1,224,128]{2,1,0:T(8,128)(2,1)S(1)} %get-tuple-element.41), channel_id=1, source_target_pairs={{0,4},{1,5},{2,6},{3,7},{4,0},{5,1},{6,2},{7,3},{8,12},{9,13},{10,... | collective-permute-start | bytes 172040 | tf_op jit(solution)/shard_map/ppermute | solution.py:315
  11.9 7.6 %collective-permute-start.4 = (bf16[1,224,128]{2,1,0:T(8,128)(2,1)S(1)}, bf16[1,224,128]{2,1,0:T(8,128)(2,1)S(1)}, u32[]{:S(2)}, u32[]{:S(2)}) collective-permute-start(bf16[1,224,128]{2,1,0:T(8,128)(2,1)S(1)} %get-tuple-element.42), channel_id=1, source_target_pairs={{0,3},{1,2},{2,1},{3,0},{4,7},{5,6},{6,5},{7,4},{8,11},{9,10},{10,... | collective-permute-start | bytes 172040 | tf_op jit(solution)/shard_map/ppermute | solution.py:315
  12.9 6.7 %collective-permute-start.5 = (bf16[1,224,128]{2,1,0:T(8,128)(2,1)S(1)}, bf16[1,224,128]{2,1,0:T(8,128)(2,1)S(1)}, u32[]{:S(2)}, u32[]{:S(2)}) collective-permute-start(bf16[1,224,128]{2,1,0:T(8,128)(2,1)S(1)} %get-tuple-element.43), channel_id=1, source_target_pairs={{0,2},{1,3},{2,0},{3,1},{4,6},{5,7},{6,4},{7,5},{8,10},{9,11},{10,... | collective-permute-start | bytes 172040 | tf_op jit(solution)/shard_map/ppermute | solution.py:315
  15.4 4.2 %collective-permute-start.6 = (bf16[1,224,128]{2,1,0:T(8,128)(2,1)S(1)}, bf16[1,224,128]{2,1,0:T(8,128)(2,1)S(1)}, u32[]{:S(2)}, u32[]{:S(2)}) collective-permute-start(bf16[1,224,128]{2,1,0:T(8,128)(2,1)S(1)} %get-tuple-element.44), channel_id=1, source_target_pairs={{0,1},{1,0},{2,3},{3,2},{4,5},{5,4},{6,7},{7,6},{8,9},{9,8},{10,11... | collective-permute-start | bytes 172040 | tf_op jit(solution)/shard_map/ppermute | solution.py:315
  19.5 31.5 %copy-start = (bf16[2,2,16,2,48,256]{5,4,3,2,1,0:T(8,128)(2,1)S(1)}, bf16[2,2,16,2,48,256]{5,4,3,2,1,0:T(8,128)(2,1)}, u32[]{:S(2)}) copy-start(bf16[2,2,16,2,48,256]{5,4,3,2,1,0:T(8,128)(2,1)} %param.9) | copy-start | bytes 9437188
  21.0 5.3 %collective-permute-start.7 = (bf16[2,32,512]{2,1,0:T(8,128)(2,1)S(1)}, bf16[2,32,512]{2,1,0:T(8,128)(2,1)S(1)}, u32[]{:S(2)}, u32[]{:S(2)}) collective-permute-start(bf16[2,32,512]{2,1,0:T(8,128)(2,1)S(1)} %get-tuple-element.45), channel_id=1, source_target_pairs={{0,24},{8,16},{16,8},{24,0},{1,25},{9,17},{17,9},{25,1},{2,26},{10... | collective-permute-start | bytes 196616 | tf_op jit(solution)/shard_map/ppermute | solution.py:315
  23.5 4.3 %collective-permute-start.8 = (bf16[2,32,512]{2,1,0:T(8,128)(2,1)S(1)}, bf16[2,32,512]{2,1,0:T(8,128)(2,1)S(1)}, u32[]{:S(2)}, u32[]{:S(2)}) collective-permute-start(bf16[2,32,512]{2,1,0:T(8,128)(2,1)S(1)} %get-tuple-element.46), channel_id=1, source_target_pairs={{0,16},{8,24},{16,0},{24,8},{1,17},{9,25},{17,1},{25,9},{2,18},{10... | collective-permute-start | bytes 196616 | tf_op jit(solution)/shard_map/ppermute | solution.py:315
  24.0 4.3 %collective-permute-start.9 = (bf16[2,32,512]{2,1,0:T(8,128)(2,1)S(1)}, bf16[2,32,512]{2,1,0:T(8,128)(2,1)S(1)}, u32[]{:S(2)}, u32[]{:S(2)}) collective-permute-start(bf16[2,32,512]{2,1,0:T(8,128)(2,1)S(1)} %get-tuple-element.47), channel_id=1, source_target_pairs={{0,8},{8,0},{16,24},{24,16},{1,9},{9,1},{17,25},{25,17},{2,10},{10... | collective-permute-start | bytes 196616 | tf_op jit(solution)/shard_map/ppermute | solution.py:315
  28.6 5.2 %collective-permute-start.10 = (bf16[2,32,512]{2,1,0:T(8,128)(2,1)S(1)}, bf16[2,32,512]{2,1,0:T(8,128)(2,1)S(1)}, u32[]{:S(2)}, u32[]{:S(2)}) collective-permute-start(bf16[2,32,512]{2,1,0:T(8,128)(2,1)S(1)} %get-tuple-element.49), channel_id=1, source_target_pairs={{0,24},{8,16},{16,8},{24,0},{1,25},{9,17},{17,9},{25,1},{2,26},{10... | collective-permute-start | bytes 196616 | tf_op jit(solution)/shard_map/ppermute | solution.py:315
  30.2 4.4 %collective-permute-start.11 = (bf16[2,32,512]{2,1,0:T(8,128)(2,1)S(1)}, bf16[2,32,512]{2,1,0:T(8,128)(2,1)S(1)}, u32[]{:S(2)}, u32[]{:S(2)}) collective-permute-start(bf16[2,32,512]{2,1,0:T(8,128)(2,1)S(1)} %get-tuple-element.50), channel_id=1, source_target_pairs={{0,16},{8,24},{16,0},{24,8},{1,17},{9,25},{17,1},{25,9},{2,18},{10... | collective-permute-start | bytes 196616 | tf_op jit(solution)/shard_map/ppermute | solution.py:315
  30.7 4.3 %collective-permute-start.12 = (bf16[2,32,512]{2,1,0:T(8,128)(2,1)S(1)}, bf16[2,32,512]{2,1,0:T(8,128)(2,1)S(1)}, u32[]{:S(2)}, u32[]{:S(2)}) collective-permute-start(bf16[2,32,512]{2,1,0:T(8,128)(2,1)S(1)} %get-tuple-element.51), channel_id=1, source_target_pairs={{0,8},{8,0},{16,24},{24,16},{1,9},{9,1},{17,25},{25,17},{2,10},{10... | collective-permute-start | bytes 196616 | tf_op jit(solution)/shard_map/ppermute | solution.py:315
  36.6 7.6 %collective-permute-start.13 = (bf16[1,224,128]{2,1,0:T(8,128)(2,1)S(1)}, bf16[1,224,128]{2,1,0:T(8,128)(2,1)S(1)}, u32[]{:S(2)}, u32[]{:S(2)}) collective-permute-start(bf16[1,224,128]{2,1,0:T(8,128)(2,1)S(1)} %get-tuple-element.53), channel_id=1, source_target_pairs={{0,7},{1,6},{2,5},{3,4},{4,3},{5,2},{6,1},{7,0},{8,15},{9,14},{10,... | collective-permute-start | bytes 172040 | tf_op jit(solution)/shard_map/ppermute | solution.py:315
  39.0 6.0 %collective-permute-start.14 = (bf16[1,224,128]{2,1,0:T(8,128)(2,1)S(1)}, bf16[1,224,128]{2,1,0:T(8,128)(2,1)S(1)}, u32[]{:S(2)}, u32[]{:S(2)}) collective-permute-start(bf16[1,224,128]{2,1,0:T(8,128)(2,1)S(1)} %get-tuple-element.54), channel_id=1, source_target_pairs={{0,6},{1,7},{2,4},{3,5},{4,2},{5,3},{6,0},{7,1},{8,14},{9,15},{10,... | collective-permute-start | bytes 172040 | tf_op jit(solution)/shard_map/ppermute | solution.py:315
  40.6 8.7 %collective-permute-start.15 = (bf16[1,224,128]{2,1,0:T(8,128)(2,1)S(1)}, bf16[1,224,128]{2,1,0:T(8,128)(2,1)S(1)}, u32[]{:S(2)}, u32[]{:S(2)}) collective-permute-start(bf16[1,224,128]{2,1,0:T(8,128)(2,1)S(1)} %get-tuple-element.55), channel_id=1, source_target_pairs={{0,5},{1,4},{2,7},{3,6},{4,1},{5,0},{6,3},{7,2},{8,13},{9,12},{10,... | collective-permute-start | bytes 172040 | tf_op jit(solution)/shard_map/ppermute | solution.py:315
  40.9 9.7 %collective-permute-start.16 = (bf16[1,224,128]{2,1,0:T(8,128)(2,1)S(1)}, bf16[1,224,128]{2,1,0:T(8,128)(2,1)S(1)}, u32[]{:S(2)}, u32[]{:S(2)}) collective-permute-start(bf16[1,224,128]{2,1,0:T(8,128)(2,1)S(1)} %get-tuple-element.56), channel_id=1, source_target_pairs={{0,4},{1,5},{2,6},{3,7},{4,0},{5,1},{6,2},{7,3},{8,12},{9,13},{10,... | collective-permute-start | bytes 172040 | tf_op jit(solution)/shard_map/ppermute | solution.py:315
  43.2 7.4 %collective-permute-start.17 = (bf16[1,224,128]{2,1,0:T(8,128)(2,1)S(1)}, bf16[1,224,128]{2,1,0:T(8,128)(2,1)S(1)}, u32[]{:S(2)}, u32[]{:S(2)}) collective-permute-start(bf16[1,224,128]{2,1,0:T(8,128)(2,1)S(1)} %get-tuple-element.57), channel_id=1, source_target_pairs={{0,3},{1,2},{2,1},{3,0},{4,7},{5,6},{6,5},{7,4},{8,11},{9,10},{10,... | collective-permute-start | bytes 172040 | tf_op jit(solution)/shard_map/ppermute | solution.py:315
  44.1 6.9 %collective-permute-start.18 = (bf16[1,224,128]{2,1,0:T(8,128)(2,1)S(1)}, bf16[1,224,128]{2,1,0:T(8,128)(2,1)S(1)}, u32[]{:S(2)}, u32[]{:S(2)}) collective-permute-start(bf16[1,224,128]{2,1,0:T(8,128)(2,1)S(1)} %get-tuple-element.58), channel_id=1, source_target_pairs={{0,2},{1,3},{2,0},{3,1},{4,6},{5,7},{6,4},{7,5},{8,10},{9,11},{10,... | collective-permute-start | bytes 172040 | tf_op jit(solution)/shard_map/ppermute | solution.py:315
  45.0 6.1 %collective-permute-start.19 = (bf16[1,224,128]{2,1,0:T(8,128)(2,1)S(1)}, bf16[1,224,128]{2,1,0:T(8,128)(2,1)S(1)}, u32[]{:S(2)}, u32[]{:S(2)}) collective-permute-start(bf16[1,224,128]{2,1,0:T(8,128)(2,1)S(1)} %get-tuple-element.59), channel_id=1, source_target_pairs={{0,1},{1,0},{2,3},{3,2},{4,5},{5,4},{6,7},{7,6},{8,9},{9,8},{10,11... | collective-permute-start | bytes 172040 | tf_op jit(solution)/shard_map/ppermute | solution.py:315

commit v4 on v3

--- a/solution.py
+++ b/solution.py
@@ -124,25 +124,26 @@
                 copies[f, i, p] = pltpu.make_async_copy(
                     basis_far.at[f, i, at], basis.at[f, i, at], sems.at[2 + (f * rows + i) * parts + p]
                 )
-                copies[f, i, p].start()
+                copies[f, i, p].start(priority=(p + f) % 2)
     data_copy.wait()
     for f in range(freqs):
-        values = u_ref[f].astype(f32)
-        lane = lax.broadcasted_iota(jnp.int32, values.shape, 1)
-        rolled = pltpu.roll(values, half, 1)
-        turned[f] = jnp.where(lane < half, rolled, -rolled).astype(bf16)
+        for i in range(rows):
+            values = u_ref[f, i * tile : (i + 1) * tile, :]
+            wide = values.astype(f32)
+            lane = lax.broadcasted_iota(jnp.int32, wide.shape, 1)
+            rolled = pltpu.roll(wide, half, 1)
+            turned[f, i, :tile, :] = values
+            turned[f, i, tile:, :] = jnp.where(lane < half, rolled, -rolled).astype(bf16)
     waited = False
     for m in range(freqs // 2):
         for i in range(rows):
-            here = pl.ds(i * tile, tile)
             for p in range(parts):
                 pair = []
                 at = pl.ds(p * per, per)
                 for f in (2 * m, 2 * m + 1):
                     copies[f, i, p].wait()
                     both = side_by_side(basis[f, i, at, :, 0], basis[f, i, at, :, 1])
-                    data = jnp.concatenate([u_ref[f, here, :], turned[f, here, :]], axis=0)
-                    pair.append(dot(both, data, 1, 0))
+                    pair.append(dot(both, turned[f, i], 1, 0))
                 if not waited:
                     rank_copy.wait()
                     waited = True
@@ -197,10 +198,14 @@
     freqs, devices, rows, cols = basis_far.shape[:4]
     row_tiles, col_tiles = ranks.shape[1:]
     me = lax.axis_index("tile")
-    basis_copy = pltpu.make_async_copy(basis_far, basis, sems.at[0])
-    rank_copy = pltpu.make_async_copy(ranks_far, ranks, sems.at[1])
+    rank_copy = pltpu.make_async_copy(ranks_far, ranks, sems.at[freqs * devices])
     rank_copy.start()
-    basis_copy.start()
+    basis_copies = []
+    for f in range(freqs):
+        for d in range(devices):
+            n = f * devices + d
+            basis_copies.append(pltpu.make_async_copy(basis_far.at[f, d], basis.at[f, d], sems.at[n]))
+            basis_copies[n].start(priority=n % 2)
     exact = lax.Precision.HIGHEST
     full[...] = dot(mask[...].astype(f32), table[...], 0, 0, exact)
     quarter, side = same.shape
@@ -223,7 +228,8 @@
             for col in range(col_tiles):
                 short[0, at] = ranks[2 * m, me * rows + i, col]
                 at += 1
-    basis_copy.wait()
+    for copy in basis_copies:
+        copy.wait()
 
 
 def mix_kernel(owners, high, low, *rest):
@@ -343,7 +349,7 @@
 
     table = lag_tables(count, time_mask.shape[0], 128)
     choice, same = lag_choice(count, quarter)
-    parts = math.gcd(devices, 2)
+    parts = math.gcd(devices, 4)
     packed = call(
         functools.partial(adjoint_kernel, devices, parts),
         "adjoint",
@@ -353,7 +359,7 @@
             pltpu.SMEM(ranks.shape, jnp.int32),
             pltpu.VMEM((freqs, row_count, width), bf16),
             pltpu.VMEM(by_cols.shape, bf16),
-            pltpu.VMEM((freqs, row_count, width), bf16),
+            pltpu.VMEM((freqs, rows, 2 * tile, width), bf16),
             stage,
             one((2 + freqs * rows * parts,)),
         ],
@@ -366,7 +372,7 @@
         + [(whole, jnp.asarray(x)) for x in (time_mask, table, choice, same)]
         + [(anywhere, packed[0])],
         [(by_rows.shape, bf16), ((1, count_short), jnp.int32)] + [((side, side), bf16)] * 2,
-        [pltpu.SMEM(ranks.shape, jnp.int32), pltpu.VMEM((width // 2, 128), f32), one((2,))],
+        [pltpu.SMEM(ranks.shape, jnp.int32), pltpu.VMEM((width // 2, 128), f32), one((freqs * devices + 1,))],
         specs=[whole, scalars, whole, whole],
         moved=u_basis.size * 2,
     )

time: 53.4 us -> 54.1 us (1.013)
  transfers between devices with their start and end apart: 20 -> 20, of which waited for: 11 -> 11; matrix products, arithmetic and copies ran while one was open for 0% -> 0% of each run, Pallas kernels for 6% -> 5%
where the time goes in v4:
time: 54.1 us; the launch traced here: 53.8 us
  starting transfers between devices  26.1 us (48%)
  waiting for transfers between devices  14.5 us (27%)
  Pallas kernels  13.1 us (24%)
    ppermute x20, starting transfers between devices, send(): lax.ppermute(value, axis, [(d, d ^ s) for d in range(lax.axis_size(axis))])  26.1 us
    ppermute x20, waiting for transfers between devices, send(): lax.ppermute(value, axis, [(d, d ^ s) for d in range(lax.axis_size(axis))])  14.5 us
    pallas_call x6, Pallas kernels, call(): pl.pallas_call(kernel, in_specs=[spec for spec, _ in ins], out_specs=spec...  13.1 us
  transfers between devices with their start and end apart: 20, of which 11 were waited for; matrix products, arithmetic and copies ran while one was open for 0% of the time, Pallas kernels for 5%

profile of v4, /device:TPU:0, one launch (start us, length us, event | category | flops | bytes accessed | tf_op | source)
XLA Modules:
  0.0 53.8 jit_solution(3032810346632526748)
XLA Ops:
  0.0 4.8 %adjoint.1 = (bf16[1,224,128]{2,1,0:T(8,128)(2,1)S(1)}, bf16[1,224,128]{2,1,0:T(8,128)(2,1)S(1)}, bf16[1,224,128]{2,1,0:T(8,128)(2,1)S(1)}, bf16[1,224,128]{2,1,...) custom-call(s32[2,16,16]{2,1,0:T(8,128)} %ranks_far.3, ...), custom_call_target="tpu_custom_call" | custom-call | flops 805306368 | bytes 3145728 | tf_op jit(solution)/shard_map/adjoint/pallas_call | solution.py:28
  4.8 4.5 %collective-permute-start = (bf16[1,224,128]{2,1,0:T(8,128)(2,1)S(1)}, bf16[1,224,128]{2,1,0:T(8,128)(2,1)S(1)}, u32[]{:S(2)}, u32[]{:S(2)}) collective-permute-start(bf16[1,224,128]{2,1,0:T(8,128)(2,1)S(1)} %get-tuple-element.38), channel_id=1, source_target_pairs={{0,7},{1,6},{2,5},{3,4},{4,3},{5,2},{6,1},{7,0},{8,15},{9,14},{10,... | collective-permute-start | bytes 172040 | tf_op jit(solution)/shard_map/ppermute | solution.py:321
  9.3 0.7 %collective-permute-start.1 = (bf16[1,224,128]{2,1,0:T(8,128)(2,1)S(1)}, bf16[1,224,128]{2,1,0:T(8,128)(2,1)S(1)}, u32[]{:S(2)}, u32[]{:S(2)}) collective-permute-start(bf16[1,224,128]{2,1,0:T(8,128)(2,1)S(1)} %get-tuple-element.39), channel_id=1, source_target_pairs={{0,6},{1,7},{2,4},{3,5},{4,2},{5,3},{6,0},{7,1},{8,14},{9,15},{10,... | collective-permute-start | bytes 172040 | tf_op jit(solution)/shard_map/ppermute | solution.py:321
  10.3 2.3 %collective-permute-start.3 = (bf16[1,224,128]{2,1,0:T(8,128)(2,1)S(1)}, bf16[1,224,128]{2,1,0:T(8,128)(2,1)S(1)}, u32[]{:S(2)}, u32[]{:S(2)}) collective-permute-start(bf16[1,224,128]{2,1,0:T(8,128)(2,1)S(1)} %get-tuple-element.41), channel_id=1, source_target_pairs={{0,4},{1,5},{2,6},{3,7},{4,0},{5,1},{6,2},{7,3},{8,12},{9,13},{10,... | collective-permute-start | bytes 172040 | tf_op jit(solution)/shard_map/ppermute | solution.py:321
  12.6 0.9 %collective-permute-start.4 = (bf16[1,224,128]{2,1,0:T(8,128)(2,1)S(1)}, bf16[1,224,128]{2,1,0:T(8,128)(2,1)S(1)}, u32[]{:S(2)}, u32[]{:S(2)}) collective-permute-start(bf16[1,224,128]{2,1,0:T(8,128)(2,1)S(1)} %get-tuple-element.42), channel_id=1, source_target_pairs={{0,3},{1,2},{2,1},{3,0},{4,7},{5,6},{6,5},{7,4},{8,11},{9,10},{10,... | collective-permute-start | bytes 172040 | tf_op jit(solution)/shard_map/ppermute | solution.py:321
  13.5 0.9 %collective-permute-start.5 = (bf16[1,224,128]{2,1,0:T(8,128)(2,1)S(1)}, bf16[1,224,128]{2,1,0:T(8,128)(2,1)S(1)}, u32[]{:S(2)}, u32[]{:S(2)}) collective-permute-start(bf16[1,224,128]{2,1,0:T(8,128)(2,1)S(1)} %get-tuple-element.43), channel_id=1, source_target_pairs={{0,2},{1,3},{2,0},{3,1},{4,6},{5,7},{6,4},{7,5},{8,10},{9,11},{10,... | collective-permute-start | bytes 172040 | tf_op jit(solution)/shard_map/ppermute | solution.py:321
  14.4 1.6 %collective-permute-done.1.rest_1_ = bf16[1,224,128]{2,1,0:T(8,128)(2,1)S(1)} collective-permute-done((bf16[1,224,128]{2,1,0:T(8,128)(2,1)S(1)}, bf16[1,224,128]{2,1,0:T(8,128)(2,1)S(1)}, u32[]{:S(2)}, u32[]{:S(2)}) %collective-permute-start.1) | collective-permute-done | bytes 57376 | tf_op jit(solution)/shard_map/ppermute | solution.py:321
  16.0 2.8 %prepare.1 = (bf16[2,8,2,2,2,48,256]{6,5,4,3,2,1,0:T(8,128)(2,1)S(1)}, s32[1,64]{1,0:T(1,128)S(1)}, bf16[256,256]{1,0:T(8,128)(2,1)S(1)}, bf16[256,256]{1,0:T(8,128)(2,1)S(1)}) custom-call(s32[2,16,16]{2,1,0:T(8,128)} %ranks_far.3, bf16[2,8,2,2,2,48,256]{6,5,4,3,2,1,0:T(8,128)(2,1)} %bitcast.4, s32[64,64]{1,0:T(8,128)S(1)} %copy-done.2, ...), custom_call_target="tpu_custom_call" | custom-call | bytes 3145728 | tf_op jit(solution)/shard_map/prepare/pallas_call | solution.py:28
  18.9 1.2 %collective-permute-done.3.rest_3_ = bf16[1,224,128]{2,1,0:T(8,128)(2,1)S(1)} collective-permute-done((bf16[1,224,128]{2,1,0:T(8,128)(2,1)S(1)}, bf16[1,224,128]{2,1,0:T(8,128)(2,1)S(1)}, u32[]{:S(2)}, u32[]{:S(2)}) %collective-permute-start.3) | collective-permute-done | bytes 57376 | tf_op jit(solution)/shard_map/ppermute | solution.py:321
  20.1 1.4 %image.1 = (bf16[2,32,512]{2,1,0:T(8,128)(2,1)S(1)}, bf16[2,32,512]{2,1,0:T(8,128)(2,1)S(1)}, bf16[2,32,512]{2,1,0:T(8,128)(2,1)S(1)}, bf16[2,32,512]{2,1,0:T(8,128)(2,1)S(1)}) custom-call(s32[1,64]{1,0:T(1,128)S(1)} %get-tuple-element.34.ranks_near, bf16[2,8,2,2,2,48,256]{6,5,4,3,2,1,0:T(8,128)(2,1)S(1)} %get-tuple-element.35.basis, ...), custom_call_target="tpu_custom_call" | custom-call | flops 805306368 | bytes 3145728 | tf_op jit(solution)/shard_map/image/pallas_call | solution.py:28
  21.5 2.6 %collective-permute-start.7 = (bf16[2,32,512]{2,1,0:T(8,128)(2,1)S(1)}, bf16[2,32,512]{2,1,0:T(8,128)(2,1)S(1)}, u32[]{:S(2)}, u32[]{:S(2)}) collective-permute-start(bf16[2,32,512]{2,1,0:T(8,128)(2,1)S(1)} %get-tuple-element.45), channel_id=1, source_target_pairs={{0,24},{8,16},{16,8},{24,0},{1,25},{9,17},{17,9},{25,1},{2,26},{10... | collective-permute-start | bytes 196616 | tf_op jit(solution)/shard_map/ppermute | solution.py:321
  24.1 0.4 collective-permute-start.8
  24.6 0.5 collective-permute-start.9
  25.1 1.7 %collective-permute-done.7.rest_0_ = bf16[2,32,512]{2,1,0:T(8,128)(2,1)S(1)} collective-permute-done((bf16[2,32,512]{2,1,0:T(8,128)(2,1)S(1)}, bf16[2,32,512]{2,1,0:T(8,128)(2,1)S(1)}, u32[]{:S(2)}, u32[]{:S(2)}) %collective-permute-start.7) | collective-permute-done | bytes 65568 | tf_op jit(solution)/shard_map/ppermute | solution.py:321
  26.8 1.6 %collective-permute-done.8.rest_1_ = bf16[2,32,512]{2,1,0:T(8,128)(2,1)S(1)} collective-permute-done((bf16[2,32,512]{2,1,0:T(8,128)(2,1)S(1)}, bf16[2,32,512]{2,1,0:T(8,128)(2,1)S(1)}, u32[]{:S(2)}, u32[]{:S(2)}) %collective-permute-start.8) | collective-permute-done | bytes 65568 | tf_op jit(solution)/shard_map/ppermute | solution.py:321
  29.2 1.6 %collective-permute-start.10 = (bf16[2,32,512]{2,1,0:T(8,128)(2,1)S(1)}, bf16[2,32,512]{2,1,0:T(8,128)(2,1)S(1)}, u32[]{:S(2)}, u32[]{:S(2)}) collective-permute-start(bf16[2,32,512]{2,1,0:T(8,128)(2,1)S(1)} %get-tuple-element.49), channel_id=1, source_target_pairs={{0,24},{8,16},{16,8},{24,0},{1,25},{9,17},{17,9},{25,1},{2,26},{10... | collective-permute-start | bytes 196616 | tf_op jit(solution)/shard_map/ppermute | solution.py:321
  30.8 0.6 %collective-permute-start.11 = (bf16[2,32,512]{2,1,0:T(8,128)(2,1)S(1)}, bf16[2,32,512]{2,1,0:T(8,128)(2,1)S(1)}, u32[]{:S(2)}, u32[]{:S(2)}) collective-permute-start(bf16[2,32,512]{2,1,0:T(8,128)(2,1)S(1)} %get-tuple-element.50), channel_id=1, source_target_pairs={{0,16},{8,24},{16,0},{24,8},{1,17},{9,25},{17,1},{25,9},{2,18},{10... | collective-permute-start | bytes 196616 | tf_op jit(solution)/shard_map/ppermute | solution.py:321
  31.4 1.4 %collective-permute-start.12 = (bf16[2,32,512]{2,1,0:T(8,128)(2,1)S(1)}, bf16[2,32,512]{2,1,0:T(8,128)(2,1)S(1)}, u32[]{:S(2)}, u32[]{:S(2)}) collective-permute-start(bf16[2,32,512]{2,1,0:T(8,128)(2,1)S(1)} %get-tuple-element.51), channel_id=1, source_target_pairs={{0,8},{8,0},{16,24},{24,16},{1,9},{9,1},{17,25},{25,17},{2,10},{10... | collective-permute-start | bytes 196616 | tf_op jit(solution)/shard_map/ppermute | solution.py:321
  32.8 1.7 %collective-permute-done.10.rest_0_ = bf16[2,32,512]{2,1,0:T(8,128)(2,1)S(1)} collective-permute-done((bf16[2,32,512]{2,1,0:T(8,128)(2,1)S(1)}, bf16[2,32,512]{2,1,0:T(8,128)(2,1)S(1)}, u32[]{:S(2)}, u32[]{:S(2)}) %collective-permute-start.10) | collective-permute-done | bytes 65568 | tf_op jit(solution)/shard_map/ppermute | solution.py:321
  34.5 0.7 %collective-permute-done.11.rest_1_ = bf16[2,32,512]{2,1,0:T(8,128)(2,1)S(1)} collective-permute-done((bf16[2,32,512]{2,1,0:T(8,128)(2,1)S(1)}, bf16[2,32,512]{2,1,0:T(8,128)(2,1)S(1)}, u32[]{:S(2)}, u32[]{:S(2)}) %collective-permute-start.11) | collective-permute-done | bytes 65568 | tf_op jit(solution)/shard_map/ppermute | solution.py:321
  35.2 0.5 collective-permute-done.12.rest_2_
  35.7 1.6 %forward.1 = (bf16[1,224,128]{2,1,0:T(8,128)(2,1)S(1)}, bf16[1,224,128]{2,1,0:T(8,128)(2,1)S(1)}, bf16[1,224,128]{2,1,0:T(8,128)(2,1)S(1)}, bf16[1,224,128]{2,1,...) custom-call(s32[1,64]{1,0:T(1,128)S(1)} %get-tuple-element.34.ranks_, ...), custom_call_target="tpu_custom_call" | custom-call | flops 805306368 | bytes 3145728 | tf_op jit(solution)/shard_map/forward/pallas_call | solution.py:28
  37.3 2.3 %collective-permute-start.13 = (bf16[1,224,128]{2,1,0:T(8,128)(2,1)S(1)}, bf16[1,224,128]{2,1,0:T(8,128)(2,1)S(1)}, u32[]{:S(2)}, u32[]{:S(2)}) collective-permute-start(bf16[1,224,128]{2,1,0:T(8,128)(2,1)S(1)} %get-tuple-element.53), channel_id=1, source_target_pairs={{0,7},{1,6},{2,5},{3,4},{4,3},{5,2},{6,1},{7,0},{8,15},{9,14},{10,... | collective-permute-start | bytes 172040 | tf_op jit(solution)/shard_map/ppermute | solution.py:321
  39.6 1.7 %collective-permute-start.14 = (bf16[1,224,128]{2,1,0:T(8,128)(2,1)S(1)}, bf16[1,224,128]{2,1,0:T(8,128)(2,1)S(1)}, u32[]{:S(2)}, u32[]{:S(2)}) collective-permute-start(bf16[1,224,128]{2,1,0:T(8,128)(2,1)S(1)} %get-tuple-element.54), channel_id=1, source_target_pairs={{0,6},{1,7},{2,4},{3,5},{4,2},{5,3},{6,0},{7,1},{8,14},{9,15},{10,... | collective-permute-start | bytes 172040 | tf_op jit(solution)/shard_map/ppermute | solution.py:321
  41.3 2.5 %collective-permute-start.16 = (bf16[1,224,128]{2,1,0:T(8,128)(2,1)S(1)}, bf16[1,224,128]{2,1,0:T(8,128)(2,1)S(1)}, u32[]{:S(2)}, u32[]{:S(2)}) collective-permute-start(bf16[1,224,128]{2,1,0:T(8,128)(2,1)S(1)} %get-tuple-element.56), channel_id=1, source_target_pairs={{0,4},{1,5},{2,6},{3,7},{4,0},{5,1},{6,2},{7,3},{8,12},{9,13},{10,... | collective-permute-start | bytes 172040 | tf_op jit(solution)/shard_map/ppermute | solution.py:321
  43.8 0.9 %collective-permute-start.17 = (bf16[1,224,128]{2,1,0:T(8,128)(2,1)S(1)}, bf16[1,224,128]{2,1,0:T(8,128)(2,1)S(1)}, u32[]{:S(2)}, u32[]{:S(2)}) collective-permute-start(bf16[1,224,128]{2,1,0:T(8,128)(2,1)S(1)} %get-tuple-element.57), channel_id=1, source_target_pairs={{0,3},{1,2},{2,1},{3,0},{4,7},{5,6},{6,5},{7,4},{8,11},{9,10},{10,... | collective-permute-start | bytes 172040 | tf_op jit(solution)/shard_map/ppermute | solution.py:321
  44.7 0.9 %collective-permute-start.18 = (bf16[1,224,128]{2,1,0:T(8,128)(2,1)S(1)}, bf16[1,224,128]{2,1,0:T(8,128)(2,1)S(1)}, u32[]{:S(2)}, u32[]{:S(2)}) collective-permute-start(bf16[1,224,128]{2,1,0:T(8,128)(2,1)S(1)} %get-tuple-element.58), channel_id=1, source_target_pairs={{0,2},{1,3},{2,0},{3,1},{4,6},{5,7},{6,4},{7,5},{8,10},{9,11},{10,... | collective-permute-start | bytes 172040 | tf_op jit(solution)/shard_map/ppermute | solution.py:321
  45.6 1.1 %collective-permute-start.19 = (bf16[1,224,128]{2,1,0:T(8,128)(2,1)S(1)}, bf16[1,224,128]{2,1,0:T(8,128)(2,1)S(1)}, u32[]{:S(2)}, u32[]{:S(2)}) collective-permute-start(bf16[1,224,128]{2,1,0:T(8,128)(2,1)S(1)} %get-tuple-element.59), channel_id=1, source_target_pairs={{0,1},{1,0},{2,3},{3,2},{4,5},{5,4},{6,7},{7,6},{8,9},{9,8},{10,11... | collective-permute-start | bytes 172040 | tf_op jit(solution)/shard_map/ppermute | solution.py:321
  46.7 3.2 %collective-permute-done.15.rest_2_ = bf16[1,224,128]{2,1,0:T(8,128)(2,1)S(1)} collective-permute-done((bf16[1,224,128]{2,1,0:T(8,128)(2,1)S(1)}, bf16[1,224,128]{2,1,0:T(8,128)(2,1)S(1)}, u32[]{:S(2)}, u32[]{:S(2)}) %collective-permute-start.15) | collective-permute-done | bytes 57376 | tf_op jit(solution)/shard_map/ppermute | solution.py:321
  49.9 1.3 %collective-permute-done.16.rest_3_ = bf16[1,224,128]{2,1,0:T(8,128)(2,1)S(1)} collective-permute-done((bf16[1,224,128]{2,1,0:T(8,128)(2,1)S(1)}, bf16[1,224,128]{2,1,0:T(8,128)(2,1)S(1)}, u32[]{:S(2)}, u32[]{:S(2)}) %collective-permute-start.16) | collective-permute-done | bytes 57376 | tf_op jit(solution)/shard_map/ppermute | solution.py:321
  51.2 0.5 collective-permute-done.18.rest_5_
  51.7 2.1 %result.1 = bf16[2,512,128]{2,1,0:T(8,128)(2,1)} custom-call(s32[1,64]{1,0:T(1,128)S(1)} %get-tuple-element.34.ranks_near, bf16[2,2,8,2,2,48,256]{6,5,4,3,2,1,0:T(8,128)(2,1)S(1)} %bitcast.3, bf16[1,224,128]{2,1,0:T(8,128)(2,1)S(1)} %collective-permute-done.13.rest_0_, bf16[1,224,128]{2,1,0:T(8,128)(2,1)S(1)} %collective-permute-done.14.rest_1_, ...), custom_call_target="tpu_custom_call" | custom-call | flops 805306368 | bytes 3145728 | tf_op jit(solution)/shard_map/result/pallas_call | solution.py:28
  (24 shorter events, 1.2 us)
Async XLA Ops:
  0.0 16.0 %copy-start.3 = (f32[64,128]{1,0:T(8,128)S(1)}, f32[64,128]{1,0:T(8,128)}, u32[]{:S(2)}) copy-start(f32[64,128]{1,0:T(8,128)} %constant.6.clone.table) | copy-start | bytes 98308
  0.0 16.0 %copy-start.1 = (f32[16,4096]{1,0:T(8,128)S(1)}, f32[16,4096]{1,0:T(8,128)}, u32[]{:S(2)}) copy-start(f32[16,4096]{1,0:T(8,128)} %constant.7.clone.choice) | copy-start | bytes 786436
  0.0 16.0 %copy-start.4 = (f32[16,256]{1,0:T(8,128)S(1)}, f32[16,256]{1,0:T(8,128)}, u32[]{:S(2)}) copy-start(f32[16,256]{1,0:T(8,128)} %constant.8.clone.same) | copy-start | bytes 49156
  0.0 16.0 %copy-start.2 = (s32[64,64]{1,0:T(8,128)S(1)}, s32[64,64]{1,0:T(8,128)}, u32[]{:S(2)}) copy-start(s32[64,64]{1,0:T(8,128)} %mask.1) | copy-start | bytes 49156
  4.8 8.7 %collective-permute-start = (bf16[1,224,128]{2,1,0:T(8,128)(2,1)S(1)}, bf16[1,224,128]{2,1,0:T(8,128)(2,1)S(1)}, u32[]{:S(2)}, u32[]{:S(2)}) collective-permute-start(bf16[1,224,128]{2,1,0:T(8,128)(2,1)S(1)} %get-tuple-element.38), channel_id=1, source_target_pairs={{0,7},{1,6},{2,5},{3,4},{4,3},{5,2},{6,1},{7,0},{8,15},{9,14},{10,... | collective-permute-start | bytes 172040 | tf_op jit(solution)/shard_map/ppermute | solution.py:321
  9.3 6.7 %collective-permute-start.1 = (bf16[1,224,128]{2,1,0:T(8,128)(2,1)S(1)}, bf16[1,224,128]{2,1,0:T(8,128)(2,1)S(1)}, u32[]{:S(2)}, u32[]{:S(2)}) collective-permute-start(bf16[1,224,128]{2,1,0:T(8,128)(2,1)S(1)} %get-tuple-element.39), channel_id=1, source_target_pairs={{0,6},{1,7},{2,4},{3,5},{4,2},{5,3},{6,0},{7,1},{8,14},{9,15},{10,... | collective-permute-start | bytes 172040 | tf_op jit(solution)/shard_map/ppermute | solution.py:321
  10.0 8.9 %collective-permute-start.2 = (bf16[1,224,128]{2,1,0:T(8,128)(2,1)S(1)}, bf16[1,224,128]{2,1,0:T(8,128)(2,1)S(1)}, u32[]{:S(2)}, u32[]{:S(2)}) collective-permute-start(bf16[1,224,128]{2,1,0:T(8,128)(2,1)S(1)} %get-tuple-element.40), channel_id=1, source_target_pairs={{0,5},{1,4},{2,7},{3,6},{4,1},{5,0},{6,3},{7,2},{8,13},{9,12},{10,... | collective-permute-start | bytes 172040 | tf_op jit(solution)/shard_map/ppermute | solution.py:321
  10.3 9.8 %collective-permute-start.3 = (bf16[1,224,128]{2,1,0:T(8,128)(2,1)S(1)}, bf16[1,224,128]{2,1,0:T(8,128)(2,1)S(1)}, u32[]{:S(2)}, u32[]{:S(2)}) collective-permute-start(bf16[1,224,128]{2,1,0:T(8,128)(2,1)S(1)} %get-tuple-element.41), channel_id=1, source_target_pairs={{0,4},{1,5},{2,6},{3,7},{4,0},{5,1},{6,2},{7,3},{8,12},{9,13},{10,... | collective-permute-start | bytes 172040 | tf_op jit(solution)/shard_map/ppermute | solution.py:321
  12.6 7.5 %collective-permute-start.4 = (bf16[1,224,128]{2,1,0:T(8,128)(2,1)S(1)}, bf16[1,224,128]{2,1,0:T(8,128)(2,1)S(1)}, u32[]{:S(2)}, u32[]{:S(2)}) collective-permute-start(bf16[1,224,128]{2,1,0:T(8,128)(2,1)S(1)} %get-tuple-element.42), channel_id=1, source_target_pairs={{0,3},{1,2},{2,1},{3,0},{4,7},{5,6},{6,5},{7,4},{8,11},{9,10},{10,... | collective-permute-start | bytes 172040 | tf_op jit(solution)/shard_map/ppermute | solution.py:321
  13.5 6.6 %collective-permute-start.5 = (bf16[1,224,128]{2,1,0:T(8,128)(2,1)S(1)}, bf16[1,224,128]{2,1,0:T(8,128)(2,1)S(1)}, u32[]{:S(2)}, u32[]{:S(2)}) collective-permute-start(bf16[1,224,128]{2,1,0:T(8,128)(2,1)S(1)} %get-tuple-element.43), channel_id=1, source_target_pairs={{0,2},{1,3},{2,0},{3,1},{4,6},{5,7},{6,4},{7,5},{8,10},{9,11},{10,... | collective-permute-start | bytes 172040 | tf_op jit(solution)/shard_map/ppermute | solution.py:321
  16.0 4.1 %collective-permute-start.6 = (bf16[1,224,128]{2,1,0:T(8,128)(2,1)S(1)}, bf16[1,224,128]{2,1,0:T(8,128)(2,1)S(1)}, u32[]{:S(2)}, u32[]{:S(2)}) collective-permute-start(bf16[1,224,128]{2,1,0:T(8,128)(2,1)S(1)} %get-tuple-element.44), channel_id=1, source_target_pairs={{0,1},{1,0},{2,3},{3,2},{4,5},{5,4},{6,7},{7,6},{8,9},{9,8},{10,11... | collective-permute-start | bytes 172040 | tf_op jit(solution)/shard_map/ppermute | solution.py:321
  20.1 31.6 %copy-start = (bf16[2,2,16,2,48,256]{5,4,3,2,1,0:T(8,128)(2,1)S(1)}, bf16[2,2,16,2,48,256]{5,4,3,2,1,0:T(8,128)(2,1)}, u32[]{:S(2)}) copy-start(bf16[2,2,16,2,48,256]{5,4,3,2,1,0:T(8,128)(2,1)} %param.9) | copy-start | bytes 9437188
  21.5 5.3 %collective-permute-start.7 = (bf16[2,32,512]{2,1,0:T(8,128)(2,1)S(1)}, bf16[2,32,512]{2,1,0:T(8,128)(2,1)S(1)}, u32[]{:S(2)}, u32[]{:S(2)}) collective-permute-start(bf16[2,32,512]{2,1,0:T(8,128)(2,1)S(1)} %get-tuple-element.45), channel_id=1, source_target_pairs={{0,24},{8,16},{16,8},{24,0},{1,25},{9,17},{17,9},{25,1},{2,26},{10... | collective-permute-start | bytes 196616 | tf_op jit(solution)/shard_map/ppermute | solution.py:321
  24.1 4.3 %collective-permute-start.8 = (bf16[2,32,512]{2,1,0:T(8,128)(2,1)S(1)}, bf16[2,32,512]{2,1,0:T(8,128)(2,1)S(1)}, u32[]{:S(2)}, u32[]{:S(2)}) collective-permute-start(bf16[2,32,512]{2,1,0:T(8,128)(2,1)S(1)} %get-tuple-element.46), channel_id=1, source_target_pairs={{0,16},{8,24},{16,0},{24,8},{1,17},{9,25},{17,1},{25,9},{2,18},{10... | collective-permute-start | bytes 196616 | tf_op jit(solution)/shard_map/ppermute | solution.py:321
  24.6 4.3 %collective-permute-start.9 = (bf16[2,32,512]{2,1,0:T(8,128)(2,1)S(1)}, bf16[2,32,512]{2,1,0:T(8,128)(2,1)S(1)}, u32[]{:S(2)}, u32[]{:S(2)}) collective-permute-start(bf16[2,32,512]{2,1,0:T(8,128)(2,1)S(1)} %get-tuple-element.47), channel_id=1, source_target_pairs={{0,8},{8,0},{16,24},{24,16},{1,9},{9,1},{17,25},{25,17},{2,10},{10... | collective-permute-start | bytes 196616 | tf_op jit(solution)/shard_map/ppermute | solution.py:321
  29.2 5.2 %collective-permute-start.10 = (bf16[2,32,512]{2,1,0:T(8,128)(2,1)S(1)}, bf16[2,32,512]{2,1,0:T(8,128)(2,1)S(1)}, u32[]{:S(2)}, u32[]{:S(2)}) collective-permute-start(bf16[2,32,512]{2,1,0:T(8,128)(2,1)S(1)} %get-tuple-element.49), channel_id=1, source_target_pairs={{0,24},{8,16},{16,8},{24,0},{1,25},{9,17},{17,9},{25,1},{2,26},{10... | collective-permute-start | bytes 196616 | tf_op jit(solution)/shard_map/ppermute | solution.py:321
  30.8 4.4 %collective-permute-start.11 = (bf16[2,32,512]{2,1,0:T(8,128)(2,1)S(1)}, bf16[2,32,512]{2,1,0:T(8,128)(2,1)S(1)}, u32[]{:S(2)}, u32[]{:S(2)}) collective-permute-start(bf16[2,32,512]{2,1,0:T(8,128)(2,1)S(1)} %get-tuple-element.50), channel_id=1, source_target_pairs={{0,16},{8,24},{16,0},{24,8},{1,17},{9,25},{17,1},{25,9},{2,18},{10... | collective-permute-start | bytes 196616 | tf_op jit(solution)/shard_map/ppermute | solution.py:321
  31.4 4.3 %collective-permute-start.12 = (bf16[2,32,512]{2,1,0:T(8,128)(2,1)S(1)}, bf16[2,32,512]{2,1,0:T(8,128)(2,1)S(1)}, u32[]{:S(2)}, u32[]{:S(2)}) collective-permute-start(bf16[2,32,512]{2,1,0:T(8,128)(2,1)S(1)} %get-tuple-element.51), channel_id=1, source_target_pairs={{0,8},{8,0},{16,24},{24,16},{1,9},{9,1},{17,25},{25,17},{2,10},{10... | collective-permute-start | bytes 196616 | tf_op jit(solution)/shard_map/ppermute | solution.py:321
  37.3 7.5 %collective-permute-start.13 = (bf16[1,224,128]{2,1,0:T(8,128)(2,1)S(1)}, bf16[1,224,128]{2,1,0:T(8,128)(2,1)S(1)}, u32[]{:S(2)}, u32[]{:S(2)}) collective-permute-start(bf16[1,224,128]{2,1,0:T(8,128)(2,1)S(1)} %get-tuple-element.53), channel_id=1, source_target_pairs={{0,7},{1,6},{2,5},{3,4},{4,3},{5,2},{6,1},{7,0},{8,15},{9,14},{10,... | collective-permute-start | bytes 172040 | tf_op jit(solution)/shard_map/ppermute | solution.py:321
  39.6 6.1 %collective-permute-start.14 = (bf16[1,224,128]{2,1,0:T(8,128)(2,1)S(1)}, bf16[1,224,128]{2,1,0:T(8,128)(2,1)S(1)}, u32[]{:S(2)}, u32[]{:S(2)}) collective-permute-start(bf16[1,224,128]{2,1,0:T(8,128)(2,1)S(1)} %get-tuple-element.54), channel_id=1, source_target_pairs={{0,6},{1,7},{2,4},{3,5},{4,2},{5,3},{6,0},{7,1},{8,14},{9,15},{10,... | collective-permute-start | bytes 172040 | tf_op jit(solution)/shard_map/ppermute | solution.py:321
  41.2 8.7 %collective-permute-start.15 = (bf16[1,224,128]{2,1,0:T(8,128)(2,1)S(1)}, bf16[1,224,128]{2,1,0:T(8,128)(2,1)S(1)}, u32[]{:S(2)}, u32[]{:S(2)}) collective-permute-start(bf16[1,224,128]{2,1,0:T(8,128)(2,1)S(1)} %get-tuple-element.55), channel_id=1, source_target_pairs={{0,5},{1,4},{2,7},{3,6},{4,1},{5,0},{6,3},{7,2},{8,13},{9,12},{10,... | collective-permute-start | bytes 172040 | tf_op jit(solution)/shard_map/ppermute | solution.py:321
  41.3 9.9 %collective-permute-start.16 = (bf16[1,224,128]{2,1,0:T(8,128)(2,1)S(1)}, bf16[1,224,128]{2,1,0:T(8,128)(2,1)S(1)}, u32[]{:S(2)}, u32[]{:S(2)}) collective-permute-start(bf16[1,224,128]{2,1,0:T(8,128)(2,1)S(1)} %get-tuple-element.56), channel_id=1, source_target_pairs={{0,4},{1,5},{2,6},{3,7},{4,0},{5,1},{6,2},{7,3},{8,12},{9,13},{10,... | collective-permute-start | bytes 172040 | tf_op jit(solution)/shard_map/ppermute | solution.py:321
  43.8 7.4 %collective-permute-start.17 = (bf16[1,224,128]{2,1,0:T(8,128)(2,1)S(1)}, bf16[1,224,128]{2,1,0:T(8,128)(2,1)S(1)}, u32[]{:S(2)}, u32[]{:S(2)}) collective-permute-start(bf16[1,224,128]{2,1,0:T(8,128)(2,1)S(1)} %get-tuple-element.57), channel_id=1, source_target_pairs={{0,3},{1,2},{2,1},{3,0},{4,7},{5,6},{6,5},{7,4},{8,11},{9,10},{10,... | collective-permute-start | bytes 172040 | tf_op jit(solution)/shard_map/ppermute | solution.py:321
  44.7 6.9 %collective-permute-start.18 = (bf16[1,224,128]{2,1,0:T(8,128)(2,1)S(1)}, bf16[1,224,128]{2,1,0:T(8,128)(2,1)S(1)}, u32[]{:S(2)}, u32[]{:S(2)}) collective-permute-start(bf16[1,224,128]{2,1,0:T(8,128)(2,1)S(1)} %get-tuple-element.58), channel_id=1, source_target_pairs={{0,2},{1,3},{2,0},{3,1},{4,6},{5,7},{6,4},{7,5},{8,10},{9,11},{10,... | collective-permute-start | bytes 172040 | tf_op jit(solution)/shard_map/ppermute | solution.py:321
  45.6 6.1 %collective-permute-start.19 = (bf16[1,224,128]{2,1,0:T(8,128)(2,1)S(1)}, bf16[1,224,128]{2,1,0:T(8,128)(2,1)S(1)}, u32[]{:S(2)}, u32[]{:S(2)}) collective-permute-start(bf16[1,224,128]{2,1,0:T(8,128)(2,1)S(1)} %get-tuple-element.59), channel_id=1, source_target_pairs={{0,1},{1,0},{2,3},{3,2},{4,5},{5,4},{6,7},{7,6},{8,9},{9,8},{10,11... | collective-permute-start | bytes 172040 | tf_op jit(solution)/shard_map/ppermute | solution.py:321

commit v5 on v3

--- a/solution.py
+++ b/solution.py
@@ -97,66 +97,88 @@
     return jnp.concatenate([lead[:half] - trail[half:], lead[half:] + trail[:half]], axis=0)
 
 
-def unstage(outs, stage, m, span, size, me):
-    for s in range(len(outs)):
+def split_blocks(devices):
+    part = devices // 4
+    return [[(3 * part, part)], [(2 * part, part), (0, 2 * part)]]
+
+
+def block_base(me, block):
+    first, size = block
+    return (me ^ first) & ~(size - 1)
+
+
+def unstage(outs, stage, m, slots, span, size, places):
+    for out, place in zip(outs, places):
         for c in range(span):
-            block = stage[(m * len(outs) + (me ^ s)) * span + c, pl.ds(0, size), :]
-            outs[s][m, pl.ds(c * size, size), :] = block.astype(bf16)
-
-
-def adjoint_kernel(devices, parts, ranks_far, u_far, basis_far, *rest):
-    outs = rest[:devices]
-    ranks, u_ref, basis, turned, stage, sems = rest[devices:]
+            rows = stage[(m * slots + place) * span + c, pl.ds(0, size), :]
+            out[m, pl.ds(c * size, size), :] = rows.astype(bf16)
+
+
+def adjoint_kernel(blocks, turn, ranks_far, basis_far, u_far, *rest):
+    partners = sum(size for _, size in blocks)
+    ranks, u_ref, basis, stage, sems = rest[-5:]
+    outs = rest[-5 - partners - turn : -5 - turn]
+    turned = rest[-6] if turn else u_far
     freqs, rows, _, cols, _, slots, tile = basis_far.shape
     total = slots + slots // 6
-    half = u_ref.shape[2] // 2
-    per = devices // parts
+    half = turned.shape[3] // 2
     me = lax.axis_index("tile")
     rank_copy = pltpu.make_async_copy(ranks_far, ranks, sems.at[0])
-    data_copy = pltpu.make_async_copy(u_far, u_ref, sems.at[1])
-    data_copy.start()
+    if turn:
+        data_copy = pltpu.make_async_copy(u_far, u_ref, sems.at[1])
+        data_copy.start()
     rank_copy.start()
-    copies = {}
+    copies = [[] for _ in range(rows)]
+    at = 0
+    for b, block in enumerate(blocks):
+        for i in range(rows):
+            for f in range(freqs):
+                copy = pltpu.make_async_copy(
+                    basis_far.at[f, i, pl.ds(block_base(me, block), block[1])],
+                    basis.at[f, i, pl.ds(at, block[1])],
+                    sems.at[2 + (b * rows + i) * freqs + f],
+                )
+                copy.start(priority=f % 2)
+                copies[i].append(copy)
+        at += block[1]
+    if turn:
+        data_copy.wait()
+        for f in range(freqs):
+            for i in range(rows):
+                values = u_ref[f, i * tile : (i + 1) * tile, :]
+                wide = values.astype(f32)
+                lane = lax.broadcasted_iota(jnp.int32, wide.shape, 1)
+                rolled = pltpu.roll(wide, half, 1)
+                turned[f, i, :tile, :] = values
+                turned[f, i, tile:, :] = jnp.where(lane < half, rolled, -rolled).astype(bf16)
+    rank_copy.wait()
     for i in range(rows):
-        for p in range(parts):
-            for f in range(freqs):
-                at = pl.ds(p * per, per)
-                copies[f, i, p] = pltpu.make_async_copy(
-                    basis_far.at[f, i, at], basis.at[f, i, at], sems.at[2 + (f * rows + i) * parts + p]
-                )
-                copies[f, i, p].start()
-    data_copy.wait()
-    for f in range(freqs):
-        values = u_ref[f].astype(f32)
-        lane = lax.broadcasted_iota(jnp.int32, values.shape, 1)
-        rolled = pltpu.roll(values, half, 1)
-        turned[f] = jnp.where(lane < half, rolled, -rolled).astype(bf16)
-    waited = False
-    for m in range(freqs // 2):
-        for i in range(rows):
-            here = pl.ds(i * tile, tile)
-            for p in range(parts):
-                pair = []
-                at = pl.ds(p * per, per)
-                for f in (2 * m, 2 * m + 1):
-                    copies[f, i, p].wait()
-                    both = side_by_side(basis[f, i, at, :, 0], basis[f, i, at, :, 1])
-                    data = jnp.concatenate([u_ref[f, here, :], turned[f, here, :]], axis=0)
-                    pair.append(dot(both, data, 1, 0))
-                if not waited:
-                    rank_copy.wait()
-                    waited = True
-                for n in range(per * cols):
-                    col = p * per * cols + n
-                    rank = ranks[2 * m, me * rows + i, col]
-                    cut = slice(n * slots, (n + 1) * slots)
-                    pack_rows(stage, m * devices * cols + col, i * total, rank, pair[0][cut], pair[1][cut])
-        unstage(outs, stage, m, cols, rows * total, me)
-
-
-def image_kernel(devices, owners, ranks_near, basis, *rest):
-    packed = rest[:devices][::-1]
-    outs = rest[-owners - 5 : -5]
+        for copy in copies[i]:
+            copy.wait()
+        for m in range(freqs // 2):
+            pair = []
+            for f in (2 * m, 2 * m + 1):
+                both = side_by_side(basis[f, i, :, :, 0], basis[f, i, :, :, 1])
+                pair.append(dot(both, turned[f, i], 1, 0))
+            at = 0
+            for block in blocks:
+                for n in range(block[1] * cols):
+                    rank = ranks[2 * m, me * rows + i, block_base(me, block) * cols + n]
+                    cut = slice((at * cols + n) * slots, (at * cols + n + 1) * slots)
+                    slot = (m * partners + at) * cols + n
+                    pack_rows(stage, slot, i * total, rank, pair[0][cut], pair[1][cut])
+                at += block[1]
+    at = 0
+    for first, size in blocks:
+        places = [at + ((me ^ (first + n)) & (size - 1)) for n in range(size)]
+        for m in range(freqs // 2):
+            unstage(outs[at : at + size], stage, m, partners, cols, rows * total, places)
+        at += size
+
+
+def image_kernel(blocks, owners, first, last, ranks_near, basis, *rest):
+    partners = sum(size for _, size in blocks)
+    packed, rest = rest[:partners], rest[partners:]
     ranks, stage, coeffs, z, sem = rest[-5:]
     freqs, _, rows, cols, _, slots, tile = basis.shape
     total = slots + slots // 6
@@ -166,41 +188,56 @@
     me, mine = lax.axis_index("tile"), lax.axis_index("freq")
     rank_copy = pltpu.make_async_copy(ranks_near, ranks, sem)
     rank_copy.start()
-    for m in range(freqs // 2):
-        for s in range(devices):
+    order = [start + n for start, count in blocks for n in reversed(range(count))]
+    for m in range(freqs // 2):
+        for n in range(partners):
             for c in range(cols):
-                block = packed[s][m, pl.ds(c * size, size), :]
-                stage[(m * devices + s) * cols + c, pl.ds(0, size), :] = block.astype(f32)
+                rows_in = packed[n][m, pl.ds(c * size, size), :]
+                stage[(m * partners + n) * cols + c, pl.ds(0, size), :] = rows_in.astype(f32)
     rank_copy.wait()
     for m in range(freqs // 2):
         for c in range(cols):
-            for s in range(devices):
-                for i in range(rows):
-                    row = (me ^ s) * rows + i
-                    rank = ranks[0, (m * devices * rows + row) * cols + c]
-                    slot = (m * devices + s) * cols + c
-                    unpack_rows(stage, slot, i * total, rank, total, coeffs.at[c], row * slots)
+            at = 0
+            for start, count in blocks:
+                for n in range(at, at + count):
+                    partner = me ^ order[n]
+                    for i in range(rows):
+                        rank = ranks[0, (m * basis.shape[1] * rows + partner * rows + i) * cols + c]
+                        slot = (m * partners + n) * cols + c
+                        place = ((at + (partner & (count - 1))) * rows + i) * slots
+                        unpack_rows(stage, slot, i * total, rank, total, coeffs.at[c], place)
+                at += count
             for n in range(2):
                 f = 2 * m + n
-                both = side_by_side(basis[f, :, :, c, 0], basis[f, :, :, c, 1])
-                z[f, :, pl.ds(c * tile, tile)] = plain_product(coeffs[c, n], both)
-    for r in range(owners):
-        low = pl.multiple_of((mine ^ r) * quarter, quarter)
-        for f in range(freqs):
-            real = z[f, pl.ds(low, quarter), :]
-            imag = z[f, pl.ds(half + low, quarter), :]
-            outs[r][f] = jnp.concatenate([real, imag], axis=0).astype(bf16)
-
-
-def prepare_kernel(ranks_far, basis_far, mask, table, choice, same, *rest):
-    basis, short, high, low, ranks, full, sems = rest[-7:]
-    freqs, devices, rows, cols = basis_far.shape[:4]
-    row_tiles, col_tiles = ranks.shape[1:]
+                part = None if first else rest[0][f, :, pl.ds(c * tile, tile)]
+                at = 0
+                for block in blocks:
+                    here = pl.ds(block_base(me, block), block[1])
+                    both = side_by_side(basis[f, here, :, c, 0], basis[f, here, :, c, 1])
+                    rows_at = slice(at * rows * slots, (at + block[1]) * rows * slots)
+                    term = plain_product(coeffs[c, n, rows_at], both)
+                    part = term if part is None else part + term
+                    at += block[1]
+                if last:
+                    z[f, :, pl.ds(c * tile, tile)] = part
+                else:
+                    rest[-6][f, :, pl.ds(c * tile, tile)] = part
+    if last:
+        outs = rest[-5 - owners : -5]
+        for r in range(owners):
+            low = pl.multiple_of((mine ^ r) * quarter, quarter)
+            for f in range(freqs):
+                real = z[f, pl.ds(low, quarter), :]
+                imag = z[f, pl.ds(half + low, quarter), :]
+                outs[r][f] = jnp.concatenate([real, imag], axis=0).astype(bf16)
+
+
+def prepare_kernel(rows, cols, ranks_far, mask, table, choice, same, *rest):
+    short, high, low, ranks, full, sem = rest[-6:]
+    freqs, row_tiles, col_tiles = ranks.shape
     me = lax.axis_index("tile")
-    basis_copy = pltpu.make_async_copy(basis_far, basis, sems.at[0])
-    rank_copy = pltpu.make_async_copy(ranks_far, ranks, sems.at[1])
+    rank_copy = pltpu.make_async_copy(ranks_far, ranks, sem)
     rank_copy.start()
-    basis_copy.start()
     exact = lax.Precision.HIGHEST
     full[...] = dot(mask[...].astype(f32), table[...], 0, 0, exact)
     quarter, side = same.shape
@@ -223,7 +260,6 @@
             for col in range(col_tiles):
                 short[0, at] = ranks[2 * m, me * rows + i, col]
                 at += 1
-    basis_copy.wait()
 
 
 def mix_kernel(owners, high, low, *rest):
@@ -275,7 +311,7 @@
                     cut = slice((d * rows + i) * slots, (d * rows + i + 1) * slots)
                     slot = (m * devices + d) * cols + c
                     pack_rows(stage, slot, i * total, rank, pair[0][cut], pair[1][cut])
-        unstage(outs, stage, m, cols, rows * total, me)
+        unstage(outs, stage, m, devices, cols, rows * total, [me ^ n for n in range(devices)])
 
 
 def result_kernel(devices, ranks_near, basis, *rest):
@@ -315,8 +351,8 @@
     return lax.ppermute(value, axis, [(d, d ^ s) for d in range(lax.axis_size(axis))])
 
 
-def spread(values, axis):
-    return [(whole, send(values[s], axis, s)) for s in reversed(range(len(values)))]
+def spread(values, axis, first=0):
+    return [(whole, send(values[s], axis, first + s)) for s in reversed(range(len(values)))]
 
 
 def local(u_data, u_basis, v_basis, ranks, time_mask):
@@ -343,47 +379,67 @@
 
     table = lag_tables(count, time_mask.shape[0], 128)
     choice, same = lag_choice(count, quarter)
-    parts = math.gcd(devices, 2)
-    packed = call(
-        functools.partial(adjoint_kernel, devices, parts),
-        "adjoint",
-        [(far, hold(x)) for x in (ranks, u_data, by_cols)],
-        per_device,
-        [
-            pltpu.SMEM(ranks.shape, jnp.int32),
-            pltpu.VMEM((freqs, row_count, width), bf16),
-            pltpu.VMEM(by_cols.shape, bf16),
-            pltpu.VMEM((freqs, row_count, width), bf16),
-            stage,
-            one((2 + freqs * rows * parts,)),
-        ],
-        **work,
-    )
-    near, short, *window = call(
-        prepare_kernel,
+    def share(partners):
+        return {name: value * partners // devices for name, value in work.items()}
+
+    def stage_for(partners):
+        return pltpu.VMEM((pairs * partners * cols, stage_rows, width), f32)
+
+    calls = split_blocks(devices)
+    data, after, packed = (far, hold(u_data)), [], {}
+    for k, blocks in enumerate(calls):
+        turn = int(k == 0)
+        partners = sum(size for _, size in blocks)
+        made = call(
+            functools.partial(adjoint_kernel, blocks, turn),
+            "adjoint",
+            [(far, hold(ranks)), (far, hold(by_cols)), data] + after,
+            [((pairs, cols * rows * total, width), bf16)] * partners
+            + [((freqs, rows, 2 * tile, width), bf16)] * turn,
+            [
+                pltpu.SMEM(ranks.shape, jnp.int32),
+                pltpu.VMEM((freqs, row_count, width), bf16),
+                pltpu.VMEM((freqs, rows, partners, cols, 2, slots, tile), bf16),
+                stage_for(partners),
+                one((2 + freqs * rows * len(blocks),)),
+            ],
+            **share(partners),
+        )
+        if turn:
+            data = (whole, made[-1])
+        for block in blocks:
+            packed[block], made = made[: block[1]], made[block[1] :]
+    short, *window = call(
+        functools.partial(prepare_kernel, rows, cols),
         "prepare",
-        [(far, hold(ranks)), (far, hold(by_rows))]
+        [(far, hold(ranks))]
         + [(whole, jnp.asarray(x)) for x in (time_mask, table, choice, same)]
-        + [(anywhere, packed[0])],
-        [(by_rows.shape, bf16), ((1, count_short), jnp.int32)] + [((side, side), bf16)] * 2,
-        [pltpu.SMEM(ranks.shape, jnp.int32), pltpu.VMEM((width // 2, 128), f32), one((2,))],
-        specs=[whole, scalars, whole, whole],
-        moved=u_basis.size * 2,
-    )
-    images = call(
-        functools.partial(image_kernel, devices, owners),
-        "image",
-        [(whole, short), (whole, near)] + spread(packed, "tile"),
-        per_owner,
-        [
-            ranks_here,
-            stage,
-            pltpu.VMEM((cols, 2, row_tiles * slots, width), bf16),
-            pltpu.VMEM((freqs, width, cols * tile), f32),
-            one,
-        ],
-        **work,
-    )
+        + [(anywhere, packed[calls[-1][-1]][0])],
+        [((1, count_short), jnp.int32)] + [((side, side), bf16)] * 2,
+        [pltpu.SMEM(ranks.shape, jnp.int32), pltpu.VMEM((width // 2, 128), f32), one],
+        specs=[scalars, whole, whole],
+        flops=6 * quarter * 2 * count * 2 * count * side,
+    )
+    images = []
+    for k, blocks in enumerate(calls):
+        first, last = k == 0, k == len(calls) - 1
+        partners = sum(size for _, size in blocks)
+        images = call(
+            functools.partial(image_kernel, blocks, owners, first, last),
+            "image",
+            [(whole, short), (whole, by_rows)]
+            + [x for block in blocks for x in spread(packed[block], "tile", block[0])]
+            + [(whole, x) for x in images],
+            per_owner if last else [((freqs, width, cols * tile), f32)],
+            [
+                ranks_here,
+                stage_for(partners),
+                pltpu.VMEM((cols, 2, partners * rows * slots, width), bf16),
+                pltpu.VMEM((freqs, width, cols * tile), f32),
+                one,
+            ],
+            **share(partners),
+        )
     mixed = call(
         functools.partial(mix_kernel, owners),
         "mix",
@@ -395,7 +451,7 @@
     packed = call(
         functools.partial(forward_kernel, devices, owners),
         "forward",
-        [(whole, short), (whole, near)] + spread(mixed, "freq"),
+        [(whole, short), (whole, by_rows)] + spread(mixed, "freq"),
         per_device,
         [ranks_here, pltpu.VMEM((freqs, cols, width, 2 * tile), bf16), stage, one],
         **work,

time: 53.4 us -> 53.3 us (level)
    pallas_call x6 -> x8, Pallas kernels: 12.6 us -> 12.5 us  [call(): pl.pallas_call(kernel, in_specs=[spec for spec, _ in ins], out_specs=spec...]
  transfers between devices with their start and end apart: 20 -> 20, of which waited for: 11 -> 11; matrix products, arithmetic and copies ran while one was open for 0% -> 0% of each run, Pallas kernels for 6% -> 10%
where the time goes in v5:
time: 53.3 us; the launch traced here: 53 us
  starting transfers between devices  26.2 us (49%)
  waiting for transfers between devices  14.2 us (27%)
  Pallas kernels  12.5 us (23%)
    ppermute x20, starting transfers between devices, send(): lax.ppermute(value, axis, [(d, d ^ s) for d in range(lax.axis_size(axis))])  26.2 us
    ppermute x20, waiting for transfers between devices, send(): lax.ppermute(value, axis, [(d, d ^ s) for d in range(lax.axis_size(axis))])  14.2 us
    pallas_call x8, Pallas kernels, call(): pl.pallas_call(kernel, in_specs=[spec for spec, _ in ins], out_specs=spec...  12.5 us
  transfers between devices with their start and end apart: 20, of which 11 were waited for; matrix products, arithmetic and copies ran while one was open for 0% of the time, Pallas kernels for 10%

profile of v5, /device:TPU:0, one launch (start us, length us, event | category | flops | bytes accessed | tf_op | source)
XLA Modules:
  0.0 53.0 jit_solution(6974955742846303016)
XLA Ops:
  0.0 1.9 %adjoint.2 = (bf16[1,224,128]{2,1,0:T(8,128)(2,1)S(1)}, bf16[1,224,128]{2,1,0:T(8,128)(2,1)S(1)}, bf16[2,2,512,128]{3,2,1,0:T(8,128)(2,1)S(1)}) custom-call(s32[2,16,16]{2,1,0:T(8,128)} %ranks_far.5, bf16[2,2,8,2,2,48,256]{6,5,4,3,2,1,0:T(8,128)(2,1)} %bitcast.5, bf16[2,512,128]{2,1,0:T(8,128)(2,1)} %u_far.1), custom_call_target="tpu_custom_call" | custom-call | flops 201326592 | bytes 786432 | tf_op jit(solution)/shard_map/adjoint/pallas_call | solution.py:28
  1.9 4.6 %collective-permute-start.5 = (bf16[1,224,128]{2,1,0:T(8,128)(2,1)S(1)}, bf16[1,224,128]{2,1,0:T(8,128)(2,1)S(1)}, u32[]{:S(2)}, u32[]{:S(2)}) collective-permute-start(bf16[1,224,128]{2,1,0:T(8,128)(2,1)S(1)} %get-tuple-element.43), channel_id=1, source_target_pairs={{0,7},{1,6},{2,5},{3,4},{4,3},{5,2},{6,1},{7,0},{8,15},{9,14},{10,... | collective-permute-start | bytes 172040 | tf_op jit(solution)/shard_map/ppermute | solution.py:351
  6.5 0.6 %collective-permute-start.6 = (bf16[1,224,128]{2,1,0:T(8,128)(2,1)S(1)}, bf16[1,224,128]{2,1,0:T(8,128)(2,1)S(1)}, u32[]{:S(2)}, u32[]{:S(2)}) collective-permute-start(bf16[1,224,128]{2,1,0:T(8,128)(2,1)S(1)} %get-tuple-element.44), channel_id=1, source_target_pairs={{0,6},{1,7},{2,4},{3,5},{4,2},{5,3},{6,0},{7,1},{8,14},{9,15},{10,... | collective-permute-start | bytes 172040 | tf_op jit(solution)/shard_map/ppermute | solution.py:351
  7.2 2.7 %adjoint.3 = (bf16[1,224,128]{2,1,0:T(8,128)(2,1)S(1)}, bf16[1,224,128]{2,1,0:T(8,128)(2,1)S(1)}, bf16[1,224,128]{2,1,0:T(8,128)(2,1)S(1)}, bf16[1,224,128]{2,1,...) custom-call(s32[2,16,16]{2,1,0:T(8,128)} %ranks_far.5, ...), custom_call_target="tpu_custom_call" | custom-call | flops 603979776 | bytes 2359296 | tf_op jit(solution)/shard_map/adjoint/pallas_call | solution.py:28
  10.3 2.2 %collective-permute-start.1 = (bf16[1,224,128]{2,1,0:T(8,128)(2,1)S(1)}, bf16[1,224,128]{2,1,0:T(8,128)(2,1)S(1)}, u32[]{:S(2)}, u32[]{:S(2)}) collective-permute-start(bf16[1,224,128]{2,1,0:T(8,128)(2,1)S(1)} %get-tuple-element.39), channel_id=1, source_target_pairs={{0,4},{1,5},{2,6},{3,7},{4,0},{5,1},{6,2},{7,3},{8,12},{9,13},{10,... | collective-permute-start | bytes 172040 | tf_op jit(solution)/shard_map/ppermute | solution.py:351
  12.5 1.0 %collective-permute-start.2 = (bf16[1,224,128]{2,1,0:T(8,128)(2,1)S(1)}, bf16[1,224,128]{2,1,0:T(8,128)(2,1)S(1)}, u32[]{:S(2)}, u32[]{:S(2)}) collective-permute-start(bf16[1,224,128]{2,1,0:T(8,128)(2,1)S(1)} %get-tuple-element.40), channel_id=1, source_target_pairs={{0,3},{1,2},{2,1},{3,0},{4,7},{5,6},{6,5},{7,4},{8,11},{9,10},{10,... | collective-permute-start | bytes 172040 | tf_op jit(solution)/shard_map/ppermute | solution.py:351
  13.5 0.8 %collective-permute-start.3 = (bf16[1,224,128]{2,1,0:T(8,128)(2,1)S(1)}, bf16[1,224,128]{2,1,0:T(8,128)(2,1)S(1)}, u32[]{:S(2)}, u32[]{:S(2)}) collective-permute-start(bf16[1,224,128]{2,1,0:T(8,128)(2,1)S(1)} %get-tuple-element.41), channel_id=1, source_target_pairs={{0,2},{1,3},{2,0},{3,1},{4,6},{5,7},{6,4},{7,5},{8,10},{9,11},{10,... | collective-permute-start | bytes 172040 | tf_op jit(solution)/shard_map/ppermute | solution.py:351
  14.4 1.6 %prepare.1 = (s32[1,64]{1,0:T(1,128)S(1)}, bf16[256,256]{1,0:T(8,128)(2,1)S(1)}, bf16[256,256]{1,0:T(8,128)(2,1)S(1)}) custom-call(s32[2,16,16]{2,1,0:T(8,128)} %ranks_far.5, s32[64,64]{1,0:T(8,128)S(1)} %copy-done.3, f32[64,128]{1,0:T(8,128)S(1)} %copy-done.4, f32[16,4096]{1,0:T(8,128)S(1)} %copy-done.2, f32[16,256]{1,0:T(8,128)S(1)} %copy-done.5, ...), custom_call_target="tpu_custom_call" | custom-call | flops 6291456 | tf_op jit(solution)/shard_map/prepare/pallas_call | solution.py:28
  16.0 0.9 %image.2.rest_6_ = f32[2,128,512]{2,1,0:T(8,128)S(1)} custom-call(s32[1,64]{1,0:T(1,128)S(1)} %get-tuple-element.35.ranks_near, bf16[2,8,2,2,2,48,256]{6,5,4,3,2,1,0:T(8,128)(2,1)S(1)} %bitcast.2, bf16[1,224,128]{2,1,0:T(8,128)(2,1)S(1)} %collective-permute-done.5.rest_0_, bf16[1,224,128]{2,1,0:T(8,128)(2,1)S(1)} %collective-permute-done.6.rest_1_), custom_call_target="tpu_custom_call" | custom-call | flops 201326592 | bytes 786432 | tf_op jit(solution)/shard_map/image/pallas_call | solution.py:28
  16.9 1.8 %collective-permute-done.1.rest_1_ = bf16[1,224,128]{2,1,0:T(8,128)(2,1)S(1)} collective-permute-done((bf16[1,224,128]{2,1,0:T(8,128)(2,1)S(1)}, bf16[1,224,128]{2,1,0:T(8,128)(2,1)S(1)}, u32[]{:S(2)}, u32[]{:S(2)}) %collective-permute-start.1) | collective-permute-done | bytes 57376 | tf_op jit(solution)/shard_map/ppermute | solution.py:351
  18.8 1.0 %collective-permute-done.3.rest_3_ = bf16[1,224,128]{2,1,0:T(8,128)(2,1)S(1)} collective-permute-done((bf16[1,224,128]{2,1,0:T(8,128)(2,1)S(1)}, bf16[1,224,128]{2,1,0:T(8,128)(2,1)S(1)}, u32[]{:S(2)}, u32[]{:S(2)}) %collective-permute-start.3) | collective-permute-done | bytes 57376 | tf_op jit(solution)/shard_map/ppermute | solution.py:351
  19.7 1.3 %image.3 = (bf16[2,32,512]{2,1,0:T(8,128)(2,1)S(1)}, bf16[2,32,512]{2,1,0:T(8,128)(2,1)S(1)}, bf16[2,32,512]{2,1,0:T(8,128)(2,1)S(1)}, bf16[2,32,512]{2,1,0:T(8,128)(2,1)S(1)}) custom-call(s32[1,64]{1,0:T(1,128)S(1)} %get-tuple-element.35.ranks_near, bf16[2,8,2,2,2,48,256]{6,5,4,3,2,1,0:T(8,128)(2,1)S(1)} %bitcast.3, ...), custom_call_target="tpu_custom_call" | custom-call | flops 603979776 | bytes 2359296 | tf_op jit(solution)/shard_map/image/pallas_call | solution.py:28
  21.1 2.5 %collective-permute-start.7 = (bf16[2,32,512]{2,1,0:T(8,128)(2,1)S(1)}, bf16[2,32,512]{2,1,0:T(8,128)(2,1)S(1)}, u32[]{:S(2)}, u32[]{:S(2)}) collective-permute-start(bf16[2,32,512]{2,1,0:T(8,128)(2,1)S(1)} %get-tuple-element.45), channel_id=1, source_target_pairs={{0,24},{8,16},{16,8},{24,0},{1,25},{9,17},{17,9},{25,1},{2,26},{10... | collective-permute-start | bytes 196616 | tf_op jit(solution)/shard_map/ppermute | solution.py:351
  23.6 0.5 collective-permute-start.8
  24.1 0.5 collective-permute-start.9
  24.6 1.7 %collective-permute-done.7.rest_0_ = bf16[2,32,512]{2,1,0:T(8,128)(2,1)S(1)} collective-permute-done((bf16[2,32,512]{2,1,0:T(8,128)(2,1)S(1)}, bf16[2,32,512]{2,1,0:T(8,128)(2,1)S(1)}, u32[]{:S(2)}, u32[]{:S(2)}) %collective-permute-start.7) | collective-permute-done | bytes 65568 | tf_op jit(solution)/shard_map/ppermute | solution.py:351
  26.4 1.5 %collective-permute-done.8.rest_1_ = bf16[2,32,512]{2,1,0:T(8,128)(2,1)S(1)} collective-permute-done((bf16[2,32,512]{2,1,0:T(8,128)(2,1)S(1)}, bf16[2,32,512]{2,1,0:T(8,128)(2,1)S(1)}, u32[]{:S(2)}, u32[]{:S(2)}) %collective-permute-start.8) | collective-permute-done | bytes 65568 | tf_op jit(solution)/shard_map/ppermute | solution.py:351
  27.8 0.5 collective-permute-done.9.rest_2_
  28.7 1.5 %collective-permute-start.10 = (bf16[2,32,512]{2,1,0:T(8,128)(2,1)S(1)}, bf16[2,32,512]{2,1,0:T(8,128)(2,1)S(1)}, u32[]{:S(2)}, u32[]{:S(2)}) collective-permute-start(bf16[2,32,512]{2,1,0:T(8,128)(2,1)S(1)} %get-tuple-element.49), channel_id=1, source_target_pairs={{0,24},{8,16},{16,8},{24,0},{1,25},{9,17},{17,9},{25,1},{2,26},{10... | collective-permute-start | bytes 196616 | tf_op jit(solution)/shard_map/ppermute | solution.py:351
  30.8 1.5 %collective-permute-start.12 = (bf16[2,32,512]{2,1,0:T(8,128)(2,1)S(1)}, bf16[2,32,512]{2,1,0:T(8,128)(2,1)S(1)}, u32[]{:S(2)}, u32[]{:S(2)}) collective-permute-start(bf16[2,32,512]{2,1,0:T(8,128)(2,1)S(1)} %get-tuple-element.51), channel_id=1, source_target_pairs={{0,8},{8,0},{16,24},{24,16},{1,9},{9,1},{17,25},{25,17},{2,10},{10... | collective-permute-start | bytes 196616 | tf_op jit(solution)/shard_map/ppermute | solution.py:351
  32.3 1.7 %collective-permute-done.10.rest_0_ = bf16[2,32,512]{2,1,0:T(8,128)(2,1)S(1)} collective-permute-done((bf16[2,32,512]{2,1,0:T(8,128)(2,1)S(1)}, bf16[2,32,512]{2,1,0:T(8,128)(2,1)S(1)}, u32[]{:S(2)}, u32[]{:S(2)}) %collective-permute-start.10) | collective-permute-done | bytes 65568 | tf_op jit(solution)/shard_map/ppermute | solution.py:351
  34.0 0.7 %collective-permute-done.11.rest_1_ = bf16[2,32,512]{2,1,0:T(8,128)(2,1)S(1)} collective-permute-done((bf16[2,32,512]{2,1,0:T(8,128)(2,1)S(1)}, bf16[2,32,512]{2,1,0:T(8,128)(2,1)S(1)}, u32[]{:S(2)}, u32[]{:S(2)}) %collective-permute-start.11) | collective-permute-done | bytes 65568 | tf_op jit(solution)/shard_map/ppermute | solution.py:351
  35.1 1.6 %forward.1 = (bf16[1,224,128]{2,1,0:T(8,128)(2,1)S(1)}, bf16[1,224,128]{2,1,0:T(8,128)(2,1)S(1)}, bf16[1,224,128]{2,1,0:T(8,128)(2,1)S(1)}, bf16[1,224,128]{2,1,...) custom-call(s32[1,64]{1,0:T(1,128)S(1)} %get-tuple-element.35.ranks_, ...), custom_call_target="tpu_custom_call" | custom-call | flops 805306368 | bytes 3145728 | tf_op jit(solution)/shard_map/forward/pallas_call | solution.py:28
  36.6 2.1 %collective-permute-start.13 = (bf16[1,224,128]{2,1,0:T(8,128)(2,1)S(1)}, bf16[1,224,128]{2,1,0:T(8,128)(2,1)S(1)}, u32[]{:S(2)}, u32[]{:S(2)}) collective-permute-start(bf16[1,224,128]{2,1,0:T(8,128)(2,1)S(1)} %get-tuple-element.53), channel_id=1, source_target_pairs={{0,7},{1,6},{2,5},{3,4},{4,3},{5,2},{6,1},{7,0},{8,15},{9,14},{10,... | collective-permute-start | bytes 172040 | tf_op jit(solution)/shard_map/ppermute | solution.py:351
  38.8 1.6 %collective-permute-start.14 = (bf16[1,224,128]{2,1,0:T(8,128)(2,1)S(1)}, bf16[1,224,128]{2,1,0:T(8,128)(2,1)S(1)}, u32[]{:S(2)}, u32[]{:S(2)}) collective-permute-start(bf16[1,224,128]{2,1,0:T(8,128)(2,1)S(1)} %get-tuple-element.54), channel_id=1, source_target_pairs={{0,6},{1,7},{2,4},{3,5},{4,2},{5,3},{6,0},{7,1},{8,14},{9,15},{10,... | collective-permute-start | bytes 172040 | tf_op jit(solution)/shard_map/ppermute | solution.py:351
  40.4 2.6 %collective-permute-start.16 = (bf16[1,224,128]{2,1,0:T(8,128)(2,1)S(1)}, bf16[1,224,128]{2,1,0:T(8,128)(2,1)S(1)}, u32[]{:S(2)}, u32[]{:S(2)}) collective-permute-start(bf16[1,224,128]{2,1,0:T(8,128)(2,1)S(1)} %get-tuple-element.56), channel_id=1, source_target_pairs={{0,4},{1,5},{2,6},{3,7},{4,0},{5,1},{6,2},{7,3},{8,12},{9,13},{10,... | collective-permute-start | bytes 172040 | tf_op jit(solution)/shard_map/ppermute | solution.py:351
  43.0 0.9 %collective-permute-start.17 = (bf16[1,224,128]{2,1,0:T(8,128)(2,1)S(1)}, bf16[1,224,128]{2,1,0:T(8,128)(2,1)S(1)}, u32[]{:S(2)}, u32[]{:S(2)}) collective-permute-start(bf16[1,224,128]{2,1,0:T(8,128)(2,1)S(1)} %get-tuple-element.57), channel_id=1, source_target_pairs={{0,3},{1,2},{2,1},{3,0},{4,7},{5,6},{6,5},{7,4},{8,11},{9,10},{10,... | collective-permute-start | bytes 172040 | tf_op jit(solution)/shard_map/ppermute | solution.py:351
  43.9 0.9 %collective-permute-start.18 = (bf16[1,224,128]{2,1,0:T(8,128)(2,1)S(1)}, bf16[1,224,128]{2,1,0:T(8,128)(2,1)S(1)}, u32[]{:S(2)}, u32[]{:S(2)}) collective-permute-start(bf16[1,224,128]{2,1,0:T(8,128)(2,1)S(1)} %get-tuple-element.58), channel_id=1, source_target_pairs={{0,2},{1,3},{2,0},{3,1},{4,6},{5,7},{6,4},{7,5},{8,10},{9,11},{10,... | collective-permute-start | bytes 172040 | tf_op jit(solution)/shard_map/ppermute | solution.py:351
  44.8 1.2 %collective-permute-start.19 = (bf16[1,224,128]{2,1,0:T(8,128)(2,1)S(1)}, bf16[1,224,128]{2,1,0:T(8,128)(2,1)S(1)}, u32[]{:S(2)}, u32[]{:S(2)}) collective-permute-start(bf16[1,224,128]{2,1,0:T(8,128)(2,1)S(1)} %get-tuple-element.59), channel_id=1, source_target_pairs={{0,1},{1,0},{2,3},{3,2},{4,5},{5,4},{6,7},{7,6},{8,9},{9,8},{10,11... | collective-permute-start | bytes 172040 | tf_op jit(solution)/shard_map/ppermute | solution.py:351
  46.0 3.1 %collective-permute-done.15.rest_2_ = bf16[1,224,128]{2,1,0:T(8,128)(2,1)S(1)} collective-permute-done((bf16[1,224,128]{2,1,0:T(8,128)(2,1)S(1)}, bf16[1,224,128]{2,1,0:T(8,128)(2,1)S(1)}, u32[]{:S(2)}, u32[]{:S(2)}) %collective-permute-start.15) | collective-permute-done | bytes 57376 | tf_op jit(solution)/shard_map/ppermute | solution.py:351
  49.1 1.2 %collective-permute-done.16.rest_3_ = bf16[1,224,128]{2,1,0:T(8,128)(2,1)S(1)} collective-permute-done((bf16[1,224,128]{2,1,0:T(8,128)(2,1)S(1)}, bf16[1,224,128]{2,1,0:T(8,128)(2,1)S(1)}, u32[]{:S(2)}, u32[]{:S(2)}) %collective-permute-start.16) | collective-permute-done | bytes 57376 | tf_op jit(solution)/shard_map/ppermute | solution.py:351
  50.8 2.1 %result.1 = bf16[2,512,128]{2,1,0:T(8,128)(2,1)} custom-call(s32[1,64]{1,0:T(1,128)S(1)} %get-tuple-element.35.ranks_near, bf16[2,2,8,2,2,48,256]{6,5,4,3,2,1,0:T(8,128)(2,1)S(1)} %bitcast.7, bf16[1,224,128]{2,1,0:T(8,128)(2,1)S(1)} %collective-permute-done.13.rest_0_, bf16[1,224,128]{2,1,0:T(8,128)(2,1)S(1)} %collective-permute-done.14.rest_1_, ...), custom_call_target="tpu_custom_call" | custom-call | flops 805306368 | bytes 3145728 | tf_op jit(solution)/shard_map/result/pallas_call | solution.py:28
  (28 shorter events, 2.2 us)
Async XLA Ops:
  0.0 14.3 %copy-start.2 = (f32[16,4096]{1,0:T(8,128)S(1)}, f32[16,4096]{1,0:T(8,128)}, u32[]{:S(2)}) copy-start(f32[16,4096]{1,0:T(8,128)} %constant.7.clone.choice) | copy-start | bytes 786436
  0.0 14.3 %copy-start.3 = (s32[64,64]{1,0:T(8,128)S(1)}, s32[64,64]{1,0:T(8,128)}, u32[]{:S(2)}) copy-start(s32[64,64]{1,0:T(8,128)} %mask.1) | copy-start | bytes 49156
  0.0 14.3 %copy-start.4 = (f32[64,128]{1,0:T(8,128)S(1)}, f32[64,128]{1,0:T(8,128)}, u32[]{:S(2)}) copy-start(f32[64,128]{1,0:T(8,128)} %constant.6.clone.table) | copy-start | bytes 98308
  0.0 14.3 %copy-start.5 = (f32[16,256]{1,0:T(8,128)S(1)}, f32[16,256]{1,0:T(8,128)}, u32[]{:S(2)}) copy-start(f32[16,256]{1,0:T(8,128)} %constant.8.clone.same) | copy-start | bytes 49156
  0.0 16.0 %copy-start = (bf16[2,16,2,2,48,256]{5,4,3,2,1,0:T(8,128)(2,1)S(1)}, bf16[2,16,2,2,48,256]{5,4,3,2,1,0:T(8,128)(2,1)}, u32[]{:S(2)}) copy-start(bf16[2,16,2,2,48,256]{5,4,3,2,1,0:T(8,128)(2,1)} %param.10) | copy-start | bytes 9437188
  1.9 11.6 %collective-permute-start.5 = (bf16[1,224,128]{2,1,0:T(8,128)(2,1)S(1)}, bf16[1,224,128]{2,1,0:T(8,128)(2,1)S(1)}, u32[]{:S(2)}, u32[]{:S(2)}) collective-permute-start(bf16[1,224,128]{2,1,0:T(8,128)(2,1)S(1)} %get-tuple-element.43), channel_id=1, source_target_pairs={{0,7},{1,6},{2,5},{3,4},{4,3},{5,2},{6,1},{7,0},{8,15},{9,14},{10,... | collective-permute-start | bytes 172040 | tf_op jit(solution)/shard_map/ppermute | solution.py:351
  6.5 7.8 %collective-permute-start.6 = (bf16[1,224,128]{2,1,0:T(8,128)(2,1)S(1)}, bf16[1,224,128]{2,1,0:T(8,128)(2,1)S(1)}, u32[]{:S(2)}, u32[]{:S(2)}) collective-permute-start(bf16[1,224,128]{2,1,0:T(8,128)(2,1)S(1)} %get-tuple-element.44), channel_id=1, source_target_pairs={{0,6},{1,7},{2,4},{3,5},{4,2},{5,3},{6,0},{7,1},{8,14},{9,15},{10,... | collective-permute-start | bytes 172040 | tf_op jit(solution)/shard_map/ppermute | solution.py:351
  9.8 7.1 %collective-permute-start = (bf16[1,224,128]{2,1,0:T(8,128)(2,1)S(1)}, bf16[1,224,128]{2,1,0:T(8,128)(2,1)S(1)}, u32[]{:S(2)}, u32[]{:S(2)}) collective-permute-start(bf16[1,224,128]{2,1,0:T(8,128)(2,1)S(1)} %get-tuple-element.38), channel_id=1, source_target_pairs={{0,5},{1,4},{2,7},{3,6},{4,1},{5,0},{6,3},{7,2},{8,13},{9,12},{10,... | collective-permute-start | bytes 172040 | tf_op jit(solution)/shard_map/ppermute | solution.py:351
  10.3 8.5 %collective-permute-start.1 = (bf16[1,224,128]{2,1,0:T(8,128)(2,1)S(1)}, bf16[1,224,128]{2,1,0:T(8,128)(2,1)S(1)}, u32[]{:S(2)}, u32[]{:S(2)}) collective-permute-start(bf16[1,224,128]{2,1,0:T(8,128)(2,1)S(1)} %get-tuple-element.39), channel_id=1, source_target_pairs={{0,4},{1,5},{2,6},{3,7},{4,0},{5,1},{6,2},{7,3},{8,12},{9,13},{10,... | collective-permute-start | bytes 172040 | tf_op jit(solution)/shard_map/ppermute | solution.py:351
  12.5 6.3 %collective-permute-start.2 = (bf16[1,224,128]{2,1,0:T(8,128)(2,1)S(1)}, bf16[1,224,128]{2,1,0:T(8,128)(2,1)S(1)}, u32[]{:S(2)}, u32[]{:S(2)}) collective-permute-start(bf16[1,224,128]{2,1,0:T(8,128)(2,1)S(1)} %get-tuple-element.40), channel_id=1, source_target_pairs={{0,3},{1,2},{2,1},{3,0},{4,7},{5,6},{6,5},{7,4},{8,11},{9,10},{10,... | collective-permute-start | bytes 172040 | tf_op jit(solution)/shard_map/ppermute | solution.py:351
  13.5 6.2 %collective-permute-start.3 = (bf16[1,224,128]{2,1,0:T(8,128)(2,1)S(1)}, bf16[1,224,128]{2,1,0:T(8,128)(2,1)S(1)}, u32[]{:S(2)}, u32[]{:S(2)}) collective-permute-start(bf16[1,224,128]{2,1,0:T(8,128)(2,1)S(1)} %get-tuple-element.41), channel_id=1, source_target_pairs={{0,2},{1,3},{2,0},{3,1},{4,6},{5,7},{6,4},{7,5},{8,10},{9,11},{10,... | collective-permute-start | bytes 172040 | tf_op jit(solution)/shard_map/ppermute | solution.py:351
  14.3 5.4 %collective-permute-start.4 = (bf16[1,224,128]{2,1,0:T(8,128)(2,1)S(1)}, bf16[1,224,128]{2,1,0:T(8,128)(2,1)S(1)}, u32[]{:S(2)}, u32[]{:S(2)}) collective-permute-start(bf16[1,224,128]{2,1,0:T(8,128)(2,1)S(1)} %get-tuple-element.42), channel_id=1, source_target_pairs={{0,1},{1,0},{2,3},{3,2},{4,5},{5,4},{6,7},{7,6},{8,9},{9,8},{10,11... | collective-permute-start | bytes 172040 | tf_op jit(solution)/shard_map/ppermute | solution.py:351
  16.9 33.9 %copy-start.1 = (bf16[2,2,16,2,48,256]{5,4,3,2,1,0:T(8,128)(2,1)S(1)}, bf16[2,2,16,2,48,256]{5,4,3,2,1,0:T(8,128)(2,1)}, u32[]{:S(2)}) copy-start(bf16[2,2,16,2,48,256]{5,4,3,2,1,0:T(8,128)(2,1)} %param.9) | copy-start | bytes 9437188
  21.1 5.3 %collective-permute-start.7 = (bf16[2,32,512]{2,1,0:T(8,128)(2,1)S(1)}, bf16[2,32,512]{2,1,0:T(8,128)(2,1)S(1)}, u32[]{:S(2)}, u32[]{:S(2)}) collective-permute-start(bf16[2,32,512]{2,1,0:T(8,128)(2,1)S(1)} %get-tuple-element.45), channel_id=1, source_target_pairs={{0,24},{8,16},{16,8},{24,0},{1,25},{9,17},{17,9},{25,1},{2,26},{10... | collective-permute-start | bytes 196616 | tf_op jit(solution)/shard_map/ppermute | solution.py:351
  23.6 4.3 %collective-permute-start.8 = (bf16[2,32,512]{2,1,0:T(8,128)(2,1)S(1)}, bf16[2,32,512]{2,1,0:T(8,128)(2,1)S(1)}, u32[]{:S(2)}, u32[]{:S(2)}) collective-permute-start(bf16[2,32,512]{2,1,0:T(8,128)(2,1)S(1)} %get-tuple-element.46), channel_id=1, source_target_pairs={{0,16},{8,24},{16,0},{24,8},{1,17},{9,25},{17,1},{25,9},{2,18},{10... | collective-permute-start | bytes 196616 | tf_op jit(solution)/shard_map/ppermute | solution.py:351
  24.1 4.3 %collective-permute-start.9 = (bf16[2,32,512]{2,1,0:T(8,128)(2,1)S(1)}, bf16[2,32,512]{2,1,0:T(8,128)(2,1)S(1)}, u32[]{:S(2)}, u32[]{:S(2)}) collective-permute-start(bf16[2,32,512]{2,1,0:T(8,128)(2,1)S(1)} %get-tuple-element.47), channel_id=1, source_target_pairs={{0,8},{8,0},{16,24},{24,16},{1,9},{9,1},{17,25},{25,17},{2,10},{10... | collective-permute-start | bytes 196616 | tf_op jit(solution)/shard_map/ppermute | solution.py:351
  28.7 5.2 %collective-permute-start.10 = (bf16[2,32,512]{2,1,0:T(8,128)(2,1)S(1)}, bf16[2,32,512]{2,1,0:T(8,128)(2,1)S(1)}, u32[]{:S(2)}, u32[]{:S(2)}) collective-permute-start(bf16[2,32,512]{2,1,0:T(8,128)(2,1)S(1)} %get-tuple-element.49), channel_id=1, source_target_pairs={{0,24},{8,16},{16,8},{24,0},{1,25},{9,17},{17,9},{25,1},{2,26},{10... | collective-permute-start | bytes 196616 | tf_op jit(solution)/shard_map/ppermute | solution.py:351
  30.3 4.4 %collective-permute-start.11 = (bf16[2,32,512]{2,1,0:T(8,128)(2,1)S(1)}, bf16[2,32,512]{2,1,0:T(8,128)(2,1)S(1)}, u32[]{:S(2)}, u32[]{:S(2)}) collective-permute-start(bf16[2,32,512]{2,1,0:T(8,128)(2,1)S(1)} %get-tuple-element.50), channel_id=1, source_target_pairs={{0,16},{8,24},{16,0},{24,8},{1,17},{9,25},{17,1},{25,9},{2,18},{10... | collective-permute-start | bytes 196616 | tf_op jit(solution)/shard_map/ppermute | solution.py:351
  30.8 4.3 %collective-permute-start.12 = (bf16[2,32,512]{2,1,0:T(8,128)(2,1)S(1)}, bf16[2,32,512]{2,1,0:T(8,128)(2,1)S(1)}, u32[]{:S(2)}, u32[]{:S(2)}) collective-permute-start(bf16[2,32,512]{2,1,0:T(8,128)(2,1)S(1)} %get-tuple-element.51), channel_id=1, source_target_pairs={{0,8},{8,0},{16,24},{24,16},{1,9},{9,1},{17,25},{25,17},{2,10},{10... | collective-permute-start | bytes 196616 | tf_op jit(solution)/shard_map/ppermute | solution.py:351
  36.6 7.3 %collective-permute-start.13 = (bf16[1,224,128]{2,1,0:T(8,128)(2,1)S(1)}, bf16[1,224,128]{2,1,0:T(8,128)(2,1)S(1)}, u32[]{:S(2)}, u32[]{:S(2)}) collective-permute-start(bf16[1,224,128]{2,1,0:T(8,128)(2,1)S(1)} %get-tuple-element.53), channel_id=1, source_target_pairs={{0,7},{1,6},{2,5},{3,4},{4,3},{5,2},{6,1},{7,0},{8,15},{9,14},{10,... | collective-permute-start | bytes 172040 | tf_op jit(solution)/shard_map/ppermute | solution.py:351
  38.8 6.0 %collective-permute-start.14 = (bf16[1,224,128]{2,1,0:T(8,128)(2,1)S(1)}, bf16[1,224,128]{2,1,0:T(8,128)(2,1)S(1)}, u32[]{:S(2)}, u32[]{:S(2)}) collective-permute-start(bf16[1,224,128]{2,1,0:T(8,128)(2,1)S(1)} %get-tuple-element.54), channel_id=1, source_target_pairs={{0,6},{1,7},{2,4},{3,5},{4,2},{5,3},{6,0},{7,1},{8,14},{9,15},{10,... | collective-permute-start | bytes 172040 | tf_op jit(solution)/shard_map/ppermute | solution.py:351
  40.4 8.7 %collective-permute-start.15 = (bf16[1,224,128]{2,1,0:T(8,128)(2,1)S(1)}, bf16[1,224,128]{2,1,0:T(8,128)(2,1)S(1)}, u32[]{:S(2)}, u32[]{:S(2)}) collective-permute-start(bf16[1,224,128]{2,1,0:T(8,128)(2,1)S(1)} %get-tuple-element.55), channel_id=1, source_target_pairs={{0,5},{1,4},{2,7},{3,6},{4,1},{5,0},{6,3},{7,2},{8,13},{9,12},{10,... | collective-permute-start | bytes 172040 | tf_op jit(solution)/shard_map/ppermute | solution.py:351
  40.4 10.0 %collective-permute-start.16 = (bf16[1,224,128]{2,1,0:T(8,128)(2,1)S(1)}, bf16[1,224,128]{2,1,0:T(8,128)(2,1)S(1)}, u32[]{:S(2)}, u32[]{:S(2)}) collective-permute-start(bf16[1,224,128]{2,1,0:T(8,128)(2,1)S(1)} %get-tuple-element.56), channel_id=1, source_target_pairs={{0,4},{1,5},{2,6},{3,7},{4,0},{5,1},{6,2},{7,3},{8,12},{9,13},{10,... | collective-permute-start | bytes 172040 | tf_op jit(solution)/shard_map/ppermute | solution.py:351
  43.0 7.4 %collective-permute-start.17 = (bf16[1,224,128]{2,1,0:T(8,128)(2,1)S(1)}, bf16[1,224,128]{2,1,0:T(8,128)(2,1)S(1)}, u32[]{:S(2)}, u32[]{:S(2)}) collective-permute-start(bf16[1,224,128]{2,1,0:T(8,128)(2,1)S(1)} %get-tuple-element.57), channel_id=1, source_target_pairs={{0,3},{1,2},{2,1},{3,0},{4,7},{5,6},{6,5},{7,4},{8,11},{9,10},{10,... | collective-permute-start | bytes 172040 | tf_op jit(solution)/shard_map/ppermute | solution.py:351
  43.9 6.9 %collective-permute-start.18 = (bf16[1,224,128]{2,1,0:T(8,128)(2,1)S(1)}, bf16[1,224,128]{2,1,0:T(8,128)(2,1)S(1)}, u32[]{:S(2)}, u32[]{:S(2)}) collective-permute-start(bf16[1,224,128]{2,1,0:T(8,128)(2,1)S(1)} %get-tuple-element.58), channel_id=1, source_target_pairs={{0,2},{1,3},{2,0},{3,1},{4,6},{5,7},{6,4},{7,5},{8,10},{9,11},{10,... | collective-permute-start | bytes 172040 | tf_op jit(solution)/shard_map/ppermute | solution.py:351
  44.8 6.1 %collective-permute-start.19 = (bf16[1,224,128]{2,1,0:T(8,128)(2,1)S(1)}, bf16[1,224,128]{2,1,0:T(8,128)(2,1)S(1)}, u32[]{:S(2)}, u32[]{:S(2)}) collective-permute-start(bf16[1,224,128]{2,1,0:T(8,128)(2,1)S(1)} %get-tuple-element.59), channel_id=1, source_target_pairs={{0,1},{1,0},{2,3},{3,2},{4,5},{5,4},{6,7},{7,6},{8,9},{9,8},{10,11... | collective-permute-start | bytes 172040 | tf_op jit(solution)/shard_map/ppermute | solution.py:351
